TPU v7x, 32 devices: a whole 2x2x4 slice. The times are simulated.
32 devices in a mesh: seq: 32 (over z, y, x, core), rep: 1.
Axes of the slice: x: 2, y: 2, z: 4, core: 2. Of those that a mesh axis runs over, the one named last changes fastest.
Arguments:
- queries: bfloat16 [1, 4096, 2048], P('rep', 'seq'), may hold values from -9 to 9
- keys: bfloat16 [1, 4096, 512], P('rep', 'seq'), may hold values from -9 to 9
- values: bfloat16 [1, 4096, 512], P('rep', 'seq'), may hold values from -6 to 6
- conv_taps: float32 [4, 512], replicated, may hold values from -2 to 2
- grad_out: bfloat16 [1, 4096, 2048], P('rep', 'seq'), may hold values from -24 to 24
Outputs:
- grad_queries: bfloat16 [1, 4096, 2048], P('rep', 'seq')
- grad_keys: bfloat16 [1, 4096, 512], P('rep', 'seq')
- grad_values: bfloat16 [1, 4096, 512], P('rep', 'seq')
- grad_taps: float32 [2048], P('seq')
All inputs are finite; a program needn't handle non-finite values.
Results may differ from a plain program's by a relative error of at most 0.012.
Values may be sent and summed in bfloat16 or wider, within the bound.
No kernel may reach another device: no remote copies, remote signals or barrier semaphores. Data moves between devices by JAX's collectives and lax.ppermute only.
A program may use at most 64 MiB of HBM per device.

v0:
```python
import math

import jax
import jax.numpy as jnp
from jax import lax
from jax.sharding import PartitionSpec as P

HEAD_SIZE = 128
WINDOW = 1024


NEG_FILL = -1e30


def passed_along(block, axis, distance):
    devices = range(lax.axis_size(axis))
    route = [(i - distance, i) for i in devices if i - distance in devices]
    return lax.ppermute(block, axis, route)


def conv_apply(extended, conv_taps, tok_rows):
    tap_count = conv_taps.shape[0]
    summed = jnp.zeros((tok_rows, extended.shape[1]), jnp.float32)
    for index_k in range(tap_count):
        begin = tap_count - 1 - index_k
        summed = summed + conv_taps[index_k] * extended[begin : begin + tok_rows]
    return summed


def attend(query_block, grad_block, key_block, value_block, first_query, window):
    tok_rows = query_block.shape[0]
    keys_len = key_block.shape[0]
    kv_heads = key_block.shape[1] // HEAD_SIZE
    group_size = query_block.shape[1] // (HEAD_SIZE * kv_heads)
    inv_root = 1.0 / math.sqrt(HEAD_SIZE)
    query_pos = first_query + jnp.arange(tok_rows, dtype=jnp.int32)
    key_pos = first_query - window + jnp.arange(keys_len, dtype=jnp.int32)
    offset = query_pos[:, None] - key_pos[None, :]
    visible = (offset >= 0) & (offset < window) & (key_pos[None, :] >= 0)
    queries_grouped = query_block.reshape(tok_rows, kv_heads, group_size * HEAD_SIZE).transpose(
        1, 0, 2
    )
    grads_grouped = grad_block.reshape(tok_rows, kv_heads, group_size * HEAD_SIZE).transpose(
        1, 0, 2
    )
    keys_grouped = key_block.reshape(keys_len, kv_heads, HEAD_SIZE).transpose(1, 0, 2)
    values_grouped = value_block.reshape(keys_len, kv_heads, HEAD_SIZE).transpose(1, 0, 2)

    def one_group(operands):
        query_head, grad_head, key_head, value_head = operands
        query_head = query_head.reshape(tok_rows, group_size, HEAD_SIZE)
        grad_head = grad_head.reshape(tok_rows, group_size, HEAD_SIZE)
        scores = (
            jnp.einsum("tgd,ld->gtl", query_head, key_head, preferred_element_type=jnp.float32)
            * inv_root
        )
        scores = jnp.where(visible[None], scores, NEG_FILL)
        row_max = jnp.max(scores, axis=-1, keepdims=True)
        row_sum = jnp.sum(jnp.exp(scores - row_max), axis=-1, keepdims=True)
        log_total = row_max + jnp.log(row_sum)
        attn_prob = jnp.exp(scores - log_total)
        prob_low = attn_prob.astype(jnp.bfloat16)
        grad_prob = jnp.einsum(
            "tgd,ld->gtl", grad_head, value_head, preferred_element_type=jnp.float32
        )
        row_delta = jnp.sum(attn_prob * grad_prob, axis=-1, keepdims=True)
        grad_score = (attn_prob * (grad_prob - row_delta) * inv_root).astype(jnp.bfloat16)
        grad_query = jnp.einsum(
            "gtl,ld->tgd", grad_score, key_head, preferred_element_type=jnp.float32
        )
        grad_key = jnp.einsum(
            "gtl,tgd->ld", grad_score, query_head, preferred_element_type=jnp.float32
        )
        grad_value = jnp.einsum(
            "gtl,tgd->ld", prob_low, grad_head, preferred_element_type=jnp.float32
        )
        return (grad_query.reshape(tok_rows, group_size * HEAD_SIZE), grad_key, grad_value)

    grad_query, grad_key, grad_value = lax.map(
        one_group, (queries_grouped, grads_grouped, keys_grouped, values_grouped)
    )
    grad_query = grad_query.transpose(1, 0, 2).reshape(tok_rows, kv_heads * group_size * HEAD_SIZE)
    grad_key = grad_key.transpose(1, 0, 2).reshape(keys_len, kv_heads * HEAD_SIZE)
    grad_value = grad_value.transpose(1, 0, 2).reshape(keys_len, kv_heads * HEAD_SIZE)
    return (grad_query, grad_key, grad_value)


def on_device(queries, keys, values, conv_taps, grad_out):
    tok_rows = queries.shape[1]
    tap_count = conv_taps.shape[0]
    kv_width = keys.shape[2]
    reach_blocks = WINDOW // tok_rows
    device_index = lax.axis_index("seq")
    first_query = device_index * tok_rows
    value_rows = values[0]
    value_tail = passed_along(value_rows[tok_rows - (tap_count - 1) :], "seq", 1)
    value_ext = jnp.concatenate([value_tail, value_rows], axis=0).astype(jnp.float32)
    mixed = conv_apply(value_ext, conv_taps, tok_rows).astype(jnp.bfloat16)
    paired = jnp.concatenate([keys[0], mixed], axis=1)

    def advance(step_index, carry):
        latest, holder = carry
        latest = passed_along(latest, "seq", 1)
        holder = lax.dynamic_update_slice_in_dim(
            holder, latest[None], reach_blocks - 1 - step_index, 0
        )
        return (latest, holder)

    holder = jnp.zeros((reach_blocks, tok_rows, 2 * kv_width), jnp.bfloat16)
    last_block, holder = lax.fori_loop(0, reach_blocks, advance, (paired, holder))
    window_rows = jnp.concatenate(
        [holder.reshape(reach_blocks * tok_rows, 2 * kv_width), paired], axis=0
    )
    grad_query, grad_key, grad_value = attend(
        queries[0],
        grad_out[0],
        window_rows[:, :kv_width],
        window_rows[:, kv_width:],
        first_query,
        WINDOW,
    )
    returned = jnp.concatenate([grad_key, grad_value], axis=1)
    blocks = returned.reshape(reach_blocks + 1, tok_rows, 2 * kv_width)

    def gather_back(step_index, running):
        block_part = lax.dynamic_slice_in_dim(blocks, step_index + 1, 1, 0)[0]
        return passed_along(running, "seq", -1) + block_part

    owned = lax.fori_loop(0, reach_blocks, gather_back, blocks[0])
    grad_keys_out = owned[:, :kv_width]
    grad_mixed = owned[:, kv_width:]
    grad_head = passed_along(grad_mixed[: tap_count - 1], "seq", -1)
    grad_ext = jnp.concatenate([grad_mixed, grad_head], axis=0)
    grad_values = jnp.zeros((tok_rows, kv_width), jnp.float32)
    tap_rows = []
    for index_k in range(tap_count):
        grad_values = grad_values + conv_taps[index_k] * grad_ext[index_k : index_k + tok_rows]
        begin = tap_count - 1 - index_k
        tap_rows.append(jnp.sum(grad_mixed * value_ext[begin : begin + tok_rows], axis=0))
    total_tokens = tok_rows * lax.axis_size("seq") * lax.axis_size("rep")
    local_bucket = jnp.stack(tap_rows, axis=0).reshape(-1) * (1.0 / math.sqrt(total_tokens))
    owned_shard = lax.psum_scatter(local_bucket, "seq", scatter_dimension=0, tiled=True)
    grad_taps = lax.psum(owned_shard, "rep")
    return (
        grad_query.astype(jnp.bfloat16)[None],
        grad_keys_out.astype(jnp.bfloat16)[None],
        grad_values.astype(jnp.bfloat16)[None],
        grad_taps,
    )


def solution(mesh):
    in_specs = (
        P("rep", "seq", None),
        P("rep", "seq", None),
        P("rep", "seq", None),
        P(),
        P("rep", "seq", None),
    )
    out_specs = (P("rep", "seq", None), P("rep", "seq", None), P("rep", "seq", None), P("seq"))
    return jax.shard_map(
        on_device, mesh=mesh, in_specs=in_specs, out_specs=out_specs, check_vma=False
    )
```

profile of v0, /device:TPU:0, one launch (start us, length us, event | category | flops | bytes accessed | tf_op | source)
XLA Modules:
  0.0 355.0 jit_solution(14989048383651725343)
XLA Ops:
  11.9 64.8 %while.45 = (s32[]{:T(128)}, bf16[128,1024]{1,0:T(8,128)(2,1)}, bf16[8,128,1024]{2,1,0:T(8,128)(2,1)S(1)}, s32[]{:T(128)}, s32[]{:T(128)}, /*index=5*/s32[]{:T(128)}, s32[]{:T(128)}) while((s32[]{:T(128)}, bf16[128,1024]{1,0:T(8,128)(2,1)}, bf16[8,128,1024]{2,1,0:T(8,128)(2,1)S(1)}, s32[]{:T(128)}, s32[]{:T(128)}, /*index=5*/s32[]{:T(128)}, ...), condition=%wide.region_1.0_spmd, body=%wide.region_0.0_spmd.sunk | while | flops 6 | bytes 2097319 | solution.py:110
  11.9 4.5 %collective-permute-start = (bf16[128,1024]{1,0:T(8,128)(2,1)}, bf16[128,1024]{1,0:T(8,128)(2,1)S(1)}, u32[]{:S(2)}, u32[]{:S(2)}) collective-permute-start(bf16[128,1024]{1,0:T(8,128)(2,1)} %get-tuple-element.449), channel_id=1, source_target_pairs={{0,1},{1,2},{2,3},{3,4},{4,5},{5,6},{6,7},{7,8},{8,9},{9,10},{10,1... | collective-permute-start | bytes 786440 | tf_op jit(solution)/shard_map/while/body/eval_jaxpr/ppermute | solution.py:18
  24.8 6.6 %collective-permute-start = (bf16[128,1024]{1,0:T(8,128)(2,1)}, bf16[128,1024]{1,0:T(8,128)(2,1)S(1)}, u32[]{:S(2)}, u32[]{:S(2)}) collective-permute-start(bf16[128,1024]{1,0:T(8,128)(2,1)} %get-tuple-element.449), channel_id=1, source_target_pairs={{0,1},{1,2},{2,3},{3,4},{4,5},{5,6},{6,7},{7,8},{8,9},{9,10},{10,1... | collective-permute-start | bytes 786440 | tf_op jit(solution)/shard_map/while/body/eval_jaxpr/ppermute | solution.py:18
  33.5 6.6 %collective-permute-start = (bf16[128,1024]{1,0:T(8,128)(2,1)}, bf16[128,1024]{1,0:T(8,128)(2,1)S(1)}, u32[]{:S(2)}, u32[]{:S(2)}) collective-permute-start(bf16[128,1024]{1,0:T(8,128)(2,1)} %get-tuple-element.449), channel_id=1, source_target_pairs={{0,1},{1,2},{2,3},{3,4},{4,5},{5,6},{6,7},{7,8},{8,9},{9,10},{10,1... | collective-permute-start | bytes 786440 | tf_op jit(solution)/shard_map/while/body/eval_jaxpr/ppermute | solution.py:18
  42.1 6.6 %collective-permute-start = (bf16[128,1024]{1,0:T(8,128)(2,1)}, bf16[128,1024]{1,0:T(8,128)(2,1)S(1)}, u32[]{:S(2)}, u32[]{:S(2)}) collective-permute-start(bf16[128,1024]{1,0:T(8,128)(2,1)} %get-tuple-element.449), channel_id=1, source_target_pairs={{0,1},{1,2},{2,3},{3,4},{4,5},{5,6},{6,7},{7,8},{8,9},{9,10},{10,1... | collective-permute-start | bytes 786440 | tf_op jit(solution)/shard_map/while/body/eval_jaxpr/ppermute | solution.py:18
  50.8 6.6 %collective-permute-start = (bf16[128,1024]{1,0:T(8,128)(2,1)}, bf16[128,1024]{1,0:T(8,128)(2,1)S(1)}, u32[]{:S(2)}, u32[]{:S(2)}) collective-permute-start(bf16[128,1024]{1,0:T(8,128)(2,1)} %get-tuple-element.449), channel_id=1, source_target_pairs={{0,1},{1,2},{2,3},{3,4},{4,5},{5,6},{6,7},{7,8},{8,9},{9,10},{10,1... | collective-permute-start | bytes 786440 | tf_op jit(solution)/shard_map/while/body/eval_jaxpr/ppermute | solution.py:18
  59.4 6.6 %collective-permute-start = (bf16[128,1024]{1,0:T(8,128)(2,1)}, bf16[128,1024]{1,0:T(8,128)(2,1)S(1)}, u32[]{:S(2)}, u32[]{:S(2)}) collective-permute-start(bf16[128,1024]{1,0:T(8,128)(2,1)} %get-tuple-element.449), channel_id=1, source_target_pairs={{0,1},{1,2},{2,3},{3,4},{4,5},{5,6},{6,7},{7,8},{8,9},{9,10},{10,1... | collective-permute-start | bytes 786440 | tf_op jit(solution)/shard_map/while/body/eval_jaxpr/ppermute | solution.py:18
  68.1 6.6 %collective-permute-start = (bf16[128,1024]{1,0:T(8,128)(2,1)}, bf16[128,1024]{1,0:T(8,128)(2,1)S(1)}, u32[]{:S(2)}, u32[]{:S(2)}) collective-permute-start(bf16[128,1024]{1,0:T(8,128)(2,1)} %get-tuple-element.449), channel_id=1, source_target_pairs={{0,1},{1,2},{2,3},{3,4},{4,5},{5,6},{6,7},{7,8},{8,9},{9,10},{10,1... | collective-permute-start | bytes 786440 | tf_op jit(solution)/shard_map/while/body/eval_jaxpr/ppermute | solution.py:18
  82.8 67.7 %while.47 = (s32[]{:T(128)}, bf16[4,128,512]{1,2,0:T(8,128)(2,1)}, f32[4,1152,128]{2,1,0:T(8,128)}, f32[4,1152,128]{2,1,0:T(8,128)}, bf16[4,1152,128]{1,2,0:T(8,...) while((s32[]{:T(128)}, bf16[4,128,512]{1,2,0:T(8,128)(2,1)}, ...), condition=%wide.region_6.7_spmd.clone, body=%wide.region_2.6_spmd.clone.sunk | while | flops 768101120 | bytes 32144124 | solution.py:79
  125.0 4.3 %fusion.86 = f32[4,1152,128]{2,1,0:T(8,128)} fusion(f32[4,1152,128]{2,1,0:T(8,128)} %get-tuple-element.476, s32[]{:T(128)} %get-tuple-element.474, bf16[128,4,128]{0,2,1:T(8,128)(2,1)S(1)} %bitcast.122, f32[4,128,1152]{1,2,0:T(8,128)} %convolution_bitcast_fusion.4, f32[4,128,1152]{1,2,0:T(8,128)S(1)} %get-tuple-element.439, ...), kind=kOutput, calls=%fused_computation.15.clone.1 | convolution fusion | flops 155125376 | bytes 10162180 | tf_op jit(solution)/shard_map/while/body/eval_jaxpr/gtl,tgd->ld/dot_general | solution.py:71
  141.9 4.3 %fusion.86 = f32[4,1152,128]{2,1,0:T(8,128)} fusion(f32[4,1152,128]{2,1,0:T(8,128)} %get-tuple-element.476, s32[]{:T(128)} %get-tuple-element.474, bf16[128,4,128]{0,2,1:T(8,128)(2,1)S(1)} %bitcast.122, f32[4,128,1152]{1,2,0:T(8,128)} %convolution_bitcast_fusion.4, f32[4,128,1152]{1,2,0:T(8,128)S(1)} %get-tuple-element.439, ...), kind=kOutput, calls=%fused_computation.15.clone.1 | convolution fusion | flops 155125376 | bytes 10162180 | tf_op jit(solution)/shard_map/while/body/eval_jaxpr/gtl,tgd->ld/dot_general | solution.py:71
  153.7 5.9 %copy.54 = f32[1152,4,128]{2,1,0:T(4,128)} copy(f32[1152,4,128]{2,0,1:T(8,128)S(1)} %bitcast.123) | data formatting | bytes 4718592 | tf_op jit(solution)/shard_map/transpose | solution.py:83
  165.4 5.9 %copy.55 = f32[1152,4,128]{2,1,0:T(4,128)} copy(f32[1152,4,128]{2,0,1:T(8,128)S(1)} %bitcast.124) | data formatting | bytes 4718592 | tf_op jit(solution)/shard_map/transpose | solution.py:84
  176.2 5.1 %pad_maximum_fusion = f32[9,128,1024]{2,1,0:T(8,128)} fusion(f32[9,128,512]{2,1,0:T(8,128)} %concatenate.27, f32[9,128,512]{2,1,0:T(8,128)} %concatenate.26), kind=kLoop, calls=%fused_computation.48 | loop fusion | flops 1179648 | bytes 9437184 | tf_op jit(solution)/shard_map/concatenate | solution.py:122
  181.4 94.4 %while.46 = (s32[]{:T(128)}, f32[128,1024]{1,0:T(8,128)S(1)}, f32[9,128,1024]{2,1,0:T(8,128)}, s32[]{:T(128)}, s32[]{:T(128)}, /*index=5*/s32[]{:T(128)}) while((s32[]{:T(128)}, f32[128,1024]{1,0:T(8,128)S(1)}, f32[9,128,1024]{2,1,0:T(8,128)}, s32[]{:T(128)}, s32[]{:T(128)}, /*index=5*/s32[]{:T(128)}) %tuple.107), condition=%wide.region_8.9_spmd, body=%wide.region_7.8_spmd.sunk | while | flops 131077 | bytes 3670171 | solution.py:129
  182.7 6.6 %collective-permute-done.1 = f32[128,1024]{1,0:T(8,128)S(1)} collective-permute-done((f32[128,1024]{1,0:T(8,128)S(1)}, f32[128,1024]{1,0:T(8,128)S(1)}, u32[]{:S(2)}, u32[]{:S(2)}) %collective-permute-start.1) | collective-permute-done | bytes 524320 | tf_op jit(solution)/shard_map/while/body/eval_jaxpr/ppermute | solution.py:18
  191.7 9.8 %collective-permute-done.1 = f32[128,1024]{1,0:T(8,128)S(1)} collective-permute-done((f32[128,1024]{1,0:T(8,128)S(1)}, f32[128,1024]{1,0:T(8,128)S(1)}, u32[]{:S(2)}, u32[]{:S(2)}) %collective-permute-start.1) | collective-permute-done | bytes 524320 | tf_op jit(solution)/shard_map/while/body/eval_jaxpr/ppermute | solution.py:18
  204.0 9.2 %collective-permute-done.1 = f32[128,1024]{1,0:T(8,128)S(1)} collective-permute-done((f32[128,1024]{1,0:T(8,128)S(1)}, f32[128,1024]{1,0:T(8,128)S(1)}, u32[]{:S(2)}, u32[]{:S(2)}) %collective-permute-start.1) | collective-permute-done | bytes 524320 | tf_op jit(solution)/shard_map/while/body/eval_jaxpr/ppermute | solution.py:18
  215.6 9.2 %collective-permute-done.1 = f32[128,1024]{1,0:T(8,128)S(1)} collective-permute-done((f32[128,1024]{1,0:T(8,128)S(1)}, f32[128,1024]{1,0:T(8,128)S(1)}, u32[]{:S(2)}, u32[]{:S(2)}) %collective-permute-start.1) | collective-permute-done | bytes 524320 | tf_op jit(solution)/shard_map/while/body/eval_jaxpr/ppermute | solution.py:18
  227.2 10.0 %collective-permute-done.1 = f32[128,1024]{1,0:T(8,128)S(1)} collective-permute-done((f32[128,1024]{1,0:T(8,128)S(1)}, f32[128,1024]{1,0:T(8,128)S(1)}, u32[]{:S(2)}, u32[]{:S(2)}) %collective-permute-start.1) | collective-permute-done | bytes 524320 | tf_op jit(solution)/shard_map/while/body/eval_jaxpr/ppermute | solution.py:18
  239.6 10.1 %collective-permute-done.1 = f32[128,1024]{1,0:T(8,128)S(1)} collective-permute-done((f32[128,1024]{1,0:T(8,128)S(1)}, f32[128,1024]{1,0:T(8,128)S(1)}, u32[]{:S(2)}, u32[]{:S(2)}) %collective-permute-start.1) | collective-permute-done | bytes 524320 | tf_op jit(solution)/shard_map/while/body/eval_jaxpr/ppermute | solution.py:18
  252.1 10.1 %collective-permute-done.1 = f32[128,1024]{1,0:T(8,128)S(1)} collective-permute-done((f32[128,1024]{1,0:T(8,128)S(1)}, f32[128,1024]{1,0:T(8,128)S(1)}, u32[]{:S(2)}, u32[]{:S(2)}) %collective-permute-start.1) | collective-permute-done | bytes 524320 | tf_op jit(solution)/shard_map/while/body/eval_jaxpr/ppermute | solution.py:18
  264.6 10.1 %collective-permute-done.1 = f32[128,1024]{1,0:T(8,128)S(1)} collective-permute-done((f32[128,1024]{1,0:T(8,128)S(1)}, f32[128,1024]{1,0:T(8,128)S(1)}, u32[]{:S(2)}, u32[]{:S(2)}) %collective-permute-start.1) | collective-permute-done | bytes 524320 | tf_op jit(solution)/shard_map/while/body/eval_jaxpr/ppermute | solution.py:18
  279.8 73.0 %all-reduce = f32[2048]{0:T(1024)S(1)} all-reduce(f32[2048]{0:T(1024)S(1)} %bitcast.136), channel_id=2, replica_groups=mesh['seq'=32,'rep'=1] {'seq'}, use_global_device_ids=true, to_apply=%region_13.14.clone | all-reduce | flops 2048 | bytes 16384
  (148 shorter events, 135.9 us)
Async XLA Ops:
  1.8 8.2 %collective-permute-start.2 = (bf16[3,512]{0,1:T(8,128)(2,1)S(1)}, bf16[3,512]{0,1:T(8,128)(2,1)S(1)}, u32[]{:S(2)}, u32[]{:S(2)}) collective-permute-start(bf16[3,512]{0,1:T(8,128)(2,1)S(1)} %slice_bitcast_fusion), channel_id=1, source_target_pairs={{0,1},{1,2},{2,3},{3,4},{4,5},{5,6},{6,7},{7,8},{8,9},{9,10},{10,1... | collective-permute-start | bytes 9224 | tf_op jit(solution)/shard_map/ppermute | solution.py:18
  5.0 5.7 %copy-start.6 = (f32[1,512]{1,0:T(1,128)}, f32[1,512]{1,0:T(1,128)S(1)}, u32[]{:S(2)}) copy-start(f32[1,512]{1,0:T(1,128)S(1)} %get-tuple-element.324) | copy-start | bytes 6148
  5.0 5.7 %copy-start.8 = (f32[1,512]{1,0:T(1,128)}, f32[1,512]{1,0:T(1,128)S(1)}, u32[]{:S(2)}) copy-start(f32[1,512]{1,0:T(1,128)S(1)} %get-tuple-element.325) | copy-start | bytes 6148
  11.9 5.9 %collective-permute-start = (bf16[128,1024]{1,0:T(8,128)(2,1)}, bf16[128,1024]{1,0:T(8,128)(2,1)S(1)}, u32[]{:S(2)}, u32[]{:S(2)}) collective-permute-start(bf16[128,1024]{1,0:T(8,128)(2,1)} %get-tuple-element.449), channel_id=1, source_target_pairs={{0,1},{1,2},{2,3},{3,4},{4,5},{5,6},{6,7},{7,8},{8,9},{9,10},{10,1... | collective-permute-start | bytes 786440 | tf_op jit(solution)/shard_map/while/body/eval_jaxpr/ppermute | solution.py:18
  18.5 5.5 %collective-permute-start = (bf16[128,1024]{1,0:T(8,128)(2,1)}, bf16[128,1024]{1,0:T(8,128)(2,1)S(1)}, u32[]{:S(2)}, u32[]{:S(2)}) collective-permute-start(bf16[128,1024]{1,0:T(8,128)(2,1)} %get-tuple-element.449), channel_id=1, source_target_pairs={{0,1},{1,2},{2,3},{3,4},{4,5},{5,6},{6,7},{7,8},{8,9},{9,10},{10,1... | collective-permute-start | bytes 786440 | tf_op jit(solution)/shard_map/while/body/eval_jaxpr/ppermute | solution.py:18
  24.8 7.9 %collective-permute-start = (bf16[128,1024]{1,0:T(8,128)(2,1)}, bf16[128,1024]{1,0:T(8,128)(2,1)S(1)}, u32[]{:S(2)}, u32[]{:S(2)}) collective-permute-start(bf16[128,1024]{1,0:T(8,128)(2,1)} %get-tuple-element.449), channel_id=1, source_target_pairs={{0,1},{1,2},{2,3},{3,4},{4,5},{5,6},{6,7},{7,8},{8,9},{9,10},{10,1... | collective-permute-start | bytes 786440 | tf_op jit(solution)/shard_map/while/body/eval_jaxpr/ppermute | solution.py:18
  33.5 7.9 %collective-permute-start = (bf16[128,1024]{1,0:T(8,128)(2,1)}, bf16[128,1024]{1,0:T(8,128)(2,1)S(1)}, u32[]{:S(2)}, u32[]{:S(2)}) collective-permute-start(bf16[128,1024]{1,0:T(8,128)(2,1)} %get-tuple-element.449), channel_id=1, source_target_pairs={{0,1},{1,2},{2,3},{3,4},{4,5},{5,6},{6,7},{7,8},{8,9},{9,10},{10,1... | collective-permute-start | bytes 786440 | tf_op jit(solution)/shard_map/while/body/eval_jaxpr/ppermute | solution.py:18
  42.1 7.9 %collective-permute-start = (bf16[128,1024]{1,0:T(8,128)(2,1)}, bf16[128,1024]{1,0:T(8,128)(2,1)S(1)}, u32[]{:S(2)}, u32[]{:S(2)}) collective-permute-start(bf16[128,1024]{1,0:T(8,128)(2,1)} %get-tuple-element.449), channel_id=1, source_target_pairs={{0,1},{1,2},{2,3},{3,4},{4,5},{5,6},{6,7},{7,8},{8,9},{9,10},{10,1... | collective-permute-start | bytes 786440 | tf_op jit(solution)/shard_map/while/body/eval_jaxpr/ppermute | solution.py:18
  50.8 7.9 %collective-permute-start = (bf16[128,1024]{1,0:T(8,128)(2,1)}, bf16[128,1024]{1,0:T(8,128)(2,1)S(1)}, u32[]{:S(2)}, u32[]{:S(2)}) collective-permute-start(bf16[128,1024]{1,0:T(8,128)(2,1)} %get-tuple-element.449), channel_id=1, source_target_pairs={{0,1},{1,2},{2,3},{3,4},{4,5},{5,6},{6,7},{7,8},{8,9},{9,10},{10,1... | collective-permute-start | bytes 786440 | tf_op jit(solution)/shard_map/while/body/eval_jaxpr/ppermute | solution.py:18
  59.4 7.9 %collective-permute-start = (bf16[128,1024]{1,0:T(8,128)(2,1)}, bf16[128,1024]{1,0:T(8,128)(2,1)S(1)}, u32[]{:S(2)}, u32[]{:S(2)}) collective-permute-start(bf16[128,1024]{1,0:T(8,128)(2,1)} %get-tuple-element.449), channel_id=1, source_target_pairs={{0,1},{1,2},{2,3},{3,4},{4,5},{5,6},{6,7},{7,8},{8,9},{9,10},{10,1... | collective-permute-start | bytes 786440 | tf_op jit(solution)/shard_map/while/body/eval_jaxpr/ppermute | solution.py:18
  68.1 7.9 %collective-permute-start = (bf16[128,1024]{1,0:T(8,128)(2,1)}, bf16[128,1024]{1,0:T(8,128)(2,1)S(1)}, u32[]{:S(2)}, u32[]{:S(2)}) collective-permute-start(bf16[128,1024]{1,0:T(8,128)(2,1)} %get-tuple-element.449), channel_id=1, source_target_pairs={{0,1},{1,2},{2,3},{3,4},{4,5},{5,6},{6,7},{7,8},{8,9},{9,10},{10,1... | collective-permute-start | bytes 786440 | tf_op jit(solution)/shard_map/while/body/eval_jaxpr/ppermute | solution.py:18
  181.4 7.9 %collective-permute-start.1 = (f32[128,1024]{1,0:T(8,128)S(1)}, f32[128,1024]{1,0:T(8,128)S(1)}, u32[]{:S(2)}, u32[]{:S(2)}) collective-permute-start(f32[128,1024]{1,0:T(8,128)S(1)} %get-tuple-element.505), channel_id=1, source_target_pairs={{1,0},{2,1},{3,2},{4,3},{5,4},{6,5},{7,6},{8,7},{9,8},{10,9},{11,1... | collective-permute-start | bytes 1572872 | tf_op jit(solution)/shard_map/while/body/eval_jaxpr/ppermute | solution.py:18
  190.4 11.1 %collective-permute-start.1 = (f32[128,1024]{1,0:T(8,128)S(1)}, f32[128,1024]{1,0:T(8,128)S(1)}, u32[]{:S(2)}, u32[]{:S(2)}) collective-permute-start(f32[128,1024]{1,0:T(8,128)S(1)} %get-tuple-element.505), channel_id=1, source_target_pairs={{1,0},{2,1},{3,2},{4,3},{5,4},{6,5},{7,6},{8,7},{9,8},{10,9},{11,1... | collective-permute-start | bytes 1572872 | tf_op jit(solution)/shard_map/while/body/eval_jaxpr/ppermute | solution.py:18
  202.7 10.5 %collective-permute-start.1 = (f32[128,1024]{1,0:T(8,128)S(1)}, f32[128,1024]{1,0:T(8,128)S(1)}, u32[]{:S(2)}, u32[]{:S(2)}) collective-permute-start(f32[128,1024]{1,0:T(8,128)S(1)} %get-tuple-element.505), channel_id=1, source_target_pairs={{1,0},{2,1},{3,2},{4,3},{5,4},{6,5},{7,6},{8,7},{9,8},{10,9},{11,1... | collective-permute-start | bytes 1572872 | tf_op jit(solution)/shard_map/while/body/eval_jaxpr/ppermute | solution.py:18
  214.3 10.5 %collective-permute-start.1 = (f32[128,1024]{1,0:T(8,128)S(1)}, f32[128,1024]{1,0:T(8,128)S(1)}, u32[]{:S(2)}, u32[]{:S(2)}) collective-permute-start(f32[128,1024]{1,0:T(8,128)S(1)} %get-tuple-element.505), channel_id=1, source_target_pairs={{1,0},{2,1},{3,2},{4,3},{5,4},{6,5},{7,6},{8,7},{9,8},{10,9},{11,1... | collective-permute-start | bytes 1572872 | tf_op jit(solution)/shard_map/while/body/eval_jaxpr/ppermute | solution.py:18
  225.9 11.3 %collective-permute-start.1 = (f32[128,1024]{1,0:T(8,128)S(1)}, f32[128,1024]{1,0:T(8,128)S(1)}, u32[]{:S(2)}, u32[]{:S(2)}) collective-permute-start(f32[128,1024]{1,0:T(8,128)S(1)} %get-tuple-element.505), channel_id=1, source_target_pairs={{1,0},{2,1},{3,2},{4,3},{5,4},{6,5},{7,6},{8,7},{9,8},{10,9},{11,1... | collective-permute-start | bytes 1572872 | tf_op jit(solution)/shard_map/while/body/eval_jaxpr/ppermute | solution.py:18
  238.3 11.4 %collective-permute-start.1 = (f32[128,1024]{1,0:T(8,128)S(1)}, f32[128,1024]{1,0:T(8,128)S(1)}, u32[]{:S(2)}, u32[]{:S(2)}) collective-permute-start(f32[128,1024]{1,0:T(8,128)S(1)} %get-tuple-element.505), channel_id=1, source_target_pairs={{1,0},{2,1},{3,2},{4,3},{5,4},{6,5},{7,6},{8,7},{9,8},{10,9},{11,1... | collective-permute-start | bytes 1572872 | tf_op jit(solution)/shard_map/while/body/eval_jaxpr/ppermute | solution.py:18
  250.8 11.4 %collective-permute-start.1 = (f32[128,1024]{1,0:T(8,128)S(1)}, f32[128,1024]{1,0:T(8,128)S(1)}, u32[]{:S(2)}, u32[]{:S(2)}) collective-permute-start(f32[128,1024]{1,0:T(8,128)S(1)} %get-tuple-element.505), channel_id=1, source_target_pairs={{1,0},{2,1},{3,2},{4,3},{5,4},{6,5},{7,6},{8,7},{9,8},{10,9},{11,1... | collective-permute-start | bytes 1572872 | tf_op jit(solution)/shard_map/while/body/eval_jaxpr/ppermute | solution.py:18
  263.3 11.4 %collective-permute-start.1 = (f32[128,1024]{1,0:T(8,128)S(1)}, f32[128,1024]{1,0:T(8,128)S(1)}, u32[]{:S(2)}, u32[]{:S(2)}) collective-permute-start(f32[128,1024]{1,0:T(8,128)S(1)} %get-tuple-element.505), channel_id=1, source_target_pairs={{1,0},{2,1},{3,2},{4,3},{5,4},{6,5},{7,6},{8,7},{9,8},{10,9},{11,1... | collective-permute-start | bytes 1572872 | tf_op jit(solution)/shard_map/while/body/eval_jaxpr/ppermute | solution.py:18
  275.8 77.6 %copy-start.7 = (f32[1,512]{1,0:T(1,128)S(1)}, f32[1,512]{1,0:T(1,128)}, u32[]{:S(2)}) copy-start(f32[1,512]{1,0:T(1,128)} %copy-done.6) | copy-start | bytes 6148
  275.8 77.6 %copy-start.9 = (f32[1,512]{1,0:T(1,128)S(1)}, f32[1,512]{1,0:T(1,128)}, u32[]{:S(2)}) copy-start(f32[1,512]{1,0:T(1,128)} %copy-done.8) | copy-start | bytes 6148
  275.8 77.6 %copy-start.11 = (f32[1,512]{1,0:T(1,128)S(1)}, f32[1,512]{1,0:T(1,128)}, u32[]{:S(2)}) copy-start(f32[1,512]{1,0:T(1,128)} %copy-done.10) | copy-start | bytes 6148
  275.8 77.6 %copy-start.13 = (f32[1,512]{1,0:T(1,128)S(1)}, f32[1,512]{1,0:T(1,128)}, u32[]{:S(2)}) copy-start(f32[1,512]{1,0:T(1,128)} %copy-done.12) | copy-start | bytes 6148
  277.5 76.0 %collective-permute-start.3 = (f32[3,512]{0,1:T(8,128)S(1)}, f32[3,512]{0,1:T(8,128)S(1)}, u32[]{:S(2)}, u32[]{:S(2)}) collective-permute-start(f32[3,512]{0,1:T(8,128)S(1)} %copy.58), channel_id=1, source_target_pairs={{1,0},{2,1},{3,2},{4,3},{5,4},{6,5},{7,6},{8,7},{9,8},{10,9},{11,1... | collective-permute-start | bytes 18440 | tf_op jit(solution)/shard_map/ppermute | solution.py:18
  (8 other events, 32.9 us)
where the time goes:
time: 357 us; the launch traced here: 355 us
  waiting for transfers between devices  85.8 us (24%)
  blocking collectives  73 us (20%)
  starting transfers between devices  62 us (17%)
  matrix products  54 us (15%)
  local copies, waits for them, and re-layouts  52.1 us (15%)
  other arithmetic  26.4 us (7%)
    ppermute x18, waiting for transfers between devices, passed_along(): return lax.ppermute(block, axis, route)  85.8 us
    unnamed x1, blocking collectives  73 us
    ppermute x18, starting transfers between devices, passed_along(): return lax.ppermute(block, axis, route)  62 us
    dot_general x4, matrix products, one_group(): jnp.einsum('gtl,tgd->ld', grad_score, query_head, preferred_element_type=...  17 us
    dot_general x4, matrix products, one_group(): jnp.einsum('gtl,ld->tgd', grad_score, key_head, preferred_element_type=jn...  14.3 us
    dot_general x4, matrix products, one_group(): jnp.einsum('tgd,ld->gtl', grad_head, value_head, preferred_element_type=j...  11.6 us
    add x8, other arithmetic, gather_back(): return passed_along(running, 'seq', -1) + block_part  8.77 us
    concatenate x2, local copies, waits for them, and re-layouts, on_device(): returned = jnp.concatenate([grad_key, grad_value], axis=1)  7.56 us
  transfers between devices with their start and end apart: 18, of which 16 were waited for; matrix products, arithmetic and copies ran while one was open for 2% of the time, Pallas kernels for 0%

commit v1 on v0

v1 whole, which is shorter than its diff:
```python
import functools
import math

import jax
import jax.numpy as jnp
from jax import lax
from jax.experimental import pallas as pl
from jax.experimental.pallas import tpu as pltpu
from jax.sharding import PartitionSpec as P

HEAD_SIZE = 128
WINDOW = 1024
NEG_FILL = -1e30
HALO = 16
VMEM_BYTES = 56 * 1024 * 1024


def passed_along(block, axis, distance):
    devices = range(lax.axis_size(axis))
    route = [(i - distance, i) for i in devices if i - distance in devices]
    return lax.ppermute(block, axis, route)


def whole(memory_space=pltpu.VMEM):
    return pl.BlockSpec(memory_space=memory_space)


def call(kernel, out_shape, operands, scratch=(), flops=0, smem=()):
    byte_count = sum(a.size * a.dtype.itemsize for a in operands)
    byte_count += sum(math.prod(o.shape) * o.dtype.itemsize for o in jax.tree.leaves(out_shape))
    specs = [whole(pltpu.SMEM if i in smem else pltpu.VMEM) for i in range(len(operands))]
    return pl.pallas_call(
        kernel,
        out_shape=out_shape,
        in_specs=specs,
        out_specs=jax.tree.map(lambda _: whole(), out_shape),
        scratch_shapes=list(scratch),
        cost_estimate=pl.CostEstimate(flops=flops, bytes_accessed=byte_count, transcendentals=0),
        compiler_params=pltpu.CompilerParams(vmem_limit_bytes=VMEM_BYTES),
    )(*operands)


def pack_kernel(group, queries, grad_out, keys, values, halo, taps, packed):
    rows = queries.shape[0]
    tap_count = taps.shape[0]
    width = queries.shape[1] // group
    extended = jnp.concatenate([halo[...], values[...]], axis=0).astype(jnp.float32)
    mixed = jnp.zeros(values.shape, jnp.float32)
    for index_k in range(tap_count):
        begin = HALO - index_k
        mixed = mixed + taps[index_k : index_k + 1, :] * extended[begin : begin + rows]
    mixed = mixed.astype(jnp.bfloat16)
    kv_heads = keys.shape[1] // HEAD_SIZE
    for member in range(group):
        head = slice((member * kv_heads // group) * HEAD_SIZE, (member * kv_heads // group + 1) * HEAD_SIZE)
        own = slice(member * width, (member + 1) * width)
        packed[member, :, 0:width] = queries[:, own]
        packed[member, :, width : 2 * width] = grad_out[:, own]
        packed[member, :, 2 * width : 2 * width + HEAD_SIZE] = keys[:, head]
        packed[member, :, 2 * width + HEAD_SIZE :] = mixed[:, head]


NT = (((1,), (1,)), ((), ()))
TN = (((0,), (0,)), ((), ()))
BLOCK = 256


def attend_kernel(has_before, own, before, grad_q, grad_kv, grad_before, key_all, mix_all, key_t, dkey, dmix):
    length = own.shape[0]
    width = grad_q.shape[1]
    heads = width // HEAD_SIZE
    blocks = length // BLOCK
    inv_root = 1.0 / math.sqrt(HEAD_SIZE)
    log2_scale = inv_root * math.log2(math.e)
    key_all[:length] = before[:, :HEAD_SIZE]
    mix_all[:length] = before[:, HEAD_SIZE:]
    key_all[length:] = own[:, 2 * width : 2 * width + HEAD_SIZE]
    mix_all[length:] = own[:, 2 * width + HEAD_SIZE :]
    key_t[...] = jnp.transpose(key_all[...])
    dkey[...] = jnp.zeros_like(dkey)
    dmix[...] = jnp.zeros_like(dmix)
    fill = jnp.where(has_before[0] == 0, NEG_FILL, 0.0).astype(jnp.float32)
    key_at = lax.broadcasted_iota(jnp.int32, (BLOCK, BLOCK), 0)
    query_at = lax.broadcasted_iota(jnp.int32, (BLOCK, BLOCK), 1)
    causal = key_at <= query_at

    @pl.loop(0, blocks)
    def _(step):
        first = pl.multiple_of(step * BLOCK, BLOCK)
        for head in range(heads):
            columns = slice(head * HEAD_SIZE, (head + 1) * HEAD_SIZE)
            grad_columns = slice(width + head * HEAD_SIZE, width + (head + 1) * HEAD_SIZE)
            query = own[pl.ds(first, BLOCK), columns]
            grad = own[pl.ds(first, BLOCK), grad_columns]

            def at(index):
                return pl.ds(pl.multiple_of(first + index * BLOCK, BLOCK), BLOCK)

            scores = [
                lax.dot_general(key_all[at(c), :], query, NT, preferred_element_type=jnp.float32)
                for c in range(blocks + 1)
            ]
            scores = [jnp.where(causal, scores[blocks], scores[0] + fill)] + scores[1:blocks]
            fills = [jnp.float32(0.0)] + [
                jnp.where(step + c < blocks, fill, 0.0) for c in range(1, blocks)
            ]
            peak = functools.reduce(
                jnp.maximum,
                [jnp.max(s, axis=0, keepdims=True) + f for s, f in zip(scores, fills)],
            )
            peak = peak * log2_scale
            probs = [jnp.exp2(s * log2_scale + (f - peak)) for s, f in zip(scores, fills)]
            total = functools.reduce(jnp.add, [jnp.sum(p, axis=0, keepdims=True) for p in probs])
            inverse = 1.0 / total
            grads = [
                lax.dot_general(mix_all[at(c), :], grad, NT, preferred_element_type=jnp.float32)
                for c in range(blocks + 1)
            ]
            grads = [jnp.where(causal, grads[blocks], grads[0])] + grads[1:blocks]
            probs = [p * inverse for p in probs]
            delta = functools.reduce(
                jnp.add, [jnp.sum(p * g, axis=0, keepdims=True) for p, g in zip(probs, grads)]
            )
            low = [p.astype(jnp.bfloat16) for p in probs]
            score_grads = [(p * (g - delta)).astype(jnp.bfloat16) for p, g in zip(probs, grads)]
            zero = jnp.zeros((), jnp.bfloat16)
            low = [jnp.where(causal, zero, low[0])] + low[1:] + [jnp.where(causal, low[0], zero)]
            score_grads = (
                [jnp.where(causal, zero, score_grads[0])]
                + score_grads[1:]
                + [jnp.where(causal, score_grads[0], zero)]
            )
            dquery_t = jnp.zeros((HEAD_SIZE, BLOCK), jnp.float32)
            for c in range(blocks + 1):
                dmix[at(c), :] += jnp.dot(low[c], grad, preferred_element_type=jnp.float32)
                dkey[at(c), :] += jnp.dot(score_grads[c], query, preferred_element_type=jnp.float32)
                dquery_t += jnp.dot(
                    key_t[:, at(c)], score_grads[c], preferred_element_type=jnp.float32
                )
            grad_q[pl.ds(first, BLOCK), columns] = (jnp.transpose(dquery_t) * inv_root).astype(jnp.bfloat16)

    grad_before[:, :HEAD_SIZE] = (dkey[:length] * inv_root).astype(jnp.bfloat16)
    grad_before[:, HEAD_SIZE:] = dmix[:length].astype(jnp.bfloat16)
    grad_kv[:, :HEAD_SIZE] = dkey[length:] * inv_root
    grad_kv[:, HEAD_SIZE:] = dmix[length:]


def unpack_kernel(group, received, grad_keys, grad_mixed):
    kv_heads = grad_keys.shape[1] // HEAD_SIZE
    share = group // kv_heads
    for head in range(kv_heads):
        total = received[head * share].astype(jnp.float32)
        for other in range(1, share):
            total = total + received[head * share + other].astype(jnp.float32)
        columns = slice(head * HEAD_SIZE, (head + 1) * HEAD_SIZE)
        grad_keys[:, columns] = total[:, :HEAD_SIZE].astype(jnp.bfloat16)
        grad_mixed[:, columns] = total[:, HEAD_SIZE:]


def finish_kernel(scale, grad_mixed, after, values, halo, taps, grad_values, tap_grads):
    rows = values.shape[0]
    tap_count = taps.shape[0]
    grad = grad_mixed[...]
    grad_ext = jnp.concatenate([grad, after[...]], axis=0)
    value_ext = jnp.concatenate([halo[...], values[...]], axis=0).astype(jnp.float32)
    total = jnp.zeros(values.shape, jnp.float32)
    for index_k in range(tap_count):
        total = total + taps[index_k : index_k + 1, :] * grad_ext[index_k : index_k + rows]
        begin = HALO - index_k
        tap_grads[index_k : index_k + 1, :] = (
            jnp.sum(grad * value_ext[begin : begin + rows], axis=0, keepdims=True) * scale
        )
    grad_values[...] = total.astype(jnp.bfloat16)


def on_device(queries, keys, values, conv_taps, grad_out):
    rows, width = queries.shape[1:]
    kv_width = keys.shape[2]
    group = WINDOW // rows
    count = lax.axis_size("seq")
    own_width = width // group
    groups = [[g * group + i for i in range(group)] for g in range(count // group)]
    bf16, f32 = jnp.bfloat16, jnp.float32
    shape = jax.ShapeDtypeStruct
    value_rows = values[0]
    halo = passed_along(value_rows[rows - HALO :], "seq", 1)
    packed = call(
        functools.partial(pack_kernel, group),
        shape((group, rows, 2 * own_width + 2 * HEAD_SIZE), bf16),
        (queries[0], grad_out[0], keys[0], value_rows, halo, conv_taps),
    )
    own = lax.all_to_all(packed, "seq", 0, 0, axis_index_groups=groups, tiled=True)
    own = own.reshape(WINDOW, 2 * own_width + 2 * HEAD_SIZE)
    before = passed_along(own[:, 2 * own_width :], "seq", group)
    has_before = (lax.axis_index("seq") >= group).astype(jnp.int32)[None]
    grad_q, grad_kv, grad_before = call(
        attend_kernel,
        (
            shape((WINDOW, own_width), bf16),
            shape((WINDOW, 2 * HEAD_SIZE), f32),
            shape((WINDOW, 2 * HEAD_SIZE), bf16),
        ),
        (has_before, own, before),
        scratch=[
            pltpu.VMEM((2 * WINDOW, HEAD_SIZE), bf16),
            pltpu.VMEM((2 * WINDOW, HEAD_SIZE), bf16),
            pltpu.VMEM((HEAD_SIZE, 2 * WINDOW), bf16),
            pltpu.VMEM((2 * WINDOW, HEAD_SIZE), f32),
            pltpu.VMEM((2 * WINDOW, HEAD_SIZE), f32),
        ],
        flops=10 * WINDOW * (WINDOW + BLOCK) * own_width,
        smem=(0,),
    )
    returned = passed_along(grad_before, "seq", -group)
    grad_q = lax.all_to_all(
        grad_q.reshape(group, rows, own_width), "seq", 0, 0, axis_index_groups=groups, tiled=True
    )
    grad_kv = (grad_kv + returned).astype(bf16).reshape(group, rows, 2 * HEAD_SIZE)
    grad_kv = lax.all_to_all(grad_kv, "seq", 0, 0, axis_index_groups=groups, tiled=True)
    grad_queries = grad_q.transpose(1, 0, 2).reshape(rows, width)
    grad_keys, grad_mixed = call(
        functools.partial(unpack_kernel, group),
        (shape((rows, kv_width), bf16), shape((rows, kv_width), f32)),
        (grad_kv,),
    )
    after = passed_along(grad_mixed[:8], "seq", -1)
    total_tokens = rows * count * lax.axis_size("rep")
    grad_values, tap_grads = call(
        functools.partial(finish_kernel, 1.0 / math.sqrt(total_tokens)),
        (shape((rows, kv_width), bf16), shape(conv_taps.shape, f32)),
        (grad_mixed, after, value_rows, halo, conv_taps),
    )
    shares = lax.all_to_all(tap_grads.reshape(count, -1), "seq", 0, 0, tiled=True)
    grad_taps = lax.psum(jnp.sum(shares, axis=0), "rep")
    return grad_queries[None], grad_keys[None], grad_values[None], grad_taps


def solution(mesh):
    in_specs = (
        P("rep", "seq", None),
        P("rep", "seq", None),
        P("rep", "seq", None),
        P(),
        P("rep", "seq", None),
    )
    out_specs = (P("rep", "seq", None), P("rep", "seq", None), P("rep", "seq", None), P("seq"))
    return jax.shard_map(
        on_device, mesh=mesh, in_specs=in_specs, out_specs=out_specs, check_vma=False
    )
```

time: 357 us -> 126 us (0.35)
  matrix products: 54 us -> 0 us
  waiting for transfers between devices: 85.8 us -> 32.6 us
  local copies, waits for them, and re-layouts: 52.1 us -> 6.16 us
  starting transfers between devices: 62 us -> 22.3 us
  blocking collectives: 73 us -> 41 us
  other arithmetic: 26.4 us -> 1.9 us
  Pallas kernels: 0 us -> 20.3 us
    unnamed x1 -> x0, blocking collectives: 73 us -> none
    ppermute x18 -> x4, waiting for transfers between devices: 85.8 us -> 26.7 us  [passed_along(): return lax.ppermute(block, axis, route)]
    dot_general x20 -> x0, matrix products: 54 us -> none  [the longest x4 17 us: one_group(): jnp.einsum('gtl,tgd->ld', grad_score, query_head, preferred_element_type=...]
    ppermute x18 -> x4, starting transfers between devices: 62 us -> 9.98 us  [passed_along(): return lax.ppermute(block, axis, route)]
    all_to_all x0 -> x2, blocking collectives: none -> 41 us  [the longest x1 28 us: on_device(): lax.all_to_all(packed, 'seq', 0, 0, axis_index_groups=groups, tiled=True)]
    pallas_call x0 -> x4, Pallas kernels: none -> 20.3 us  [call(): pl.pallas_call(kernel, out_shape=out_shape, in_specs=specs, out_specs=jax...]
    all_to_all x0 -> x2, starting transfers between devices: none -> 12.3 us  [the longest x1 8.85 us: on_device(): lax.all_to_all(tap_grads.reshape(count, -1), 'seq', 0, 0, tiled=True)]
    while x13 -> x0, local copies, waits for them, and re-layouts: 12.1 us -> none
  transfers between devices with their start and end apart: 18 -> 6, of which waited for: 16 -> 6; matrix products, arithmetic and copies ran while one was open for 2% -> 2% of each run, Pallas kernels for 0% -> 3%
where the time goes in v1:
time: 126 us; the launch traced here: 125 us
  blocking collectives  41 us (33%)
  waiting for transfers between devices  32.6 us (26%)
  starting transfers between devices  22.3 us (18%)
  Pallas kernels  20.3 us (16%)
  local copies, waits for them, and re-layouts  6.16 us (5%)
  other arithmetic  1.9 us (2%)
    all_to_all x1, blocking collectives, on_device(): lax.all_to_all(packed, 'seq', 0, 0, axis_index_groups=groups, tiled=True)  28 us
    ppermute x4, waiting for transfers between devices, passed_along(): return lax.ppermute(block, axis, route)  26.7 us
    pallas_call x4, Pallas kernels, call(): pl.pallas_call(kernel, out_shape=out_shape, in_specs=specs, out_specs=jax...  20.3 us
    all_to_all x1, blocking collectives, on_device(): lax.all_to_all(grad_kv, 'seq', 0, 0, axis_index_groups=groups, tiled=True)  13 us
    ppermute x4, starting transfers between devices, passed_along(): return lax.ppermute(block, axis, route)  9.98 us
    all_to_all x1, starting transfers between devices, on_device(): lax.all_to_all(tap_grads.reshape(count, -1), 'seq', 0, 0, tiled=True)  8.85 us
    all_to_all x1, waiting for transfers between devices, on_device(): lax.all_to_all(tap_grads.reshape(count, -1), 'seq', 0, 0, tiled=True)  5.81 us
    all_to_all x1, starting transfers between devices, on_device(): lax.all_to_all(grad_q.reshape(group, rows, own_width), 'seq', 0, 0, axis_...  3.49 us
  transfers between devices with their start and end apart: 6, of which 6 were waited for; matrix products, arithmetic and copies ran while one was open for 2% of the time, Pallas kernels for 3%

profile of v1, /device:TPU:0, one launch (start us, length us, event | category | flops | bytes accessed | tf_op | source)
XLA Modules:
  0.0 125.0 jit_solution(3380351935217751129)
XLA Ops:
  0.6 0.7 slice_bitcast_fusion
  1.4 2.3 %collective-permute-start = (bf16[16,512]{1,0:T(8,128)(2,1)S(1)}, bf16[16,512]{1,0:T(8,128)(2,1)S(1)}, u32[]{:S(2)}, u32[]{:S(2)}) collective-permute-start(bf16[16,512]{1,0:T(8,128)(2,1)S(1)} %slice_bitcast_fusion), channel_id=1, source_target_pairs={{0,1},{1,2},{2,3},{3,4},{4,5},{5,6},{6,7},{7,8},{8,9},{9,10},{10,1... | collective-permute-start | bytes 49160 | tf_op jit(solution)/shard_map/ppermute | solution.py:21
  3.7 0.8 collective-permute-done.halo
  5.1 2.6 %shard_map.84 = bf16[8,128,768]{2,1,0:T(8,128)(2,1)} custom-call(bf16[128,2048]{1,0:T(8,128)(2,1)} %bitcast.20, bf16[128,2048]{1,0:T(8,128)(2,1)} %bitcast.21, bf16[128,512]{1,0:T(8,128)(2,1)} %bitcast.22, bf16[128,512]{1,0:T(8,128)(2,1)} %bitcast.18, bf16[16,512]{1,0:T(8,128)(2,1)} %copy-done.1, f32[4,512]{1,0:T(4,128)} %taps.3), custom_call_target="tpu_custom_call" | custom-call | bytes 2908160 | tf_op jit(solution)/shard_map/pallas_call | solution.py:32
  7.8 28.0 %all_to_all.24 = bf16[8,128,768]{2,1,0:T(8,128)(2,1)S(1)} all-to-all(bf16[8,128,768]{2,1,0:T(8,128)(2,1)} %shard_map.84), channel_id=1, replica_groups={{0,1,2,3,4,5,6,7},{8,9,10,11,12,13,14,15},{16,17,18,19,20,21,22,23},{24..., dimensions={0} | all-to-all | bytes 3145728 | tf_op jit(solution)/shard_map/all_to_all | solution.py:192
  35.8 5.1 %collective-permute-start.1 = (bf16[1024,256]{1,0:T(8,128)(2,1)S(1)}, bf16[1024,256]{1,0:T(8,128)(2,1)S(1)}, u32[]{:S(2)}, u32[]{:S(2)}) collective-permute-start(bf16[1024,256]{1,0:T(8,128)(2,1)S(1)} %slice.16), channel_id=1, source_target_pairs={{0,8},{1,9},{2,10},{3,11},{4,12},{5,13},{6,14},{7,15},{8,16},{9,17... | collective-permute-start | bytes 1572872 | tf_op jit(solution)/shard_map/ppermute | solution.py:21
  40.9 10.5 %collective-permute-done.1.before = bf16[1024,256]{1,0:T(8,128)(2,1)S(1)} collective-permute-done((bf16[1024,256]{1,0:T(8,128)(2,1)S(1)}, bf16[1024,256]{1,0:T(8,128)(2,1)S(1)}, u32[]{:S(2)}, u32[]{:S(2)}) %collective-permute-start.1) | collective-permute-done | bytes 524320 | tf_op jit(solution)/shard_map/ppermute | solution.py:21
  51.4 0.8 copy-done.3
  52.2 13.8 %shard_map.85 = (bf16[1024,256]{1,0:T(8,128)(2,1)}, f32[1024,256]{1,0:T(8,128)}, bf16[1024,256]{1,0:T(8,128)(2,1)}) custom-call(s32[1]{0:T(128)} %bitcast.has_before, bf16[1024,768]{1,0:T(8,128)(2,1)} %bitcast.15, bf16[1024,256]{1,0:T(8,128)(2,1)} %copy-done.3), custom_call_target="tpu_custom_call" | custom-call | flops 3355443200 | bytes 4194308 | tf_op jit(solution)/shard_map/pallas_call | solution.py:32
  66.0 1.3 %collective-permute-start.2 = (bf16[1024,256]{1,0:T(8,128)(2,1)}, bf16[1024,256]{1,0:T(8,128)(2,1)S(1)}, u32[]{:S(2)}, u32[]{:S(2)}) collective-permute-start(bf16[1024,256]{1,0:T(8,128)(2,1)} %get-tuple-element.13), channel_id=1, source_target_pairs={{8,0},{9,1},{10,2},{11,3},{12,4},{13,5},{14,6},{15,7},{16,8},{17,9... | collective-permute-start | bytes 1572872 | tf_op jit(solution)/shard_map/ppermute | solution.py:21
  67.2 13.6 %collective-permute-done.2 = bf16[1024,256]{1,0:T(8,128)(2,1)S(1)} collective-permute-done((bf16[1024,256]{1,0:T(8,128)(2,1)}, bf16[1024,256]{1,0:T(8,128)(2,1)S(1)}, u32[]{:S(2)}, u32[]{:S(2)}) %collective-permute-start.2) | collective-permute-done | bytes 524320 | tf_op jit(solution)/shard_map/ppermute | solution.py:21
  80.9 1.3 %add_convert_fusion = bf16[1024,256]{1,0:T(8,128)(2,1)S(1)} fusion(f32[1024,256]{1,0:T(8,128)} %get-tuple-element.12, bf16[1024,256]{1,0:T(8,128)(2,1)S(1)} %collective-permute-done.2), kind=kLoop, calls=%fused_computation | loop fusion | flops 786432 | bytes 2097152 | tf_op jit(solution)/shard_map/convert_element_type | solution.py:218
  82.2 13.0 %all_to_all.25.received = bf16[8,128,256]{2,1,0:T(8,128)(2,1)} all-to-all(bf16[8,128,256]{2,1,0:T(8,128)(2,1)S(1)} %bitcast.17), channel_id=1, replica_groups={{0,1,2,3,4,5,6,7},{8,9,10,11,12,13,14,15},{16,17,18,19,20,21,22,23},{24..., dimensions={0} | all-to-all | bytes 1048576 | tf_op jit(solution)/shard_map/all_to_all | solution.py:219
  95.3 3.5 %all-to-all-start.1 = ((bf16[8,128,256]{2,1,0:T(8,128)(2,1)}), bf16[8,128,256]{2,1,0:T(8,128)(2,1)S(1)}, u32[]{:S(2)}, u32[]{:S(2)}) async-start(bf16[8,128,256]{2,1,0:T(8,128)(2,1)} %bitcast.7), calls=%async_computation.1 | async-start | bytes 1048576 | tf_op jit(solution)/shard_map/all_to_all | solution.py:215
  98.8 1.9 %shard_map.86 = (bf16[128,512]{1,0:T(8,128)(2,1)}, f32[128,512]{1,0:T(8,128)}) custom-call(bf16[8,128,256]{2,1,0:T(8,128)(2,1)} %all_to_all.25.received), custom_call_target="tpu_custom_call" | custom-call | bytes 917504 | tf_op jit(solution)/shard_map/pallas_call | solution.py:32
  100.6 0.7 slice.15
  101.3 1.3 %collective-permute-start.3 = (f32[8,512]{1,0:T(8,128)S(1)}, f32[8,512]{1,0:T(8,128)S(1)}, u32[]{:S(2)}, u32[]{:S(2)}) collective-permute-start(f32[8,512]{1,0:T(8,128)S(1)} %slice.15), channel_id=1, source_target_pairs={{1,0},{2,1},{3,2},{4,3},{5,4},{6,5},{7,6},{8,7},{9,8},{10,9},{11,1... | collective-permute-start | bytes 49160 | tf_op jit(solution)/shard_map/ppermute | solution.py:21
  102.6 1.8 %collective-permute-done.3.after = f32[8,512]{1,0:T(8,128)S(1)} collective-permute-done((f32[8,512]{1,0:T(8,128)S(1)}, f32[8,512]{1,0:T(8,128)S(1)}, u32[]{:S(2)}, u32[]{:S(2)}) %collective-permute-start.3) | collective-permute-done | bytes 16416 | tf_op jit(solution)/shard_map/ppermute | solution.py:21
  104.4 0.6 copy-done.2
  105.0 2.0 %shard_map.87 = (bf16[128,512]{1,0:T(8,128)(2,1)}, f32[4,512]{1,0:T(4,128)}) custom-call(f32[128,512]{1,0:T(8,128)} %get-tuple-element.15.grad_mixed, f32[8,512]{1,0:T(8,128)} %copy-done.2, bf16[128,512]{1,0:T(8,128)(2,1)} %bitcast.19, bf16[16,512]{1,0:T(8,128)(2,1)} %copy-done.1, f32[4,512]{1,0:T(4,128)} %taps.3), custom_call_target="tpu_custom_call" | custom-call | bytes 573440 | tf_op jit(solution)/shard_map/pallas_call | solution.py:32
  107.0 1.4 %all_to_all.18 = f32[32,1,64]{2,0,1:T(8,128)} reshape(f32[4,512]{1,0:T(4,128)} %get-tuple-element.17) | data formatting | bytes 16384 | tf_op jit(solution)/shard_map/all_to_all | solution.py:233
  108.4 8.9 %all-to-all-start.3 = ((f32[32,1,64]{2,1,0:T(1,128)}), f32[32,1,64]{2,1,0:T(1,128)S(1)}, u32[]{:S(2)}, u32[]{:S(2)}) async-start(f32[32,1,64]{2,1,0:T(1,128)} %bitcast.12), calls=%async_computation.3 | async-start | bytes 32768 | tf_op jit(solution)/shard_map/all_to_all | solution.py:233
  117.6 1.0 broadcast_in_dim_reshape.3
  118.6 5.8 %all-to-all-done.3 = f32[32,1,64]{2,1,0:T(1,128)S(1)} async-done(((f32[32,1,64]{2,1,0:T(1,128)}), f32[32,1,64]{2,1,0:T(1,128)S(1)}, u32[]{:S(2)}, u32[]{:S(2)}) %all-to-all-start.3) | async-done | bytes 8224 | tf_op jit(solution)/shard_map/all_to_all | solution.py:233
  (10 shorter events, 1.6 us)
Async XLA Ops:
  1.4 3.2 %collective-permute-start = (bf16[16,512]{1,0:T(8,128)(2,1)S(1)}, bf16[16,512]{1,0:T(8,128)(2,1)S(1)}, u32[]{:S(2)}, u32[]{:S(2)}) collective-permute-start(bf16[16,512]{1,0:T(8,128)(2,1)S(1)} %slice_bitcast_fusion), channel_id=1, source_target_pairs={{0,1},{1,2},{2,3},{3,4},{4,5},{5,6},{6,7},{7,8},{8,9},{9,10},{10,1... | collective-permute-start | bytes 49160 | tf_op jit(solution)/shard_map/ppermute | solution.py:21
  4.5 0.6 copy-start.1
  35.8 15.6 %copy-start = (bf16[8,128,768]{2,1,0:T(8,128)(2,1)}, bf16[8,128,768]{2,1,0:T(8,128)(2,1)S(1)}, u32[]{:S(2)}) copy-start(bf16[8,128,768]{2,1,0:T(8,128)(2,1)S(1)} %all_to_all.24) | copy-start | bytes 4718596
  35.8 15.6 %collective-permute-start.1 = (bf16[1024,256]{1,0:T(8,128)(2,1)S(1)}, bf16[1024,256]{1,0:T(8,128)(2,1)S(1)}, u32[]{:S(2)}, u32[]{:S(2)}) collective-permute-start(bf16[1024,256]{1,0:T(8,128)(2,1)S(1)} %slice.16), channel_id=1, source_target_pairs={{0,8},{1,9},{2,10},{3,11},{4,12},{5,13},{6,14},{7,15},{8,16},{9,17... | collective-permute-start | bytes 1572872 | tf_op jit(solution)/shard_map/ppermute | solution.py:21
  51.4 0.8 copy-start.3
  66.0 14.9 %collective-permute-start.2 = (bf16[1024,256]{1,0:T(8,128)(2,1)}, bf16[1024,256]{1,0:T(8,128)(2,1)S(1)}, u32[]{:S(2)}, u32[]{:S(2)}) collective-permute-start(bf16[1024,256]{1,0:T(8,128)(2,1)} %get-tuple-element.13), channel_id=1, source_target_pairs={{8,0},{9,1},{10,2},{11,3},{12,4},{13,5},{14,6},{15,7},{16,8},{17,9... | collective-permute-start | bytes 1572872 | tf_op jit(solution)/shard_map/ppermute | solution.py:21
  95.3 13.2 %all-to-all-start.1 = ((bf16[8,128,256]{2,1,0:T(8,128)(2,1)}), bf16[8,128,256]{2,1,0:T(8,128)(2,1)S(1)}, u32[]{:S(2)}, u32[]{:S(2)}) async-start(bf16[8,128,256]{2,1,0:T(8,128)(2,1)} %bitcast.7), calls=%async_computation.1 | async-start | bytes 1048576 | tf_op jit(solution)/shard_map/all_to_all | solution.py:215
  101.3 3.1 %collective-permute-start.3 = (f32[8,512]{1,0:T(8,128)S(1)}, f32[8,512]{1,0:T(8,128)S(1)}, u32[]{:S(2)}, u32[]{:S(2)}) collective-permute-start(f32[8,512]{1,0:T(8,128)S(1)} %slice.15), channel_id=1, source_target_pairs={{1,0},{2,1},{3,2},{4,3},{5,4},{6,5},{7,6},{8,7},{9,8},{10,9},{11,1... | collective-permute-start | bytes 49160 | tf_op jit(solution)/shard_map/ppermute | solution.py:21
  104.4 0.6 copy-start.2
  108.4 16.0 %all-to-all-start.3 = ((f32[32,1,64]{2,1,0:T(1,128)}), f32[32,1,64]{2,1,0:T(1,128)S(1)}, u32[]{:S(2)}, u32[]{:S(2)}) async-start(f32[32,1,64]{2,1,0:T(1,128)} %bitcast.12), calls=%async_computation.3 | async-start | bytes 32768 | tf_op jit(solution)/shard_map/all_to_all | solution.py:233

commit v2 on v0

v2 whole, which is shorter than its diff:
```python
import functools
import math

import jax
import jax.numpy as jnp
from jax import lax
from jax.experimental import pallas as pl
from jax.experimental.pallas import tpu as pltpu
from jax.sharding import PartitionSpec as P

HEAD_SIZE = 128
WINDOW = 1024
NEG_FILL = -1e30
HALO = 16
VMEM_BYTES = 56 * 1024 * 1024
NT = (((1,), (1,)), ((), ()))


def attend_kernel(
    place, query_grad, kv_same, kv_other, old_same, old_other, halo, all_taps,
    grad_q, send, keep, grad_halo, tap_grads,
    key_all, key_t, value_all, mix_all, dkey, dmix,
):
    blocks, rows = query_grad.shape[:2]
    width = grad_q.shape[2]
    span = 2 * blocks
    length = span * rows
    lanes = 2 * HEAD_SIZE
    tap_count = all_taps.shape[0]
    has_before, parity, head_at = place[0], place[1], place[2]
    taps = all_taps[:, pl.ds(pl.multiple_of(head_at * HEAD_SIZE, HEAD_SIZE), HEAD_SIZE)]
    inv_root = 1.0 / math.sqrt(HEAD_SIZE)
    log2_scale = inv_root * math.log2(math.e)

    def block(index, offset=0):
        return pl.ds(pl.multiple_of(index * rows, rows) + offset, rows)

    value_all[:HALO] = halo[...].astype(jnp.float32)
    for start, same, other in ((0, old_same, old_other), (span, kv_same, kv_other)):
        for index in range(blocks):
            for source, at in ((same, start + 2 * index + parity), (other, start + 2 * index + 1 - parity)):
                key_all[block(at)] = source[index, :, :HEAD_SIZE]
                value_all[block(at, HALO)] = source[index, :, HEAD_SIZE:].astype(jnp.float32)
    mixed = taps[0:1] * value_all[HALO:]
    for index_k in range(1, tap_count):
        mixed = mixed + taps[index_k : index_k + 1] * value_all[HALO - index_k : HALO - index_k + 2 * length]
    mix_all[...] = mixed.astype(jnp.bfloat16)
    key_t[...] = jnp.transpose(key_all[...])
    dkey[...] = jnp.zeros_like(dkey)
    dmix[...] = jnp.zeros_like(dmix)
    fill = jnp.where(has_before == 0, NEG_FILL, 0.0).astype(jnp.float32)
    key_at = lax.broadcasted_iota(jnp.int32, (rows, lanes), 0)
    query_at = lax.broadcasted_iota(jnp.int32, (rows, lanes), 1) & (rows - 1)
    causal = key_at <= query_at

    @pl.loop(0, blocks)
    def _(step):
        number = 2 * step + parity
        first = pl.multiple_of(number * rows, rows)
        seen = pl.ds(first, length + rows)
        seen_halo = pl.ds(first + HALO, length + rows)
        keys = key_all[seen]
        mix = mix_all[seen]
        keys_t = key_t[:, seen]
        for pair in range(width // lanes):

            def stacked(base):
                return jnp.concatenate(
                    [query_grad[step, :, base + h * HEAD_SIZE : base + (h + 1) * HEAD_SIZE] for h in range(2)], axis=0
                )

            query = stacked(pair * lanes)
            grad = stacked(width + pair * lanes)
            scores = lax.dot_general(keys, query, NT, preferred_element_type=jnp.float32)
            grads = lax.dot_general(mix, grad, NT, preferred_element_type=jnp.float32)

            def folded(array, extra):
                edge = jnp.where(causal, array[length:], array[:rows] + extra if extra is not None else array[:rows])
                return [edge] + [array[c * rows : (c + 1) * rows] for c in range(1, span)]

            scores = folded(scores, fill)
            grads = folded(grads, None)
            fills = [jnp.float32(0.0)] + [jnp.where(number + c < span, fill, 0.0) for c in range(1, span)]
            peak = functools.reduce(
                jnp.maximum, [jnp.max(s, axis=0, keepdims=True) + f for s, f in zip(scores, fills)]
            )
            peak = peak * log2_scale
            probs = [jnp.exp2(s * log2_scale + (f - peak)) for s, f in zip(scores, fills)]
            total = functools.reduce(jnp.add, [jnp.sum(p, axis=0, keepdims=True) for p in probs])
            inverse = 1.0 / total
            probs = [p * inverse for p in probs]
            delta = functools.reduce(
                jnp.add, [jnp.sum(p * g, axis=0, keepdims=True) for p, g in zip(probs, grads)]
            )

            def unfolded(parts):
                zero = jnp.zeros((), jnp.bfloat16)
                low = [p.astype(jnp.bfloat16) for p in parts]
                return jnp.concatenate(
                    [jnp.where(causal, zero, low[0])] + low[1:] + [jnp.where(causal, low[0], zero)], axis=0
                )

            low = unfolded(probs)
            score_grads = unfolded([p * (g - delta) for p, g in zip(probs, grads)])
            dmix[seen_halo] += jnp.dot(low, grad, preferred_element_type=jnp.float32)
            dkey[seen] += jnp.dot(score_grads, query, preferred_element_type=jnp.float32)
            dquery = jnp.dot(keys_t, score_grads, preferred_element_type=jnp.float32)
            dquery = (jnp.transpose(dquery) * inv_root).astype(jnp.bfloat16)
            for h in range(2):
                base = pair * lanes + h * HEAD_SIZE
                grad_q[step, :, base : base + HEAD_SIZE] = dquery[h * rows : (h + 1) * rows]

    def convolved(start, count):
        total = taps[0:1] * dmix[pl.ds(start, count)]
        for index_k in range(1, tap_count):
            total = total + taps[index_k : index_k + 1] * dmix[pl.ds(start + index_k, count)]
        return total

    grad_halo[...] = convolved(0, HALO)
    for index in range(span):
        for target, at in ((keep, 2 * index + parity), (send, 2 * index + 1 - parity)):
            target[index, :, :HEAD_SIZE] = (dkey[block(at)] * inv_root).astype(target.dtype)
            target[index, :, HEAD_SIZE:] = convolved(pl.multiple_of(at * rows, rows) + HALO, rows).astype(target.dtype)
    for index_k in range(tap_count):
        tap_grads[index_k : index_k + 1] = jnp.sum(
            dmix[HALO : HALO + 2 * length] * value_all[HALO - index_k : HALO - index_k + 2 * length], axis=0, keepdims=True
        )


def on_device(queries, keys, values, conv_taps, grad_out):
    rows, width = queries.shape[1:]
    kv_width = keys.shape[2]
    tap_count = conv_taps.shape[0]
    kv_heads = kv_width // HEAD_SIZE
    group = WINDOW // rows
    share = group // kv_heads
    count = lax.axis_size("seq")
    planes = count // group
    own_width = width // kv_heads
    bf16, f32 = jnp.bfloat16, jnp.float32
    shape = jax.ShapeDtypeStruct
    device = lax.axis_index("seq")
    parity = device % share
    head_at = (device % group) // share
    same_core = [
        [g * group + j * share + c for j in range(kv_heads)] for g in range(planes) for c in range(share)
    ]
    across = [[g * group + p for g in range(planes)] for p in range(group)]

    def swap(array, groups):
        return lax.all_to_all(array, "seq", 0, 0, axis_index_groups=groups, tiled=True)

    def shifted(array, distance):
        route = [(i, i + distance) for i in range(count) if 0 <= i + distance < count]
        return lax.ppermute(array, "seq", route)

    def on_chip(array):
        return lax.ppermute(array, "seq", [(i, i ^ 1) for i in range(count)])

    def by_head(array):
        return array.reshape(rows, kv_heads, -1).transpose(1, 0, 2)

    kv_same = swap(jnp.concatenate([by_head(keys[0]), by_head(values[0])], axis=2), same_core)
    query_grad = swap(jnp.concatenate([by_head(queries[0]), by_head(grad_out[0])], axis=2), same_core)
    old_same = shifted(kv_same, group)
    kv_other = on_chip(kv_same)
    reach = 2 * group - (share - 1)
    halo = lax.ppermute(
        kv_same[kv_heads - 1, rows - HALO :, HEAD_SIZE:],
        "seq",
        [(i - reach, i) for i in range(count) if i % share == 0 and i - reach >= 0],
    )
    old_other = on_chip(old_same)
    place = jnp.stack([(device >= group).astype(jnp.int32), parity, head_at])
    span = 2 * kv_heads
    operands = (place, query_grad, kv_same, kv_other, old_same, old_other, halo, conv_taps)
    vmem = pl.BlockSpec(memory_space=pltpu.VMEM)
    grad_q, send, keep, grad_halo, tap_grads = pl.pallas_call(
        attend_kernel,
        out_shape=(
            shape((kv_heads, rows, own_width), bf16),
            shape((span, rows, 2 * HEAD_SIZE), bf16),
            shape((span, rows, 2 * HEAD_SIZE), f32),
            shape((HALO, HEAD_SIZE), f32),
            shape((tap_count, HEAD_SIZE), f32),
        ),
        in_specs=[pl.BlockSpec(memory_space=pltpu.SMEM)] + [vmem] * 7,
        out_specs=(vmem,) * 5,
        scratch_shapes=[
            pltpu.VMEM((2 * WINDOW, HEAD_SIZE), bf16),
            pltpu.VMEM((HEAD_SIZE, 2 * WINDOW), bf16),
            pltpu.VMEM((HALO + 2 * WINDOW, HEAD_SIZE), f32),
            pltpu.VMEM((2 * WINDOW, HEAD_SIZE), bf16),
            pltpu.VMEM((2 * WINDOW, HEAD_SIZE), f32),
            pltpu.VMEM((HALO + 2 * WINDOW + HALO, HEAD_SIZE), f32),
        ],
        cost_estimate=pl.CostEstimate(
            flops=10 * kv_heads * rows * (WINDOW + rows) * own_width, bytes_accessed=5 << 20, transcendentals=0
        ),
        compiler_params=pltpu.CompilerParams(vmem_limit_bytes=VMEM_BYTES),
    )(*operands)
    partial = keep + on_chip(send).astype(f32)
    returned = shifted(partial[:kv_heads].astype(bf16), -group)
    grad_queries = swap(grad_q, same_core).transpose(1, 0, 2).reshape(rows, width)
    returned_halo = lax.ppermute(
        grad_halo, "seq", [(i, i - reach) for i in range(count) if i % share == 0 and i - reach >= 0]
    )
    total = partial[kv_heads:] + returned.astype(f32)
    total = total.at[kv_heads - 1, rows - HALO :, HEAD_SIZE:].add(returned_halo)
    total = swap(total.astype(bf16), same_core).transpose(1, 0, 2)
    grad_keys = total[:, :, :HEAD_SIZE].reshape(rows, kv_width)
    grad_values = total[:, :, HEAD_SIZE:].reshape(rows, kv_width)
    tap_grads = tap_grads * (1.0 / math.sqrt(rows * count * lax.axis_size("rep")))
    if planes == tap_count and share == 2:
        own_tap = jnp.sum(swap(tap_grads, across), axis=0).reshape(share, -1)
        mine = jnp.where(parity == 0, own_tap[0], own_tap[1])
        theirs = jnp.where(parity == 0, own_tap[1], own_tap[0])
        grad_taps = mine + on_chip(theirs)
    else:
        spread = jnp.zeros((tap_count, kv_width), f32)
        spread = lax.dynamic_update_slice(spread, tap_grads, (0, head_at * HEAD_SIZE))
        grad_taps = jnp.sum(swap(spread.reshape(count, -1), None), axis=0)
    grad_taps = lax.psum(grad_taps, "rep")
    return grad_queries[None], grad_keys[None], grad_values[None], grad_taps


def solution(mesh):
    in_specs = (
        P("rep", "seq", None),
        P("rep", "seq", None),
        P("rep", "seq", None),
        P(),
        P("rep", "seq", None),
    )
    out_specs = (P("rep", "seq", None), P("rep", "seq", None), P("rep", "seq", None), P("seq"))
    return jax.shard_map(
        on_device, mesh=mesh, in_specs=in_specs, out_specs=out_specs, check_vma=False
    )
```

time: 357 us -> 88.2 us (0.25)
  blocking collectives: 73 us -> 0 us
  waiting for transfers between devices: 85.8 us -> 26 us
  matrix products: 54 us -> 0 us
  local copies, waits for them, and re-layouts: 52.1 us -> 8.09 us
  starting transfers between devices: 62 us -> 31.2 us
  other arithmetic: 26.4 us -> 5.93 us
  Pallas kernels: 0 us -> 15.5 us
    ppermute x18 -> x8, waiting for transfers between devices: 85.8 us -> 5.97 us  [the longest x2 4 us: shifted(): return lax.ppermute(array, 'seq', route)]
    unnamed x1 -> x0, blocking collectives: 73 us -> none
    dot_general x20 -> x0, matrix products: 54 us -> none  [the longest x4 17 us: one_group(): jnp.einsum('gtl,tgd->ld', grad_score, query_head, preferred_element_type=...]
    ppermute x18 -> x8, starting transfers between devices: 62 us -> 8.4 us  [the longest x2 4.79 us: shifted(): return lax.ppermute(array, 'seq', route)]
    all_to_all x0 -> x5, starting transfers between devices: none -> 22.8 us  [swap(): lax.all_to_all(array, 'seq', 0, 0, axis_index_groups=groups, tiled=True)]
    all_to_all x0 -> x5, waiting for transfers between devices: none -> 20 us  [swap(): lax.all_to_all(array, 'seq', 0, 0, axis_index_groups=groups, tiled=True)]
    pallas_call x0 -> x1, Pallas kernels: none -> 15.5 us  [on_device(): pl.pallas_call(attend_kernel, out_shape=(shape((kv_heads, rows, own_width...]
    while x13 -> x0, local copies, waits for them, and re-layouts: 12.1 us -> none
  transfers between devices with their start and end apart: 18 -> 13, of which waited for: 16 -> 8; matrix products, arithmetic and copies ran while one was open for 2% -> 7% of each run, Pallas kernels for 0% -> 0%
where the time goes in v2:
time: 88.2 us; the launch traced here: 87.6 us
  starting transfers between devices  31.2 us (35%)
  waiting for transfers between devices  26 us (29%)
  Pallas kernels  15.5 us (18%)
  local copies, waits for them, and re-layouts  8.09 us (9%)
  other arithmetic  5.93 us (7%)
  between operations  0.93 us (1%)
    all_to_all x5, starting transfers between devices, swap(): lax.all_to_all(array, 'seq', 0, 0, axis_index_groups=groups, tiled=True)  22.8 us
    all_to_all x5, waiting for transfers between devices, swap(): lax.all_to_all(array, 'seq', 0, 0, axis_index_groups=groups, tiled=True)  20 us
    pallas_call x1, Pallas kernels, on_device(): pl.pallas_call(attend_kernel, out_shape=(shape((kv_heads, rows, own_width...  15.5 us
    unnamed x27, local copies, waits for them, and re-layouts  6.78 us
    ppermute x2, starting transfers between devices, shifted(): return lax.ppermute(array, 'seq', route)  4.79 us
    ppermute x2, waiting for transfers between devices, shifted(): return lax.ppermute(array, 'seq', route)  4 us
    ppermute x4, starting transfers between devices, on_chip(): return lax.ppermute(array, 'seq', [(i, i ^ 1) for i in range(count)])  2.3 us
    ppermute x4, waiting for transfers between devices, on_chip(): return lax.ppermute(array, 'seq', [(i, i ^ 1) for i in range(count)])  1.97 us
  transfers between devices with their start and end apart: 13, of which 8 were waited for; matrix products, arithmetic and copies ran while one was open for 7% of the time, Pallas kernels for 0%

profile of v2, /device:TPU:0, one launch (start us, length us, event | category | flops | bytes accessed | tf_op | source)
XLA Modules:
  0.0 87.6 jit_solution(843015977027652555)
XLA Ops:
  0.6 1.1 %copy.27 = bf16[1,128,512]{1,2,0:T(8,128)(2,1)S(1)} copy(bf16[1,128,512]{2,1,0:T(8,128)(2,1)} %param.8) | data formatting | bytes 262144 | tf_op args[1]
  1.9 1.0 %copy.29 = bf16[1,128,512]{1,2,0:T(8,128)(2,1)S(1)} copy(bf16[1,128,512]{2,1,0:T(8,128)(2,1)} %param.9) | data formatting | bytes 262144 | tf_op args[2]
  3.8 5.2 %all-to-all-start.1 = ((bf16[4,128,256]{2,1,0:T(8,128)(2,1)}), bf16[4,128,256]{2,1,0:T(8,128)(2,1)S(1)}, u32[]{:S(2)}, u32[]{:S(2)}) async-start(bf16[4,128,256]{2,1,0:T(8,128)(2,1)} %pad_maximum_fusion.1), calls=%async_computation.1 | async-start | bytes 524288 | tf_op jit(solution)/shard_map/all_to_all | solution.py:151
  10.5 1.2 %pad_maximum_fusion = bf16[4,128,1024]{2,1,0:T(8,128)(2,1)} fusion(bf16[4,128,512]{2,1,0:T(8,128)(2,1)S(1)} %bitcast.28, bf16[4,128,512]{2,1,0:T(8,128)(2,1)S(1)} %bitcast.27), kind=kLoop, calls=%fused_computation | loop fusion | flops 2097152 | bytes 2097152 | tf_op jit(solution)/shard_map/concatenate | solution.py:164
  11.6 2.7 %all-to-all-done.1.kv_same = bf16[4,128,256]{2,1,0:T(8,128)(2,1)S(1)} async-done(((bf16[4,128,256]{2,1,0:T(8,128)(2,1)}), bf16[4,128,256]{2,1,0:T(8,128)(2,1)S(1)}, u32[]{:S(2)}, u32[]{:S(2)}) %all-to-all-start.1) | async-done | bytes 262176 | tf_op jit(solution)/shard_map/all_to_all | solution.py:151
  14.3 3.5 %all-to-all-start = ((bf16[4,128,1024]{2,1,0:T(8,128)(2,1)}), bf16[4,128,1024]{2,1,0:T(8,128)(2,1)S(1)}, u32[]{:S(2)}, u32[]{:S(2)}) async-start(bf16[4,128,1024]{2,1,0:T(8,128)(2,1)} %pad_maximum_fusion), calls=%async_computation | async-start | bytes 2097152 | tf_op jit(solution)/shard_map/all_to_all | solution.py:151
  17.8 3.5 %collective-permute-start.1 = (bf16[4,128,256]{2,1,0:T(8,128)(2,1)S(1)}, bf16[4,128,256]{2,1,0:T(8,128)(2,1)S(1)}, u32[]{:S(2)}, u32[]{:S(2)}) collective-permute-start(bf16[4,128,256]{2,1,0:T(8,128)(2,1)S(1)} %all-to-all-done.1.kv_same), channel_id=1, source_target_pairs={{0,8},{1,9},{2,10},{3,11},{4,12},{5,13},{6,14},{7,15},{8,16},{9,17... | collective-permute-start | bytes 786440 | tf_op jit(solution)/shard_map/ppermute | solution.py:155
  21.5 4.0 %collective-permute-done.1.old_same = bf16[4,128,256]{2,1,0:T(8,128)(2,1)S(1)} collective-permute-done((bf16[4,128,256]{2,1,0:T(8,128)(2,1)S(1)}, bf16[4,128,256]{2,1,0:T(8,128)(2,1)S(1)}, u32[]{:S(2)}, u32[]{:S(2)}) %collective-permute-start.1) | collective-permute-done | bytes 262176 | tf_op jit(solution)/shard_map/ppermute | solution.py:155
  27.0 3.3 %all-to-all-done.query_grad = bf16[4,128,1024]{2,1,0:T(8,128)(2,1)S(1)} async-done(((bf16[4,128,1024]{2,1,0:T(8,128)(2,1)}), bf16[4,128,1024]{2,1,0:T(8,128)(2,1)S(1)}, u32[]{:S(2)}, u32[]{:S(2)}) %all-to-all-start) | async-done | bytes 1048608 | tf_op jit(solution)/shard_map/all_to_all | solution.py:151
  30.3 1.0 %copy-done = bf16[4,128,1024]{2,1,0:T(8,128)(2,1)} copy-done((bf16[4,128,1024]{2,1,0:T(8,128)(2,1)}, bf16[4,128,1024]{2,1,0:T(8,128)(2,1)S(1)}, u32[]{:S(2)}) %copy-start) | copy-done | bytes 1048600
  31.3 15.5 %shard_map.84 = (bf16[4,128,512]{2,1,0:T(8,128)(2,1)}, bf16[8,128,256]{2,1,0:T(8,128)(2,1)}, f32[8,128,256]{2,1,0:T(8,128)}, f32[16,128]{1,0:T(8,128)}, f32[4,128]{1,0:T(4,128)}) custom-call(s32[3]{0:T(128)} %pad_add_fusion.place, bf16[4,128,1024]{2,1,0:T(8,128)(2,1)} %copy-done, bf16[4,128,256]{2,1,0:T(8,128)(2,1)} %copy-done.3, ...), custom_call_target="tpu_custom_call" | custom-call | flops 3019898880 | bytes 5242880 | tf_op jit(solution)/shard_map/pallas_call | solution.py:178
  46.8 2.2 %collective-permute-start.4 = (bf16[8,128,256]{2,1,0:T(8,128)(2,1)}, bf16[8,128,256]{2,1,0:T(8,128)(2,1)S(1)}, u32[]{:S(2)}, u32[]{:S(2)}) collective-permute-start(bf16[8,128,256]{2,1,0:T(8,128)(2,1)} %get-tuple-element.23), channel_id=1, source_target_pairs={{0,1},{1,0},{2,3},{3,2},{4,5},{5,4},{6,7},{7,6},{8,9},{9,8},{10,11... | collective-permute-start | bytes 1572872 | tf_op jit(solution)/shard_map/ppermute | solution.py:158
  49.0 1.7 %collective-permute-done.4 = bf16[8,128,256]{2,1,0:T(8,128)(2,1)S(1)} collective-permute-done((bf16[8,128,256]{2,1,0:T(8,128)(2,1)}, bf16[8,128,256]{2,1,0:T(8,128)(2,1)S(1)}, u32[]{:S(2)}, u32[]{:S(2)}) %collective-permute-start.4) | collective-permute-done | bytes 524320 | tf_op jit(solution)/shard_map/ppermute | solution.py:158
  50.8 1.4 %convert_add_fusion = f32[8,128,256]{2,1,0:T(8,128)S(1)} fusion(f32[8,128,256]{2,1,0:T(8,128)} %get-tuple-element.22, bf16[8,128,256]{2,1,0:T(8,128)(2,1)S(1)} %collective-permute-done.4), kind=kLoop, calls=%fused_computation.1 | loop fusion | flops 524288 | bytes 2621440 | tf_op jit(solution)/shard_map/add | solution.py:202
  52.2 1.3 %collective-permute-start.5 = (bf16[4,128,256]{2,1,0:T(8,128)(2,1)S(1)}, bf16[4,128,256]{2,1,0:T(8,128)(2,1)S(1)}, u32[]{:S(2)}, u32[]{:S(2)}) collective-permute-start(bf16[4,128,256]{2,1,0:T(8,128)(2,1)S(1)} %slice.81), channel_id=1, source_target_pairs={{8,0},{9,1},{10,2},{11,3},{12,4},{13,5},{14,6},{15,7},{16,8},{17,9... | collective-permute-start | bytes 786440 | tf_op jit(solution)/shard_map/ppermute | solution.py:155
  54.1 6.8 %all-to-all-start.4 = ((f32[4,1,128]{2,1,0:T(1,128)}), f32[4,1,128]{2,1,0:T(1,128)S(1)}, u32[]{:S(2)}, u32[]{:S(2)}) async-start(f32[4,1,128]{2,1,0:T(1,128)} %bitcast.19), calls=%async_computation.4 | async-start | bytes 4096 | tf_op jit(solution)/shard_map/all_to_all | solution.py:151
  61.5 4.8 %all-to-all-done.4 = f32[4,1,128]{2,1,0:T(1,128)S(1)} async-done(((f32[4,1,128]{2,1,0:T(1,128)}), f32[4,1,128]{2,1,0:T(1,128)S(1)}, u32[]{:S(2)}, u32[]{:S(2)}) %all-to-all-start.4) | async-done | bytes 2080 | tf_op jit(solution)/shard_map/all_to_all | solution.py:151
  66.3 3.9 %all-to-all-start.2 = ((bf16[4,128,512]{2,1,0:T(8,128)(2,1)}), bf16[4,128,512]{2,1,0:T(8,128)(2,1)S(1)}, u32[]{:S(2)}, u32[]{:S(2)}) async-start(bf16[4,128,512]{2,1,0:T(8,128)(2,1)} %get-tuple-element.21), calls=%async_computation.2 | async-start | bytes 1048576 | tf_op jit(solution)/shard_map/all_to_all | solution.py:151
  71.2 5.8 %all-to-all-done.2 = bf16[4,128,512]{2,1,0:T(8,128)(2,1)S(1)} async-done(((bf16[4,128,512]{2,1,0:T(8,128)(2,1)}), bf16[4,128,512]{2,1,0:T(8,128)(2,1)S(1)}, u32[]{:S(2)}, u32[]{:S(2)}) %all-to-all-start.2) | async-done | bytes 524320 | tf_op jit(solution)/shard_map/all_to_all | solution.py:151
  77.0 3.4 %all-to-all-start.3 = ((bf16[4,128,256]{2,1,0:T(8,128)(2,1)}), bf16[4,128,256]{2,1,0:T(8,128)(2,1)S(1)}, u32[]{:S(2)}, u32[]{:S(2)}) async-start(bf16[4,128,256]{2,1,0:T(8,128)(2,1)} %convert_element_type.13), calls=%async_computation.3 | async-start | bytes 524288 | tf_op jit(solution)/shard_map/all_to_all | solution.py:151
  81.2 1.0 %copy.35 = bf16[1,128,2048]{2,1,0:T(8,128)(2,1)} copy(bf16[1,128,2048]{1,2,0:T(8,128)(2,1)S(1)} %bitcast.24) | data formatting | bytes 1048576
  82.3 3.5 %all-to-all-done.3 = bf16[4,128,256]{2,1,0:T(8,128)(2,1)S(1)} async-done(((bf16[4,128,256]{2,1,0:T(8,128)(2,1)}), bf16[4,128,256]{2,1,0:T(8,128)(2,1)S(1)}, u32[]{:S(2)}, u32[]{:S(2)}) %all-to-all-start.3) | async-done | bytes 262176 | tf_op jit(solution)/shard_map/all_to_all | solution.py:151
  85.9 0.8 copy.37
  86.8 0.8 copy.36
  (51 shorter events, 7.4 us)
Async XLA Ops:
  0.6 8.3 %copy-start.1 = (bf16[1,128,2048]{2,1,0:T(8,128)(2,1)S(1)}, bf16[1,128,2048]{2,1,0:T(8,128)(2,1)}, u32[]{:S(2)}) copy-start(bf16[1,128,2048]{2,1,0:T(8,128)(2,1)} %param.7) | copy-start | bytes 1572868
  3.8 10.5 %all-to-all-start.1 = ((bf16[4,128,256]{2,1,0:T(8,128)(2,1)}), bf16[4,128,256]{2,1,0:T(8,128)(2,1)S(1)}, u32[]{:S(2)}, u32[]{:S(2)}) async-start(bf16[4,128,256]{2,1,0:T(8,128)(2,1)} %pad_maximum_fusion.1), calls=%async_computation.1 | async-start | bytes 524288 | tf_op jit(solution)/shard_map/all_to_all | solution.py:151
  8.9 1.0 %copy-start.2 = (bf16[1,128,2048]{2,1,0:T(8,128)(2,1)S(1)}, bf16[1,128,2048]{2,1,0:T(8,128)(2,1)}, u32[]{:S(2)}) copy-start(bf16[1,128,2048]{2,1,0:T(8,128)(2,1)} %param.11) | copy-start | bytes 1572868
  14.3 11.2 %copy-start.3 = (bf16[4,128,256]{2,1,0:T(8,128)(2,1)}, bf16[4,128,256]{2,1,0:T(8,128)(2,1)S(1)}, u32[]{:S(2)}) copy-start(bf16[4,128,256]{2,1,0:T(8,128)(2,1)S(1)} %all-to-all-done.1.kv_same) | copy-start | bytes 786436
  14.3 16.0 %all-to-all-start = ((bf16[4,128,1024]{2,1,0:T(8,128)(2,1)}), bf16[4,128,1024]{2,1,0:T(8,128)(2,1)S(1)}, u32[]{:S(2)}, u32[]{:S(2)}) async-start(bf16[4,128,1024]{2,1,0:T(8,128)(2,1)} %pad_maximum_fusion), calls=%async_computation | async-start | bytes 2097152 | tf_op jit(solution)/shard_map/all_to_all | solution.py:151
  17.8 7.6 %collective-permute-start.1 = (bf16[4,128,256]{2,1,0:T(8,128)(2,1)S(1)}, bf16[4,128,256]{2,1,0:T(8,128)(2,1)S(1)}, u32[]{:S(2)}, u32[]{:S(2)}) collective-permute-start(bf16[4,128,256]{2,1,0:T(8,128)(2,1)S(1)} %all-to-all-done.1.kv_same), channel_id=1, source_target_pairs={{0,8},{1,9},{2,10},{3,11},{4,12},{5,13},{6,14},{7,15},{8,16},{9,17... | collective-permute-start | bytes 786440 | tf_op jit(solution)/shard_map/ppermute | solution.py:155
  21.4 5.4 %collective-permute-start = (bf16[4,128,256]{2,1,0:T(8,128)(2,1)S(1)}, bf16[4,128,256]{2,1,0:T(8,128)(2,1)S(1)}, u32[]{:S(2)}, u32[]{:S(2)}) collective-permute-start(bf16[4,128,256]{2,1,0:T(8,128)(2,1)S(1)} %all-to-all-done.1.kv_same), channel_id=1, source_target_pairs={{0,1},{1,0},{2,3},{3,2},{4,5},{5,4},{6,7},{7,6},{8,9},{9,8},{10,11... | collective-permute-start | bytes 786440 | tf_op jit(solution)/shard_map/ppermute | solution.py:158
  25.5 4.8 %copy-start.5 = (bf16[4,128,256]{2,1,0:T(8,128)(2,1)}, bf16[4,128,256]{2,1,0:T(8,128)(2,1)S(1)}, u32[]{:S(2)}) copy-start(bf16[4,128,256]{2,1,0:T(8,128)(2,1)S(1)} %collective-permute-done.1.old_same) | copy-start | bytes 786436
  25.5 1.5 %collective-permute-start.2 = (bf16[4,128,256]{2,1,0:T(8,128)(2,1)S(1)}, bf16[4,128,256]{2,1,0:T(8,128)(2,1)S(1)}, u32[]{:S(2)}, u32[]{:S(2)}) collective-permute-start(bf16[4,128,256]{2,1,0:T(8,128)(2,1)S(1)} %collective-permute-done.1.old_same), channel_id=1, source_target_pairs={{0,1},{1,0},{2,3},{3,2},{4,5},{5,4},{6,7},{7,6},{8,9},{9,8},{10,11... | collective-permute-start | bytes 786440 | tf_op jit(solution)/shard_map/ppermute | solution.py:158
  25.5 1.3 %collective-permute-start.3 = (bf16[16,128]{1,0:T(8,128)(2,1)S(1)}, bf16[16,128]{1,0:T(8,128)(2,1)S(1)}, u32[]{:S(2)}, u32[]{:S(2)}) collective-permute-start(bf16[16,128]{1,0:T(8,128)(2,1)S(1)} %slice_bitcast_fusion), channel_id=1, source_target_pairs={{1,16},{3,18},{5,20},{7,22},{9,24},{11,26},{13,28},{15,30}} | collective-permute-start | bytes 12296 | tf_op jit(solution)/shard_map/ppermute | solution.py:168
  26.8 3.5 %copy-start.9 = (bf16[16,128]{1,0:T(8,128)(2,1)}, bf16[16,128]{1,0:T(8,128)(2,1)S(1)}, u32[]{:S(2)}) copy-start(bf16[16,128]{1,0:T(8,128)(2,1)S(1)} %collective-permute-done.3.halo) | copy-start | bytes 12292
  26.8 3.5 %copy-start.6 = (bf16[4,128,256]{2,1,0:T(8,128)(2,1)}, bf16[4,128,256]{2,1,0:T(8,128)(2,1)S(1)}, u32[]{:S(2)}) copy-start(bf16[4,128,256]{2,1,0:T(8,128)(2,1)S(1)} %collective-permute-done.kv_other) | copy-start | bytes 786436
  27.0 3.3 %copy-start.7 = (bf16[4,128,256]{2,1,0:T(8,128)(2,1)}, bf16[4,128,256]{2,1,0:T(8,128)(2,1)S(1)}, u32[]{:S(2)}) copy-start(bf16[4,128,256]{2,1,0:T(8,128)(2,1)S(1)} %collective-permute-done.2.old_other) | copy-start | bytes 786436
  30.3 1.0 %copy-start = (bf16[4,128,1024]{2,1,0:T(8,128)(2,1)}, bf16[4,128,1024]{2,1,0:T(8,128)(2,1)S(1)}, u32[]{:S(2)}) copy-start(bf16[4,128,1024]{2,1,0:T(8,128)(2,1)S(1)} %all-to-all-done.query_grad) | copy-start | bytes 3145732
  46.8 4.0 %collective-permute-start.4 = (bf16[8,128,256]{2,1,0:T(8,128)(2,1)}, bf16[8,128,256]{2,1,0:T(8,128)(2,1)S(1)}, u32[]{:S(2)}, u32[]{:S(2)}) collective-permute-start(bf16[8,128,256]{2,1,0:T(8,128)(2,1)} %get-tuple-element.23), channel_id=1, source_target_pairs={{0,1},{1,0},{2,3},{3,2},{4,5},{5,4},{6,7},{7,6},{8,9},{9,8},{10,11... | collective-permute-start | bytes 1572872 | tf_op jit(solution)/shard_map/ppermute | solution.py:158
  50.8 2.7 %copy-start.4 = (f32[4,128]{1,0:T(4,128)S(1)}, f32[4,128]{1,0:T(4,128)}, u32[]{:S(2)}) copy-start(f32[4,128]{1,0:T(4,128)} %get-tuple-element.25) | copy-start | bytes 6148
  50.8 10.1 %copy-start.8 = (f32[16,128]{1,0:T(8,128)S(1)}, f32[16,128]{1,0:T(8,128)}, u32[]{:S(2)}) copy-start(f32[16,128]{1,0:T(8,128)} %get-tuple-element.24) | copy-start | bytes 24580
  52.2 18.1 %collective-permute-start.5 = (bf16[4,128,256]{2,1,0:T(8,128)(2,1)S(1)}, bf16[4,128,256]{2,1,0:T(8,128)(2,1)S(1)}, u32[]{:S(2)}, u32[]{:S(2)}) collective-permute-start(bf16[4,128,256]{2,1,0:T(8,128)(2,1)S(1)} %slice.81), channel_id=1, source_target_pairs={{8,0},{9,1},{10,2},{11,3},{12,4},{13,5},{14,6},{15,7},{16,8},{17,9... | collective-permute-start | bytes 786440 | tf_op jit(solution)/shard_map/ppermute | solution.py:155
  54.1 12.3 %all-to-all-start.4 = ((f32[4,1,128]{2,1,0:T(1,128)}), f32[4,1,128]{2,1,0:T(1,128)S(1)}, u32[]{:S(2)}, u32[]{:S(2)}) async-start(f32[4,1,128]{2,1,0:T(1,128)} %bitcast.19), calls=%async_computation.4 | async-start | bytes 4096 | tf_op jit(solution)/shard_map/all_to_all | solution.py:151
  60.9 9.5 %collective-permute-start.6 = (f32[16,128]{1,0:T(8,128)S(1)}, f32[16,128]{1,0:T(8,128)S(1)}, u32[]{:S(2)}, u32[]{:S(2)}) collective-permute-start(f32[16,128]{1,0:T(8,128)S(1)} %copy-done.8), channel_id=1, source_target_pairs={{16,1},{18,3},{20,5},{22,7},{24,9},{26,11},{28,13},{30,15}} | collective-permute-start | bytes 24584 | tf_op jit(solution)/shard_map/ppermute | solution.py:205
  66.3 10.6 %all-to-all-start.2 = ((bf16[4,128,512]{2,1,0:T(8,128)(2,1)}), bf16[4,128,512]{2,1,0:T(8,128)(2,1)S(1)}, u32[]{:S(2)}, u32[]{:S(2)}) async-start(bf16[4,128,512]{2,1,0:T(8,128)(2,1)} %get-tuple-element.21), calls=%async_computation.2 | async-start | bytes 1048576 | tf_op jit(solution)/shard_map/all_to_all | solution.py:151
  70.3 10.0 %collective-permute-start.7 = (f32[64]{0:T(128)S(1)}, f32[64]{0:T(128)S(1)}, u32[]{:S(2)}, u32[]{:S(2)}) collective-permute-start(f32[64]{0:T(128)S(1)} %broadcast_select_fusion), channel_id=1, source_target_pairs={{0,1},{1,0},{2,3},{3,2},{4,5},{5,4},{6,7},{7,6},{8,9},{9,8},{10,11... | collective-permute-start | bytes 776 | tf_op jit(solution)/shard_map/ppermute | solution.py:158
  77.0 8.8 %all-to-all-start.3 = ((bf16[4,128,256]{2,1,0:T(8,128)(2,1)}), bf16[4,128,256]{2,1,0:T(8,128)(2,1)S(1)}, u32[]{:S(2)}, u32[]{:S(2)}) async-start(bf16[4,128,256]{2,1,0:T(8,128)(2,1)} %convert_element_type.13), calls=%async_computation.3 | async-start | bytes 524288 | tf_op jit(solution)/shard_map/all_to_all | solution.py:151

commit v3 on v2

v3 whole, which is shorter than its diff:
```python
import math

import jax
import jax.numpy as jnp
from jax import lax
from jax.experimental import pallas as pl
from jax.experimental.pallas import tpu as pltpu
from jax.sharding import PartitionSpec as P

HEAD_SIZE = 128
WINDOW = 1024
NEG_FILL = -1e30
HALO = 16
VMEM_BYTES = 56 * 1024 * 1024
NT = (((1,), (1,)), ((), ()))


def run(kernel, out_shape, operands, scratch=(), flops=0):
    vmem = pl.BlockSpec(memory_space=pltpu.VMEM)
    moved = list(operands) + list(out_shape)
    return pl.pallas_call(
        kernel,
        out_shape=out_shape,
        in_specs=[pl.BlockSpec(memory_space=pltpu.SMEM)] + [vmem] * (len(operands) - 1),
        out_specs=[vmem] * len(out_shape),
        scratch_shapes=list(scratch),
        cost_estimate=pl.CostEstimate(
            flops=flops, bytes_accessed=sum(math.prod(a.shape) * a.dtype.itemsize for a in moved), transcendentals=0
        ),
        compiler_params=pltpu.CompilerParams(vmem_limit_bytes=VMEM_BYTES),
    )(*operands)


def columns_of(index):
    return pl.ds(pl.multiple_of(index * HEAD_SIZE, HEAD_SIZE), HEAD_SIZE)


def pack_kernel(place, queries, grad_out, keys, values, packed, *parts):
    head_at = place[2]
    heads, _, width = packed.shape
    for head in range(heads):
        own = slice(head * (width // 2), (head + 1) * (width // 2))
        packed[head, :, : width // 2] = queries[:, own]
        packed[head, :, width // 2 :] = grad_out[:, own]
    for turn, part in enumerate(parts):
        at = columns_of(head_at ^ turn)
        part[:, :HEAD_SIZE] = keys[:, at]
        part[:, HEAD_SIZE:] = values[:, at]


def unpack_kernel(place, *refs):
    parts, (grad_keys, grad_values) = refs[:-2], refs[-2:]
    head_at = place[2]
    for turn, part in enumerate(parts):
        at = columns_of(head_at ^ turn)
        grad_keys[:, at] = part[:, :HEAD_SIZE]
        grad_values[:, at] = part[:, HEAD_SIZE:]


def prepare_kernel(
    place, kv_same, kv_other, old_same, old_other, halo, all_taps, key_all, key_t, mix_all, value_all
):
    blocks, rows = kv_same.shape[:2]
    span = 2 * blocks
    tap_count = all_taps.shape[0]
    parity, head_at = place[1], place[2]
    taps = all_taps[:, columns_of(head_at)]
    value_all[:HALO] = halo[...].astype(jnp.float32)
    for start, same, other in ((0, old_same, old_other), (span, kv_same, kv_other)):
        for turn in range(blocks):
            for source, core in ((same, parity), (other, 1 - parity)):
                first = (start + 2 * (head_at ^ turn) + core) * rows
                first = pl.multiple_of(first, rows)
                key_all[pl.ds(first, rows)] = source[turn, :, :HEAD_SIZE]
                value_all[pl.ds(first + HALO, rows)] = source[turn, :, HEAD_SIZE:].astype(jnp.float32)
    for start in range(HALO, HALO + 2 * span * rows, rows):
        mixed = taps[0:1] * value_all[start : start + rows]
        for index_k in range(1, tap_count):
            mixed = mixed + taps[index_k : index_k + 1] * value_all[start - index_k : start - index_k + rows]
        mix_all[start - HALO : start - HALO + rows] = mixed.astype(jnp.bfloat16)
    key_t[...] = jnp.transpose(key_all[...])


def attend_kernel(
    place, query_grad, key_all, key_t, mix_all, all_taps,
    grad_q, send_old, send_own, keep_old, keep_own, grad_halo, dmix,
    dkey, *work,
):
    blocks, rows = query_grad.shape[:2]
    width = grad_q.shape[2]
    span = 2 * blocks
    length = span * rows
    lanes = 2 * HEAD_SIZE
    pairs = width // lanes
    tap_count = all_taps.shape[0]
    has_before, parity, head_at = place[0], place[1], place[2]
    taps = all_taps[:, columns_of(head_at)]
    inv_root = 1.0 / math.sqrt(HEAD_SIZE)
    log2_scale = inv_root * math.log2(math.e)
    score_refs, gprob_refs, low_refs, dscore_refs = work[0:2], work[2:4], work[4:6], work[6:8]
    dkey[...] = jnp.zeros_like(dkey)
    dmix[...] = jnp.zeros_like(dmix)
    fill = jnp.where(has_before == 0, NEG_FILL, 0.0).astype(jnp.float32)
    key_at = lax.broadcasted_iota(jnp.int32, (rows, lanes), 0)
    query_at = lax.broadcasted_iota(jnp.int32, (rows, lanes), 1) & (rows - 1)
    causal = key_at <= query_at
    stats = {}

    def places(n):
        step, pair = n // pairs, n % pairs
        number = 2 * step + parity
        return step, pair, number, pl.multiple_of(number * rows, rows)

    def stacked(step, base):
        return jnp.concatenate(
            [query_grad[step, :, base + h * HEAD_SIZE : base + (h + 1) * HEAD_SIZE] for h in range(2)], axis=0
        )

    def by_eight(array):
        return array.reshape(-1, 8, array.shape[1])

    def scores_stage(n):
        step, pair, number, first = places(n)
        seen = pl.ds(first, length + rows)
        scores = lax.dot_general(
            key_all[seen], stacked(step, pair * lanes), NT, preferred_element_type=jnp.float32
        )
        grads = lax.dot_general(
            mix_all[seen], stacked(step, width + pair * lanes), NT, preferred_element_type=jnp.float32
        )
        edge = jnp.where(causal, scores[length:], scores[:rows] + fill)
        score_refs[n % 2][:rows] = edge
        score_refs[n % 2][rows:] = scores[rows:length]
        gprob_refs[n % 2][:rows] = jnp.where(causal, grads[length:], grads[:rows])
        gprob_refs[n % 2][rows:] = grads[rows:length]
        peak = jnp.max(by_eight(edge), axis=0)
        for c in range(1, span):
            part = jnp.max(by_eight(scores[c * rows : (c + 1) * rows]), axis=0)
            peak = jnp.maximum(peak, part + jnp.where(number + c < span, fill, 0.0))
        stats[n] = jnp.max(peak, axis=0, keepdims=True) * log2_scale

    def softmax_stage(n):
        step, pair, number, first = places(n)
        peak = stats[n]
        scores, gprob, low, dscore = (refs[n % 2] for refs in (score_refs, gprob_refs, low_refs, dscore_refs))
        total = jnp.zeros((8, lanes), jnp.float32)
        delta = jnp.zeros((8, lanes), jnp.float32)
        for c in range(span):
            at = slice(c * rows, (c + 1) * rows)
            shift = -peak if c == 0 else jnp.where(number + c < span, fill, 0.0) - peak
            prob = jnp.exp2(scores[at] * log2_scale + shift)
            total = total + jnp.sum(by_eight(prob), axis=0)
            delta = delta + jnp.sum(by_eight(prob * gprob[at]), axis=0)
            low[at] = prob.astype(jnp.bfloat16)
        inverse = 1.0 / jnp.sum(total, axis=0, keepdims=True)
        delta = jnp.sum(delta, axis=0, keepdims=True) * inverse
        for c in range(span):
            at = slice(c * rows, (c + 1) * rows)
            dscore[at] = low[at] * (gprob[at] - delta).astype(jnp.bfloat16)
        zero = jnp.zeros((), jnp.bfloat16)
        for ref in (low, dscore):
            edge = ref[:rows]
            ref[length:] = jnp.where(causal, edge, zero)
            ref[:rows] = jnp.where(causal, zero, edge)
        stats[n] = inverse

    def gradient_stage(n):
        step, pair, number, first = places(n)
        seen = pl.ds(first, length + rows)
        inverse = stats[n]
        column = jnp.transpose(jnp.broadcast_to(inverse, (HEAD_SIZE, lanes)))
        query = (stacked(step, pair * lanes).astype(jnp.float32) * column).astype(jnp.bfloat16)
        grad = (stacked(step, width + pair * lanes).astype(jnp.float32) * column).astype(jnp.bfloat16)
        low, dscore = low_refs[n % 2], dscore_refs[n % 2]
        dmix[pl.ds(first + HALO, length + rows)] += jnp.dot(low[...], grad, preferred_element_type=jnp.float32)
        dkey[seen] += jnp.dot(dscore[...], query, preferred_element_type=jnp.float32)
        dquery = jnp.dot(key_t[:, seen], dscore[...], preferred_element_type=jnp.float32)
        dquery = jnp.transpose(dquery * (inverse * inv_root)).astype(jnp.bfloat16)
        for h in range(2):
            base = pair * lanes + h * HEAD_SIZE
            grad_q[step, :, base : base + HEAD_SIZE] = dquery[h * rows : (h + 1) * rows]

    count = blocks * pairs
    for n in range(count + 2):
        if n < count:
            scores_stage(n)
        if 1 <= n <= count:
            softmax_stage(n - 1)
        if n >= 2:
            gradient_stage(n - 2)

    def convolved(start, size):
        total = taps[0:1] * dmix[pl.ds(start, size)]
        for index_k in range(1, tap_count):
            total = total + taps[index_k : index_k + 1] * dmix[pl.ds(start + index_k, size)]
        return total

    grad_halo[...] = convolved(0, HALO)
    for start, keep, send in ((0, keep_old, send_old), (span, keep_own, send_own)):
        for turn in range(blocks):
            for target, core in ((keep, parity), (send, 1 - parity)):
                first = pl.multiple_of((start + 2 * (head_at ^ turn) + core) * rows, rows)
                target[turn, :, :HEAD_SIZE] = (dkey[pl.ds(first, rows)] * inv_root).astype(target.dtype)
                target[turn, :, HEAD_SIZE:] = convolved(first + HALO, rows).astype(target.dtype)


def taps_kernel(scale, place, dmix, value_all, tap_grads):
    tap_count = tap_grads.shape[0]
    rows = 128
    sums = [jnp.zeros((8, HEAD_SIZE), jnp.float32)] * tap_count
    for start in range(HALO, value_all.shape[0], rows):
        grad = dmix[start : start + rows]
        for index_k in range(tap_count):
            product = grad * value_all[start - index_k : start - index_k + rows]
            sums[index_k] = sums[index_k] + jnp.sum(product.reshape(-1, 8, HEAD_SIZE), axis=0)
    for index_k in range(tap_count):
        tap_grads[index_k : index_k + 1] = jnp.sum(sums[index_k], axis=0, keepdims=True) * scale


def on_device(queries, keys, values, conv_taps, grad_out):
    rows, width = queries.shape[1:]
    kv_width = keys.shape[2]
    tap_count = conv_taps.shape[0]
    kv_heads = kv_width // HEAD_SIZE
    group = WINDOW // rows
    share = group // kv_heads
    count = lax.axis_size("seq")
    planes = count // group
    own_width = width // kv_heads
    bf16, f32 = jnp.bfloat16, jnp.float32
    shape = jax.ShapeDtypeStruct
    device = lax.axis_index("seq")
    parity = device % share
    head_at = (device % group) // share
    plane = device // group
    same_core = [[g * group + j * share + c for j in range(kv_heads)] for g in range(planes) for c in range(share)]
    place = jnp.stack([(device >= group).astype(jnp.int32), parity, head_at, plane])

    def swap(array, groups):
        return lax.all_to_all(array, "seq", 0, 0, axis_index_groups=groups, tiled=True)

    def routed(array, distance, chosen=lambda i: True):
        route = [(i, i + distance) for i in range(count) if 0 <= i + distance < count and chosen(i)]
        return lax.ppermute(array, "seq", route)

    def flipped(array, bits):
        return lax.ppermute(array, "seq", [(i, i ^ bits) for i in range(count)])

    kv_shape = shape((rows, 2 * HEAD_SIZE), bf16)
    kv_blocks = (kv_heads, rows, 2 * HEAD_SIZE)
    packed, *parts = run(
        pack_kernel,
        [shape((kv_heads, rows, 2 * own_width), bf16)] + [kv_shape] * kv_heads,
        (place, queries[0], grad_out[0], keys[0], values[0]),
    )
    query_grad = swap(packed, same_core)
    kv_same = jnp.stack([parts[0]] + [flipped(parts[turn], turn * share) for turn in range(1, kv_heads)])
    old_same = routed(kv_same, group)
    kv_other = flipped(kv_same, 1)
    old_other = flipped(old_same, 1)
    last = lax.dynamic_index_in_dim(kv_same, head_at ^ (kv_heads - 1), 0, keepdims=False)
    reach = 2 * group - (share - 1)
    halo = routed(last[rows - HALO :, HEAD_SIZE:], reach, lambda i: i % share == share - 1)
    key_all, key_t, mix_all, value_all = run(
        prepare_kernel,
        [
            shape((2 * WINDOW, HEAD_SIZE), bf16),
            shape((HEAD_SIZE, 2 * WINDOW), bf16),
            shape((2 * WINDOW, HEAD_SIZE), bf16),
            shape((HALO + 2 * WINDOW, HEAD_SIZE), f32),
        ],
        (place, kv_same, kv_other, old_same, old_other, halo, conv_taps),
    )
    lanes = 2 * HEAD_SIZE
    grad_q, send_old, send_own, keep_old, keep_own, grad_halo, dmix = run(
        attend_kernel,
        [
            shape((kv_heads, rows, own_width), bf16),
            shape(kv_blocks, bf16),
            shape(kv_blocks, bf16),
            shape(kv_blocks, f32),
            shape(kv_blocks, f32),
            shape((HALO, HEAD_SIZE), f32),
            shape((HALO + 2 * WINDOW + HALO, HEAD_SIZE), f32),
        ],
        (place, query_grad, key_all, key_t, mix_all, conv_taps),
        scratch=[pltpu.VMEM((2 * WINDOW, HEAD_SIZE), f32)]
        + [pltpu.VMEM((WINDOW, lanes), f32)] * 4
        + [pltpu.VMEM((WINDOW + rows, lanes), bf16)] * 4,
        flops=10 * kv_heads * rows * (WINDOW + rows) * own_width,
    )
    returned = routed((keep_old + flipped(send_old, 1).astype(f32)).astype(bf16), -group)
    returned_halo = routed(grad_halo, -reach, lambda i: i % share == 0)
    grad_queries = swap(grad_q, same_core).transpose(1, 0, 2).reshape(rows, width)
    total = keep_own + flipped(send_own, 1).astype(f32) + returned.astype(f32)
    halo_block = jnp.pad(returned_halo, ((rows - HALO, 0), (HEAD_SIZE, 0)))
    owned = []
    for turn in range(kv_heads):
        mine = total[turn] + jnp.where((head_at ^ turn) == kv_heads - 1, halo_block, 0.0)
        owned.append(mine.astype(bf16))
    owned = [owned[0]] + [flipped(owned[turn], turn * share) for turn in range(1, kv_heads)]
    grad_keys, grad_values = run(
        unpack_kernel, [shape((rows, kv_width), bf16), shape((rows, kv_width), bf16)], (place, *owned)
    )
    scale = 1.0 / math.sqrt(rows * count * lax.axis_size("rep"))
    (tap_grads,) = run(
        lambda *refs: taps_kernel(scale, *refs), [shape((tap_count, HEAD_SIZE), f32)], (place, dmix, value_all)
    )
    if planes == tap_count == 4 and share == 2:
        for bits, bit in ((2 * group, plane // 2), (group, plane % 2)):
            half = tap_grads.shape[0] // 2
            low, high = tap_grads[:half], tap_grads[half:]
            tap_grads = jnp.where(bit == 0, low, high) + flipped(jnp.where(bit == 0, high, low), bits)
        low, high = jnp.split(tap_grads[0], 2)
        grad_taps = jnp.where(parity == 0, low, high) + flipped(jnp.where(parity == 0, high, low), 1)
    else:
        spread = jnp.zeros((tap_count, kv_width), f32)
        spread = lax.dynamic_update_slice(spread, tap_grads, (0, head_at * HEAD_SIZE))
        grad_taps = jnp.sum(swap(spread.reshape(count, -1), None), axis=0)
    grad_taps = lax.psum(grad_taps, "rep")
    return grad_queries[None], grad_keys[None], grad_values[None], grad_taps


def solution(mesh):
    in_specs = (
        P("rep", "seq", None),
        P("rep", "seq", None),
        P("rep", "seq", None),
        P(),
        P("rep", "seq", None),
    )
    out_specs = (P("rep", "seq", None), P("rep", "seq", None), P("rep", "seq", None), P("seq"))
    return jax.shard_map(
        on_device, mesh=mesh, in_specs=in_specs, out_specs=out_specs, check_vma=False
    )
```

time: 88.2 us -> 91.8 us (1.041)
  Pallas kernels: 15.5 us -> 20.9 us
  local copies, waits for them, and re-layouts: 8.09 us -> 3.65 us
  waiting for transfers between devices: 26 us -> 30.1 us
  other arithmetic: 5.93 us -> 3 us
  starting transfers between devices: 31.2 us -> 32.7 us
    ppermute x8 -> x17, waiting for transfers between devices: 5.97 us -> 30.1 us  [the longest x13 17.4 us: flipped(): return lax.ppermute(array, 'seq', [(i, i ^ bits) for i in range(count)])]
    all_to_all x5 -> x2, waiting for transfers between devices: 20 us -> 0.01 us  [swap(): lax.all_to_all(array, 'seq', 0, 0, axis_index_groups=groups, tiled=True)]
    ppermute x8 -> x17, starting transfers between devices: 8.4 us -> 23.9 us  [the longest x13 17.8 us: flipped(): return lax.ppermute(array, 'seq', [(i, i ^ bits) for i in range(count)])]
    all_to_all x5 -> x2, starting transfers between devices: 22.8 us -> 8.79 us  [swap(): lax.all_to_all(array, 'seq', 0, 0, axis_index_groups=groups, tiled=True)]
    pallas_call x1 -> x5, Pallas kernels: 15.5 us -> 20.9 us  [run(): pl.pallas_call(kernel, out_shape=out_shape, in_specs=[pl.BlockSpec(memory...]
    unnamed x27 -> x39, local copies, waits for them, and re-layouts: 6.78 us -> 3.37 us
    concatenate x2 -> x0, other arithmetic: 1.9 us -> none  [the longest x1 1.16 us: on_device(): jnp.concatenate([by_head(queries[0]), by_head(grad_out[0])], axis=2)]
    add x3 -> x4, other arithmetic: 2 us -> 0.67 us  [the longest x1 0.58 us: on_device(): jnp.where(parity == 0, low, high)]
  transfers between devices with their start and end apart: 13 -> 19, of which waited for: 8 -> 8; matrix products, arithmetic and copies ran while one was open for 7% -> 3% of each run, Pallas kernels for 0% -> 3%
where the time goes in v3:
time: 91.8 us; the launch traced here: 91.3 us
  starting transfers between devices  32.7 us (36%)
  waiting for transfers between devices  30.1 us (33%)
  Pallas kernels  20.9 us (23%)
  local copies, waits for them, and re-layouts  3.65 us (4%)
  other arithmetic  3 us (3%)
  between operations  0.97 us (1%)
    pallas_call x5, Pallas kernels, run(): pl.pallas_call(kernel, out_shape=out_shape, in_specs=[pl.BlockSpec(memory...  20.9 us
    ppermute x13, starting transfers between devices, flipped(): return lax.ppermute(array, 'seq', [(i, i ^ bits) for i in range(count)])  17.8 us
    ppermute x13, waiting for transfers between devices, flipped(): return lax.ppermute(array, 'seq', [(i, i ^ bits) for i in range(count)])  17.4 us
    ppermute x4, waiting for transfers between devices, routed(): return lax.ppermute(array, 'seq', route)  12.7 us
    all_to_all x2, starting transfers between devices, swap(): lax.all_to_all(array, 'seq', 0, 0, axis_index_groups=groups, tiled=True)  8.79 us
    ppermute x4, starting transfers between devices, routed(): return lax.ppermute(array, 'seq', route)  6.16 us
    unnamed x39, local copies, waits for them, and re-layouts  3.37 us
  transfers between devices with their start and end apart: 19, of which 8 were waited for; matrix products, arithmetic and copies ran while one was open for 3% of the time, Pallas kernels for 3%

profile of v3, /device:TPU:0, one launch (start us, length us, event | category | flops | bytes accessed | tf_op | source)
XLA Modules:
  0.0 91.3 jit_solution(9459150478022179504)
XLA Ops:
  1.3 2.4 %shard_map.84 = (bf16[4,128,1024]{2,1,0:T(8,128)(2,1)}, bf16[128,256]{1,0:T(8,128)(2,1)}, bf16[128,256]{1,0:T(8,128)(2,1)}, bf16[128,256]{1,0:T(8,128)(2,1)}, bf16[128,256]{1,0:T(8,128)(2,1)}) custom-call(s32[4]{0:T(128)} %pad_add_fusion.place.refs_0_, bf16[128,2048]{1,0:T(8,128)(2,1)} %bitcast.42, bf16[128,2048]{1,0:T(8,128)(2,1)} %bitcast.43, ...), custom_call_target="tpu_custom_call" | custom-call | bytes 2621456 | tf_op jit(solution)/shard_map/pallas_call | solution.py:21
  3.8 5.3 %all-to-all-start = ((bf16[4,128,1024]{2,1,0:T(8,128)(2,1)}), bf16[4,128,1024]{2,1,0:T(8,128)(2,1)S(1)}, u32[]{:S(2)}, u32[]{:S(2)}) async-start(bf16[4,128,1024]{2,1,0:T(8,128)(2,1)} %get-tuple-element.22), calls=%async_computation | async-start | bytes 2097152 | tf_op jit(solution)/shard_map/all_to_all | solution.py:240
  9.1 2.0 %collective-permute-start.1 = (bf16[128,256]{1,0:T(8,128)(2,1)S(1)}, bf16[128,256]{1,0:T(8,128)(2,1)S(1)}, u32[]{:S(2)}, u32[]{:S(2)}) collective-permute-start(bf16[128,256]{1,0:T(8,128)(2,1)S(1)} %copy-done.17), channel_id=1, source_target_pairs={{0,4},{1,5},{2,6},{3,7},{4,0},{5,1},{6,2},{7,3},{8,12},{9,13},{10,... | collective-permute-start | bytes 196616 | tf_op jit(solution)/shard_map/ppermute | solution.py:247
  11.1 1.5 %collective-permute-start.2 = (bf16[128,256]{1,0:T(8,128)(2,1)S(1)}, bf16[128,256]{1,0:T(8,128)(2,1)S(1)}, u32[]{:S(2)}, u32[]{:S(2)}) collective-permute-start(bf16[128,256]{1,0:T(8,128)(2,1)S(1)} %copy-done.16), channel_id=1, source_target_pairs={{0,6},{1,7},{2,4},{3,5},{4,2},{5,3},{6,0},{7,1},{8,14},{9,15},{10,... | collective-permute-start | bytes 196616 | tf_op jit(solution)/shard_map/ppermute | solution.py:247
  12.6 12.1 %collective-permute-done.1 = bf16[128,256]{1,0:T(8,128)(2,1)S(1)} collective-permute-done((bf16[128,256]{1,0:T(8,128)(2,1)S(1)}, bf16[128,256]{1,0:T(8,128)(2,1)S(1)}, u32[]{:S(2)}, u32[]{:S(2)}) %collective-permute-start.1) | collective-permute-done | bytes 65568 | tf_op jit(solution)/shard_map/ppermute | solution.py:247
  24.8 0.9 %collective-permute-done.2 = bf16[128,256]{1,0:T(8,128)(2,1)S(1)} collective-permute-done((bf16[128,256]{1,0:T(8,128)(2,1)S(1)}, bf16[128,256]{1,0:T(8,128)(2,1)S(1)}, u32[]{:S(2)}, u32[]{:S(2)}) %collective-permute-start.2) | collective-permute-done | bytes 65568 | tf_op jit(solution)/shard_map/ppermute | solution.py:247
  25.8 3.6 %collective-permute-start.4 = (bf16[4,128,256]{2,1,0:T(8,128)(2,1)S(1)}, bf16[4,128,256]{2,1,0:T(8,128)(2,1)S(1)}, u32[]{:S(2)}, u32[]{:S(2)}) collective-permute-start(bf16[4,128,256]{2,1,0:T(8,128)(2,1)S(1)} %pad_maximum_fusion.kv_same), channel_id=1, source_target_pairs={{0,8},{1,9},{2,10},{3,11},{4,12},{5,13},{6,14},{7,15},{8,16},{9,17... | collective-permute-start | bytes 786440 | tf_op jit(solution)/shard_map/ppermute | solution.py:244
  29.4 4.2 %collective-permute-done.4.old_same = bf16[4,128,256]{2,1,0:T(8,128)(2,1)S(1)} collective-permute-done((bf16[4,128,256]{2,1,0:T(8,128)(2,1)S(1)}, bf16[4,128,256]{2,1,0:T(8,128)(2,1)S(1)}, u32[]{:S(2)}, u32[]{:S(2)}) %collective-permute-start.4) | collective-permute-done | bytes 262176 | tf_op jit(solution)/shard_map/ppermute | solution.py:244
  35.8 2.9 %shard_map.85 = (bf16[2048,128]{1,0:T(8,128)(2,1)}, bf16[128,2048]{1,0:T(8,128)(2,1)}, bf16[2048,128]{1,0:T(8,128)(2,1)}, f32[2064,128]{1,0:T(8,128)}) custom-call(s32[4]{0:T(128)} %pad_add_fusion.place.refs_0_, bf16[4,128,256]{2,1,0:T(8,128)(2,1)} %copy-done, bf16[4,128,256]{2,1,0:T(8,128)(2,1)} %copy-done.5, bf16[4,128,256]{2,1,0:T(8,128)(2,1)} %copy-done.4, ...), custom_call_target="tpu_custom_call" | custom-call | bytes 3690512 | tf_op jit(solution)/shard_map/pallas_call | solution.py:21
  38.7 1.0 %copy-done.1 = bf16[4,128,1024]{2,1,0:T(8,128)(2,1)} copy-done((bf16[4,128,1024]{2,1,0:T(8,128)(2,1)}, bf16[4,128,1024]{2,1,0:T(8,128)(2,1)S(1)}, u32[]{:S(2)}) %copy-start.1) | copy-done | bytes 1048600
  39.7 11.4 %shard_map.86 = (bf16[4,128,512]{2,1,0:T(8,128)(2,1)}, bf16[4,128,256]{2,1,0:T(8,128)(2,1)}, bf16[4,128,256]{2,1,0:T(8,128)(2,1)}, f32[4,128,256]{2,1,0:T(8,128)...) custom-call(s32[4]{0:T(128)} %pad_add_fusion.place.refs_0_, bf16[4,128,1024]{2,1,0:T(8,128)(2,1)} %copy-done.1, ...), custom_call_target="tpu_custom_call" | custom-call | flops 3019898880 | bytes 5799952 | tf_op jit(solution)/shard_map/pallas_call | solution.py:21
  51.0 2.6 %shard_map.88 = f32[4,128]{1,0:T(4,128)} custom-call(s32[4]{0:T(128)} %pad_add_fusion.place.refs_0_, f32[2080,128]{1,0:T(8,128)} %get-tuple-element.38.refs_1_, f32[2064,128]{1,0:T(8,128)} %get-tuple-element.39.refs_2_), custom_call_target="tpu_custom_call" | custom-call | bytes 2123792 | tf_op jit(solution)/shard_map/pallas_call | solution.py:21
  53.6 0.8 broadcast_select_fusion
  54.4 8.5 %collective-permute-start.14 = (f32[2,128]{1,0:T(2,128)S(1)}, f32[2,128]{1,0:T(2,128)S(1)}, u32[]{:S(2)}, u32[]{:S(2)}) collective-permute-start(f32[2,128]{1,0:T(2,128)S(1)} %broadcast_select_fusion), channel_id=1, source_target_pairs={{0,16},{1,17},{2,18},{3,19},{4,20},{5,21},{6,22},{7,23},{8,24},{9,... | collective-permute-start | bytes 3080 | tf_op jit(solution)/shard_map/ppermute | solution.py:247
  64.1 3.5 %all-to-all-start.1 = ((bf16[4,128,512]{2,1,0:T(8,128)(2,1)}), bf16[4,128,512]{2,1,0:T(8,128)(2,1)S(1)}, u32[]{:S(2)}, u32[]{:S(2)}) async-start(bf16[4,128,512]{2,1,0:T(8,128)(2,1)} %get-tuple-element.30), calls=%async_computation.1 | async-start | bytes 1048576 | tf_op jit(solution)/shard_map/all_to_all | solution.py:240
  67.7 1.6 %collective-permute-start.15 = (f32[1,128]{1,0:T(1,128)S(1)}, f32[1,128]{1,0:T(1,128)S(1)}, u32[]{:S(2)}, u32[]{:S(2)}) collective-permute-start(f32[1,128]{1,0:T(1,128)S(1)} %broadcast_select_fusion.1), channel_id=1, source_target_pairs={{0,8},{1,9},{2,10},{3,11},{4,12},{5,13},{6,14},{7,15},{8,0},{9,1},... | collective-permute-start | bytes 1544 | tf_op jit(solution)/shard_map/ppermute | solution.py:247
  69.4 1.3 %collective-permute-start.9 = (bf16[4,128,256]{2,1,0:T(8,128)(2,1)S(1)}, bf16[4,128,256]{2,1,0:T(8,128)(2,1)S(1)}, u32[]{:S(2)}, u32[]{:S(2)}) collective-permute-start(bf16[4,128,256]{2,1,0:T(8,128)(2,1)S(1)} %add_convert_fusion), channel_id=1, source_target_pairs={{8,0},{9,1},{10,2},{11,3},{12,4},{13,5},{14,6},{15,7},{16,8},{17,9... | collective-permute-start | bytes 786440 | tf_op jit(solution)/shard_map/ppermute | solution.py:244
  71.4 8.5 %collective-permute-done.9 = bf16[4,128,256]{2,1,0:T(8,128)(2,1)S(1)} collective-permute-done((bf16[4,128,256]{2,1,0:T(8,128)(2,1)S(1)}, bf16[4,128,256]{2,1,0:T(8,128)(2,1)S(1)}, u32[]{:S(2)}, u32[]{:S(2)}) %collective-permute-start.9) | collective-permute-done | bytes 262176 | tf_op jit(solution)/shard_map/ppermute | solution.py:244
  80.7 1.7 %collective-permute-start.11 = (bf16[128,256]{1,0:T(8,128)(2,1)S(1)}, bf16[128,256]{1,0:T(8,128)(2,1)S(1)}, u32[]{:S(2)}, u32[]{:S(2)}) collective-permute-start(bf16[128,256]{1,0:T(8,128)(2,1)S(1)} %get-tuple-element.45), channel_id=1, source_target_pairs={{0,2},{1,3},{2,0},{3,1},{4,6},{5,7},{6,4},{7,5},{8,10},{9,11},{10,... | collective-permute-start | bytes 196616 | tf_op jit(solution)/shard_map/ppermute | solution.py:247
  82.3 1.5 %collective-permute-start.12 = (bf16[128,256]{1,0:T(8,128)(2,1)S(1)}, bf16[128,256]{1,0:T(8,128)(2,1)S(1)}, u32[]{:S(2)}, u32[]{:S(2)}) collective-permute-start(bf16[128,256]{1,0:T(8,128)(2,1)S(1)} %get-tuple-element.46), channel_id=1, source_target_pairs={{0,4},{1,5},{2,6},{3,7},{4,0},{5,1},{6,2},{7,3},{8,12},{9,13},{10,... | collective-permute-start | bytes 196616 | tf_op jit(solution)/shard_map/ppermute | solution.py:247
  85.0 1.0 %copy.10 = bf16[1,128,2048]{2,1,0:T(8,128)(2,1)} copy(bf16[1,128,2048]{1,2,0:T(8,128)(2,1)S(1)} %bitcast.41) | data formatting | bytes 1048576
  86.0 1.3 %collective-permute-done.12.refs_2_ = bf16[128,256]{1,0:T(8,128)(2,1)S(1)} collective-permute-done((bf16[128,256]{1,0:T(8,128)(2,1)S(1)}, bf16[128,256]{1,0:T(8,128)(2,1)S(1)}, u32[]{:S(2)}, u32[]{:S(2)}) %collective-permute-start.12) | collective-permute-done | bytes 65568 | tf_op jit(solution)/shard_map/ppermute | solution.py:247
  87.3 1.7 %collective-permute-done.13.refs_3_ = bf16[128,256]{1,0:T(8,128)(2,1)S(1)} collective-permute-done((bf16[128,256]{1,0:T(8,128)(2,1)S(1)}, bf16[128,256]{1,0:T(8,128)(2,1)S(1)}, u32[]{:S(2)}, u32[]{:S(2)}) %collective-permute-start.13) | collective-permute-done | bytes 65568 | tf_op jit(solution)/shard_map/ppermute | solution.py:247
  89.6 1.7 %shard_map.87 = (bf16[128,512]{1,0:T(8,128)(2,1)}, bf16[128,512]{1,0:T(8,128)(2,1)}) custom-call(s32[4]{0:T(128)} %pad_add_fusion.place.refs_0_, bf16[128,256]{1,0:T(8,128)(2,1)} %get-tuple-element.47.refs_0_, bf16[128,256]{1,0:T(8,128)(2,1)} %copy-done.7, bf16[128,256]{1,0:T(8,128)(2,1)} %copy-done.8, bf16[128,256]{1,0:T(8,128)(2,1)} %copy-done.9), custom_call_target="tpu_custom_call" | custom-call | bytes 524304 | tf_op jit(solution)/shard_map/pallas_call | solution.py:21
  (72 shorter events, 7.5 us)
Async XLA Ops:
  3.7 22.0 %copy-start.10 = (bf16[128,256]{1,0:T(8,128)(2,1)S(1)}, bf16[128,256]{1,0:T(8,128)(2,1)}, u32[]{:S(2)}) copy-start(bf16[128,256]{1,0:T(8,128)(2,1)} %get-tuple-element.23) | copy-start | bytes 196612
  3.8 34.9 %all-to-all-start = ((bf16[4,128,1024]{2,1,0:T(8,128)(2,1)}), bf16[4,128,1024]{2,1,0:T(8,128)(2,1)S(1)}, u32[]{:S(2)}, u32[]{:S(2)}) async-start(bf16[4,128,1024]{2,1,0:T(8,128)(2,1)} %get-tuple-element.22), calls=%async_computation | async-start | bytes 2097152 | tf_op jit(solution)/shard_map/all_to_all | solution.py:240
  9.1 15.7 %collective-permute-start.1 = (bf16[128,256]{1,0:T(8,128)(2,1)S(1)}, bf16[128,256]{1,0:T(8,128)(2,1)S(1)}, u32[]{:S(2)}, u32[]{:S(2)}) collective-permute-start(bf16[128,256]{1,0:T(8,128)(2,1)S(1)} %copy-done.17), channel_id=1, source_target_pairs={{0,4},{1,5},{2,6},{3,7},{4,0},{5,1},{6,2},{7,3},{8,12},{9,13},{10,... | collective-permute-start | bytes 196616 | tf_op jit(solution)/shard_map/ppermute | solution.py:247
  11.1 14.6 %collective-permute-start.2 = (bf16[128,256]{1,0:T(8,128)(2,1)S(1)}, bf16[128,256]{1,0:T(8,128)(2,1)S(1)}, u32[]{:S(2)}, u32[]{:S(2)}) collective-permute-start(bf16[128,256]{1,0:T(8,128)(2,1)S(1)} %copy-done.16), channel_id=1, source_target_pairs={{0,6},{1,7},{2,4},{3,5},{4,2},{5,3},{6,0},{7,1},{8,14},{9,15},{10,... | collective-permute-start | bytes 196616 | tf_op jit(solution)/shard_map/ppermute | solution.py:247
  12.6 13.2 %collective-permute-start = (bf16[128,256]{1,0:T(8,128)(2,1)S(1)}, bf16[128,256]{1,0:T(8,128)(2,1)S(1)}, u32[]{:S(2)}, u32[]{:S(2)}) collective-permute-start(bf16[128,256]{1,0:T(8,128)(2,1)S(1)} %copy-done.15), channel_id=1, source_target_pairs={{0,2},{1,3},{2,0},{3,1},{4,6},{5,7},{6,4},{7,5},{8,10},{9,11},{10,... | collective-permute-start | bytes 196616 | tf_op jit(solution)/shard_map/ppermute | solution.py:247
  25.8 7.8 %collective-permute-start.4 = (bf16[4,128,256]{2,1,0:T(8,128)(2,1)S(1)}, bf16[4,128,256]{2,1,0:T(8,128)(2,1)S(1)}, u32[]{:S(2)}, u32[]{:S(2)}) collective-permute-start(bf16[4,128,256]{2,1,0:T(8,128)(2,1)S(1)} %pad_maximum_fusion.kv_same), channel_id=1, source_target_pairs={{0,8},{1,9},{2,10},{3,11},{4,12},{5,13},{6,14},{7,15},{8,16},{9,17... | collective-permute-start | bytes 786440 | tf_op jit(solution)/shard_map/ppermute | solution.py:244
  29.3 5.0 %collective-permute-start.3 = (bf16[4,128,256]{2,1,0:T(8,128)(2,1)S(1)}, bf16[4,128,256]{2,1,0:T(8,128)(2,1)S(1)}, u32[]{:S(2)}, u32[]{:S(2)}) collective-permute-start(bf16[4,128,256]{2,1,0:T(8,128)(2,1)S(1)} %pad_maximum_fusion.kv_same), channel_id=1, source_target_pairs={{0,1},{1,0},{2,3},{3,2},{4,5},{5,4},{6,7},{7,6},{8,9},{9,8},{10,11... | collective-permute-start | bytes 786440 | tf_op jit(solution)/shard_map/ppermute | solution.py:247
  33.6 1.5 %collective-permute-start.5 = (bf16[4,128,256]{2,1,0:T(8,128)(2,1)S(1)}, bf16[4,128,256]{2,1,0:T(8,128)(2,1)S(1)}, u32[]{:S(2)}, u32[]{:S(2)}) collective-permute-start(bf16[4,128,256]{2,1,0:T(8,128)(2,1)S(1)} %collective-permute-done.4.old_same), channel_id=1, source_target_pairs={{0,1},{1,0},{2,3},{3,2},{4,5},{5,4},{6,7},{7,6},{8,9},{9,8},{10,11... | collective-permute-start | bytes 786440 | tf_op jit(solution)/shard_map/ppermute | solution.py:247
  33.6 0.7 collective-permute-start.6
  51.0 12.4 %copy-start.18 = (f32[16,128]{1,0:T(8,128)S(1)}, f32[16,128]{1,0:T(8,128)}, u32[]{:S(2)}) copy-start(f32[16,128]{1,0:T(8,128)} %get-tuple-element.35) | copy-start | bytes 24580
  53.6 14.0 %copy-start.11 = (f32[4,128]{1,0:T(4,128)S(1)}, f32[4,128]{1,0:T(4,128)}, u32[]{:S(2)}) copy-start(f32[4,128]{1,0:T(4,128)} %shard_map.88) | copy-start | bytes 6148
  53.6 15.7 %copy-start.3 = (f32[4,128,256]{2,1,0:T(8,128)S(1)}, f32[4,128,256]{2,1,0:T(8,128)}, u32[]{:S(2)}) copy-start(f32[4,128,256]{2,1,0:T(8,128)} %get-tuple-element.33) | copy-start | bytes 1572868
  54.4 13.2 %collective-permute-start.14 = (f32[2,128]{1,0:T(2,128)S(1)}, f32[2,128]{1,0:T(2,128)S(1)}, u32[]{:S(2)}, u32[]{:S(2)}) collective-permute-start(f32[2,128]{1,0:T(2,128)S(1)} %broadcast_select_fusion), channel_id=1, source_target_pairs={{0,16},{1,17},{2,18},{3,19},{4,20},{5,21},{6,22},{7,23},{8,24},{9,... | collective-permute-start | bytes 3080 | tf_op jit(solution)/shard_map/ppermute | solution.py:247
  62.9 17.0 %copy-start.2 = (f32[4,128,256]{2,1,0:T(8,128)S(1)}, f32[4,128,256]{2,1,0:T(8,128)}, u32[]{:S(2)}) copy-start(f32[4,128,256]{2,1,0:T(8,128)} %get-tuple-element.31) | copy-start | bytes 1572868
  62.9 6.4 %collective-permute-start.8 = (bf16[4,128,256]{2,1,0:T(8,128)(2,1)S(1)}, bf16[4,128,256]{2,1,0:T(8,128)(2,1)S(1)}, u32[]{:S(2)}, u32[]{:S(2)}) collective-permute-start(bf16[4,128,256]{2,1,0:T(8,128)(2,1)S(1)} %copy-done.14), channel_id=1, source_target_pairs={{0,1},{1,0},{2,3},{3,2},{4,5},{5,4},{6,7},{7,6},{8,9},{9,8},{10,11... | collective-permute-start | bytes 786440 | tf_op jit(solution)/shard_map/ppermute | solution.py:247
  63.0 8.4 %collective-permute-start.7 = (bf16[4,128,256]{2,1,0:T(8,128)(2,1)S(1)}, bf16[4,128,256]{2,1,0:T(8,128)(2,1)S(1)}, u32[]{:S(2)}, u32[]{:S(2)}) collective-permute-start(bf16[4,128,256]{2,1,0:T(8,128)(2,1)S(1)} %copy-done.13), channel_id=1, source_target_pairs={{0,1},{1,0},{2,3},{3,2},{4,5},{5,4},{6,7},{7,6},{8,9},{9,8},{10,11... | collective-permute-start | bytes 786440 | tf_op jit(solution)/shard_map/ppermute | solution.py:247
  63.5 16.5 %collective-permute-start.10 = (f32[16,128]{1,0:T(8,128)S(1)}, f32[16,128]{1,0:T(8,128)S(1)}, u32[]{:S(2)}, u32[]{:S(2)}) collective-permute-start(f32[16,128]{1,0:T(8,128)S(1)} %copy-done.18), channel_id=1, source_target_pairs={{16,1},{18,3},{20,5},{22,7},{24,9},{26,11},{28,13},{30,15}} | collective-permute-start | bytes 24584 | tf_op jit(solution)/shard_map/ppermute | solution.py:244
  64.1 20.6 %all-to-all-start.1 = ((bf16[4,128,512]{2,1,0:T(8,128)(2,1)}), bf16[4,128,512]{2,1,0:T(8,128)(2,1)S(1)}, u32[]{:S(2)}, u32[]{:S(2)}) async-start(bf16[4,128,512]{2,1,0:T(8,128)(2,1)} %get-tuple-element.30), calls=%async_computation.1 | async-start | bytes 1048576 | tf_op jit(solution)/shard_map/all_to_all | solution.py:240
  67.7 3.6 %collective-permute-start.15 = (f32[1,128]{1,0:T(1,128)S(1)}, f32[1,128]{1,0:T(1,128)S(1)}, u32[]{:S(2)}, u32[]{:S(2)}) collective-permute-start(f32[1,128]{1,0:T(1,128)S(1)} %broadcast_select_fusion.1), channel_id=1, source_target_pairs={{0,8},{1,9},{2,10},{3,11},{4,12},{5,13},{6,14},{7,15},{8,0},{9,1},... | collective-permute-start | bytes 1544 | tf_op jit(solution)/shard_map/ppermute | solution.py:247
  69.4 10.5 %collective-permute-start.9 = (bf16[4,128,256]{2,1,0:T(8,128)(2,1)S(1)}, bf16[4,128,256]{2,1,0:T(8,128)(2,1)S(1)}, u32[]{:S(2)}, u32[]{:S(2)}) collective-permute-start(bf16[4,128,256]{2,1,0:T(8,128)(2,1)S(1)} %add_convert_fusion), channel_id=1, source_target_pairs={{8,0},{9,1},{10,2},{11,3},{12,4},{13,5},{14,6},{15,7},{16,8},{17,9... | collective-permute-start | bytes 786440 | tf_op jit(solution)/shard_map/ppermute | solution.py:244
  71.3 12.8 %collective-permute-start.16 = (f32[64]{0:T(128)S(1)}, f32[64]{0:T(128)S(1)}, u32[]{:S(2)}, u32[]{:S(2)}) collective-permute-start(f32[64]{0:T(128)S(1)} %fusion.10), channel_id=1, source_target_pairs={{0,1},{1,0},{2,3},{3,2},{4,5},{5,4},{6,7},{7,6},{8,9},{9,8},{10,11... | collective-permute-start | bytes 776 | tf_op jit(solution)/shard_map/ppermute | solution.py:247
  80.7 5.4 %collective-permute-start.11 = (bf16[128,256]{1,0:T(8,128)(2,1)S(1)}, bf16[128,256]{1,0:T(8,128)(2,1)S(1)}, u32[]{:S(2)}, u32[]{:S(2)}) collective-permute-start(bf16[128,256]{1,0:T(8,128)(2,1)S(1)} %get-tuple-element.45), channel_id=1, source_target_pairs={{0,2},{1,3},{2,0},{3,1},{4,6},{5,7},{6,4},{7,5},{8,10},{9,11},{10,... | collective-permute-start | bytes 196616 | tf_op jit(solution)/shard_map/ppermute | solution.py:247
  82.3 5.0 %collective-permute-start.12 = (bf16[128,256]{1,0:T(8,128)(2,1)S(1)}, bf16[128,256]{1,0:T(8,128)(2,1)S(1)}, u32[]{:S(2)}, u32[]{:S(2)}) collective-permute-start(bf16[128,256]{1,0:T(8,128)(2,1)S(1)} %get-tuple-element.46), channel_id=1, source_target_pairs={{0,4},{1,5},{2,6},{3,7},{4,0},{5,1},{6,2},{7,3},{8,12},{9,13},{10,... | collective-permute-start | bytes 196616 | tf_op jit(solution)/shard_map/ppermute | solution.py:247
  83.8 5.2 %collective-permute-start.13 = (bf16[128,256]{1,0:T(8,128)(2,1)S(1)}, bf16[128,256]{1,0:T(8,128)(2,1)S(1)}, u32[]{:S(2)}, u32[]{:S(2)}) collective-permute-start(bf16[128,256]{1,0:T(8,128)(2,1)S(1)} %get-tuple-element.44), channel_id=1, source_target_pairs={{0,6},{1,7},{2,4},{3,5},{4,2},{5,3},{6,0},{7,1},{8,14},{9,15},{10,... | collective-permute-start | bytes 196616 | tf_op jit(solution)/shard_map/ppermute | solution.py:247
  (14 other events, 64.8 us)

commit v4 on v3

v4 whole, which is shorter than its diff:
```python
import functools
import math

import jax
import jax.numpy as jnp
from jax import lax
from jax.experimental import pallas as pl
from jax.experimental.pallas import tpu as pltpu
from jax.sharding import PartitionSpec as P

HEAD_SIZE = 128
WINDOW = 1024
NEG_FILL = -1e30
HALO = 16
VMEM_BYTES = 56 * 1024 * 1024
NT = (((1,), (1,)), ((), ()))


def place_of(group, share):
    device = lax.axis_index("seq")
    return lax.div(device, group), lax.rem(device, share), lax.div(lax.rem(device, group), share)


def run(kernel, out_shape, operands, scratch=(), flops=0):
    vmem = pl.BlockSpec(memory_space=pltpu.VMEM)
    moved = list(operands) + list(out_shape)
    return pl.pallas_call(
        kernel,
        out_shape=out_shape,
        in_specs=[vmem] * len(operands),
        out_specs=[vmem] * len(out_shape),
        scratch_shapes=list(scratch),
        cost_estimate=pl.CostEstimate(
            flops=flops, bytes_accessed=sum(math.prod(a.shape) * a.dtype.itemsize for a in moved), transcendentals=0
        ),
        compiler_params=pltpu.CompilerParams(vmem_limit_bytes=VMEM_BYTES),
    )(*operands)


def columns_of(index, width=HEAD_SIZE):
    return pl.ds(pl.multiple_of(index * width, HEAD_SIZE), width)


def pack_kernel(place, queries, grad_out, keys, values, *parts):
    rows = queries.shape[0]
    turns = len(parts) // 2
    heads = queries.shape[1] // HEAD_SIZE // turns
    for turn in range(turns):
        target = place[2] ^ turn
        part = parts[turn]
        part[:, :HEAD_SIZE] = keys[:, columns_of(target)]
        part[:, HEAD_SIZE:] = values[:, columns_of(target)]
        part = parts[turns + turn]
        for base, source in ((0, queries), (heads, grad_out)):
            for head in range(heads):
                at = slice((base + head) * rows, (base + head + 1) * rows)
                part[at] = source[:, columns_of(target * heads + head)]


def unpack_queries_kernel(place, *refs):
    parts, grad_queries = refs[:-1], refs[-1]
    for turn, part in enumerate(parts):
        grad_queries[:, columns_of(place[2] ^ turn, part.shape[1])] = part[...]


def unpack_kernel(place, *refs):
    parts, (grad_keys, grad_values) = refs[:-2], refs[-2:]
    head_at = place[2]
    for turn, part in enumerate(parts):
        at = columns_of(head_at ^ turn)
        grad_keys[:, at] = part[:, :HEAD_SIZE]
        grad_values[:, at] = part[:, HEAD_SIZE:]


def attend_kernel(scale, turns, place, *refs):
    kv_same, kv_other, old_same, old_other, halo, all_taps = refs[:6]
    query_grads = refs[6 : 6 + turns]
    grad_qs = refs[6 + turns : 6 + 2 * turns]
    send, keep_old, keep_own, tap_keep = refs[6 + 2 * turns : 10 + 2 * turns]
    key_all, key_t, value_all, mix_all, dkey, dmix, *work = refs[10 + 2 * turns :]
    rows, width = grad_qs[0].shape
    blocks = turns
    span = 2 * blocks
    length = span * rows
    lanes = 2 * HEAD_SIZE
    pairs = width // lanes
    tap_count = all_taps.shape[0]
    group_at, parity, head_at = place
    taps = all_taps[:, columns_of(head_at)]
    inv_root = 1.0 / math.sqrt(HEAD_SIZE)
    log2_scale = inv_root * math.log2(math.e)
    score_refs, gprob_refs, low_refs, dscore_refs = work[0:2], work[2:4], work[4:6], work[6:8]

    def block_at(turn, core):
        return 2 * (head_at ^ turn) + core

    value_all[:HALO] = halo[...].astype(jnp.float32)
    for start, same, other in ((0, old_same, old_other), (span, kv_same, kv_other)):
        for turn in range(blocks):
            for source, core in ((same, parity), (other, 1 - parity)):
                first = pl.multiple_of((start + block_at(turn, core)) * rows, rows)
                key_all[pl.ds(first, rows)] = source[turn, :, :HEAD_SIZE]
                value_all[pl.ds(first + HALO, rows)] = source[turn, :, HEAD_SIZE:].astype(jnp.float32)
    for start in range(HALO, HALO + 2 * length, rows):
        mixed = taps[0:1] * value_all[start : start + rows]
        for index_k in range(1, tap_count):
            mixed = mixed + taps[index_k : index_k + 1] * value_all[start - index_k : start - index_k + rows]
        mix_all[start - HALO : start - HALO + rows] = mixed.astype(jnp.bfloat16)
    key_t[...] = jnp.transpose(key_all[...])
    dkey[...] = jnp.zeros_like(dkey)
    dmix[...] = jnp.zeros_like(dmix)
    fill = jnp.where(group_at == 0, NEG_FILL, 0.0).astype(jnp.float32)
    key_at = lax.broadcasted_iota(jnp.int32, (rows, lanes), 0)
    query_at = lax.broadcasted_iota(jnp.int32, (rows, lanes), 1) & (rows - 1)
    causal = key_at <= query_at
    stats = {}

    def places(n):
        step, pair = n // pairs, n % pairs
        number = block_at(step, parity)
        return step, pair, number, pl.multiple_of(number * rows, rows)

    def stacked(step, base):
        return query_grads[step][base // HEAD_SIZE * rows : (base + lanes) // HEAD_SIZE * rows]

    def by_eight(array):
        return array.reshape(-1, 8, array.shape[1])

    def scores_stage(n):
        step, pair, number, first = places(n)
        seen = pl.ds(first, length + rows)
        scores = lax.dot_general(
            key_all[seen], stacked(step, pair * lanes), NT, preferred_element_type=jnp.float32
        )
        grads = lax.dot_general(
            mix_all[seen], stacked(step, width + pair * lanes), NT, preferred_element_type=jnp.float32
        )
        edge = jnp.where(causal, scores[length:], scores[:rows] + fill)
        score_refs[n % 2][:rows] = edge
        score_refs[n % 2][rows:] = scores[rows:length]
        gprob_refs[n % 2][:rows] = jnp.where(causal, grads[length:], grads[:rows])
        gprob_refs[n % 2][rows:] = grads[rows:length]
        peak = jnp.max(by_eight(edge), axis=0)
        for c in range(1, span):
            part = jnp.max(by_eight(scores[c * rows : (c + 1) * rows]), axis=0)
            peak = jnp.maximum(peak, part + jnp.where(number + c < span, fill, 0.0))
        stats[n] = jnp.max(peak, axis=0, keepdims=True) * log2_scale

    def softmax_stage(n):
        step, pair, number, first = places(n)
        peak = stats[n]
        scores, gprob, low, dscore = (refs[n % 2] for refs in (score_refs, gprob_refs, low_refs, dscore_refs))
        total = jnp.zeros((8, lanes), jnp.float32)
        delta = jnp.zeros((8, lanes), jnp.float32)
        for c in range(span):
            at = slice(c * rows, (c + 1) * rows)
            shift = -peak if c == 0 else jnp.where(number + c < span, fill, 0.0) - peak
            prob = jnp.exp2(scores[at] * log2_scale + shift)
            total = total + jnp.sum(by_eight(prob), axis=0)
            delta = delta + jnp.sum(by_eight(prob * gprob[at]), axis=0)
            low[at] = prob.astype(jnp.bfloat16)
        inverse = 1.0 / jnp.sum(total, axis=0, keepdims=True)
        delta = jnp.sum(delta, axis=0, keepdims=True) * inverse
        for c in range(span):
            at = slice(c * rows, (c + 1) * rows)
            dscore[at] = low[at] * (gprob[at] - delta).astype(jnp.bfloat16)
        zero = jnp.zeros((), jnp.bfloat16)
        for ref in (low, dscore):
            edge = ref[:rows]
            ref[length:] = jnp.where(causal, edge, zero)
            ref[:rows] = jnp.where(causal, zero, edge)
        stats[n] = inverse

    def gradient_stage(n):
        step, pair, number, first = places(n)
        seen = pl.ds(first, length + rows)
        inverse = stats[n]
        column = jnp.transpose(jnp.broadcast_to(inverse, (HEAD_SIZE, lanes)))
        query = (stacked(step, pair * lanes).astype(jnp.float32) * column).astype(jnp.bfloat16)
        grad = (stacked(step, width + pair * lanes).astype(jnp.float32) * column).astype(jnp.bfloat16)
        low, dscore = low_refs[n % 2], dscore_refs[n % 2]
        dmix[pl.ds(first + HALO, length + rows)] += jnp.dot(low[...], grad, preferred_element_type=jnp.float32)
        dkey[seen] += jnp.dot(dscore[...], query, preferred_element_type=jnp.float32)
        dquery = jnp.dot(key_t[:, seen], dscore[...], preferred_element_type=jnp.float32)
        dquery = jnp.transpose(dquery * (inverse * inv_root)).astype(jnp.bfloat16)
        for h in range(2):
            base = pair * lanes + h * HEAD_SIZE
            grad_qs[step][:, base : base + HEAD_SIZE] = dquery[h * rows : (h + 1) * rows]

    count = blocks * pairs
    for n in range(count + 2):
        if n < count:
            scores_stage(n)
        if 1 <= n <= count:
            softmax_stage(n - 1)
        if n >= 2:
            gradient_stage(n - 2)

    def convolved(start, size):
        total = taps[0:1] * dmix[pl.ds(start, size)]
        for index_k in range(1, tap_count):
            total = total + taps[index_k : index_k + 1] * dmix[pl.ds(start + index_k, size)]
        return total

    for start, keep, base in ((0, keep_old, 0), (span, keep_own, blocks * rows)):
        for turn in range(blocks):
            for target, core, offset in ((keep, parity, 0), (send, 1 - parity, base)):
                first = pl.multiple_of((start + block_at(turn, core)) * rows, rows)
                at = slice(offset + turn * rows, offset + (turn + 1) * rows)
                target[at, :HEAD_SIZE] = (dkey[pl.ds(first, rows)] * inv_root).astype(target.dtype)
                target[at, HEAD_SIZE:] = convolved(first + HALO, rows).astype(target.dtype)
    note = slice(2 * blocks * rows, 2 * blocks * rows + HALO)
    send[note, HEAD_SIZE:] = convolved(0, HALO).astype(send.dtype)
    sums = [jnp.zeros((8, HEAD_SIZE), jnp.float32)] * tap_count
    for start in range(HALO, HALO + 2 * length, rows):
        grad = dmix[start : start + rows]
        for index_k in range(tap_count):
            sums[index_k] = sums[index_k] + jnp.sum(
                by_eight(grad * value_all[start - index_k : start - index_k + rows]), axis=0
            )
    tap_grads = jnp.concatenate([jnp.sum(total, axis=0, keepdims=True) for total in sums], axis=0) * scale
    low, high = tap_grads[:, : HEAD_SIZE // 2], tap_grads[:, HEAD_SIZE // 2 :]
    tap_keep[...] = jnp.where(parity == 0, low, high)
    theirs = jnp.where(parity == 0, high, low)
    upper = theirs.astype(send.dtype).astype(jnp.float32)
    theirs = jnp.concatenate([upper, theirs - upper], axis=0)
    theirs = jnp.concatenate([theirs, jnp.zeros((HALO - 2 * tap_count, HEAD_SIZE // 2), jnp.float32)], axis=0)
    theirs = jnp.concatenate([theirs, jnp.zeros_like(theirs)], axis=1)
    send[note, :HEAD_SIZE] = theirs.astype(send.dtype)


def on_device(queries, keys, values, conv_taps, grad_out):
    rows, width = queries.shape[1:]
    kv_width = keys.shape[2]
    tap_count = conv_taps.shape[0]
    kv_heads = kv_width // HEAD_SIZE
    group = WINDOW // rows
    share = group // kv_heads
    count = lax.axis_size("seq")
    planes = count // group
    own_width = width // kv_heads
    bf16, f32 = jnp.bfloat16, jnp.float32
    shape = jax.ShapeDtypeStruct
    plane, parity, head_at = place_of(group, share)

    def launch(kernel, out_shape, operands, **options):
        return run(lambda *refs: kernel(place_of(group, share), *refs), out_shape, operands, **options)

    def routed(array, distance, chosen=lambda i: True):
        route = [(i, i + distance) for i in range(count) if 0 <= i + distance < count and chosen(i)]
        return lax.ppermute(array, "seq", route)

    def flipped(array, bits):
        return lax.ppermute(array, "seq", [(i, i ^ bits) for i in range(count)])

    def after(others, *arrays):
        return lax.optimization_barrier((*arrays, *others))[: len(arrays)]

    def exchanged(parts):
        return [parts[0]] + [flipped(parts[turn], turn * share) for turn in range(1, kv_heads)]

    kv_shape = shape((rows, 2 * HEAD_SIZE), bf16)
    query_shape = shape((2 * own_width // HEAD_SIZE * rows, HEAD_SIZE), bf16)
    parts = launch(
        pack_kernel,
        [kv_shape] * kv_heads + [query_shape] * kv_heads,
        (queries[0], grad_out[0], keys[0], values[0]),
    )
    kv_same = jnp.stack(exchanged(parts[:kv_heads]))
    old_same = routed(kv_same, group)
    query_grads = exchanged(after([kv_same], *parts[kv_heads:]))
    kv_same, old_same = lax.optimization_barrier((kv_same, old_same))
    old_other = flipped(old_same, 1)
    kv_other = flipped(kv_same, 1)
    last = lax.dynamic_index_in_dim(kv_same, head_at ^ (kv_heads - 1), 0, keepdims=False)
    reach = 2 * group - (share - 1)
    halo = routed(last[rows - HALO :, HEAD_SIZE:], reach, lambda i: i % share == share - 1)
    lanes = 2 * HEAD_SIZE
    group_rows = kv_heads * rows
    scale = 1.0 / math.sqrt(rows * count * lax.axis_size("rep"))
    *grad_q, send, keep_old, keep_own, tap_keep = launch(
        functools.partial(attend_kernel, scale, kv_heads),
        [shape((rows, own_width), bf16)] * kv_heads
        + [
            shape((2 * group_rows + HALO, lanes), bf16),
            shape((group_rows, lanes), f32),
            shape((group_rows, lanes), f32),
            shape((tap_count, HEAD_SIZE // 2), f32),
        ],
        (kv_same, kv_other, old_same, old_other, halo, conv_taps, *query_grads),
        scratch=[
            pltpu.VMEM((2 * WINDOW, HEAD_SIZE), bf16),
            pltpu.VMEM((HEAD_SIZE, 2 * WINDOW), bf16),
            pltpu.VMEM((HALO + 2 * WINDOW, HEAD_SIZE), f32),
            pltpu.VMEM((2 * WINDOW, HEAD_SIZE), bf16),
            pltpu.VMEM((2 * WINDOW, HEAD_SIZE), f32),
            pltpu.VMEM((HALO + 2 * WINDOW + HALO, HEAD_SIZE), f32),
        ]
        + [pltpu.VMEM((WINDOW, lanes), f32)] * 4
        + [pltpu.VMEM((WINDOW + rows, lanes), bf16)] * 4,
        flops=10 * kv_heads * rows * (WINDOW + rows) * own_width,
    )
    got = flipped(send, 1)
    note = got[2 * group_rows :].astype(f32)
    old_sum = (keep_old + got[:group_rows].astype(f32)).astype(bf16)
    grad_q = after([old_sum], *grad_q)
    returned = routed(old_sum, -group)
    grad_q = exchanged(grad_q)
    halo, tap_grads = note[:, HEAD_SIZE:], note[:, : HEAD_SIZE // 2]
    tap_grads = tap_keep + (tap_grads[:tap_count] + tap_grads[tap_count : 2 * tap_count])
    short = planes == tap_count == 4
    if short:
        low, high = jnp.split(tap_grads, 2)
        mine, theirs = jnp.where(plane < 2, low, high), jnp.where(plane < 2, high, low)
        theirs = jnp.pad(theirs, ((0, 6), (0, HEAD_SIZE // 2)))
        note = flipped(jnp.concatenate([halo, theirs], axis=0), 2 * group)
        tap_grads = mine + note[HALO : HALO + 2, : HEAD_SIZE // 2]
        returned_halo = jnp.where(plane < 2, note[:HALO], 0.0)
    else:
        returned_halo = routed(halo, -2 * group)
    (keep_own,) = after(grad_q, keep_own)
    total = keep_own + got[group_rows : 2 * group_rows].astype(f32) + returned.astype(f32)
    halo_block = jnp.pad(returned_halo, ((rows - HALO, 0), (HEAD_SIZE, 0)))
    owned = []
    for turn in range(kv_heads):
        mine = total[turn * rows : (turn + 1) * rows]
        owned.append((mine + jnp.where((head_at ^ turn) == kv_heads - 1, halo_block, 0.0)).astype(bf16))
    grad_q = after(owned, *grad_q)
    owned = exchanged(owned)
    (grad_queries,) = launch(unpack_queries_kernel, [shape((rows, width), bf16)], tuple(grad_q))
    owned = after([grad_queries], *owned)
    grad_keys, grad_values = launch(
        unpack_kernel, [shape((rows, kv_width), bf16), shape((rows, kv_width), bf16)], tuple(owned)
    )
    if short:
        low, high = tap_grads[0], tap_grads[1]
        even = plane % 2 == 0
        grad_taps = jnp.where(even, low, high) + flipped(jnp.where(even, high, low), group)
    else:
        spread = jnp.zeros((tap_count, kv_width), f32)
        spread = lax.dynamic_update_slice(spread, tap_grads, (0, (2 * head_at + parity) * (HEAD_SIZE // 2)))
        grad_taps = jnp.sum(lax.all_to_all(spread.reshape(count, -1), "seq", 0, 0, tiled=True), axis=0)
    grad_taps = lax.psum(grad_taps, "rep")
    return grad_queries[None], grad_keys[None], grad_values[None], grad_taps


def solution(mesh):
    in_specs = (
        P("rep", "seq", None),
        P("rep", "seq", None),
        P("rep", "seq", None),
        P(),
        P("rep", "seq", None),
    )
    out_specs = (P("rep", "seq", None), P("rep", "seq", None), P("rep", "seq", None), P("seq"))
    return jax.shard_map(
        on_device, mesh=mesh, in_specs=in_specs, out_specs=out_specs, check_vma=False
    )
```

time: 91.8 us -> 73.7 us (0.80)
  waiting for transfers between devices: 30.1 us -> 18.2 us
  starting transfers between devices: 32.7 us -> 29.1 us
  Pallas kernels: 20.9 us -> 18.4 us
    ppermute x4 -> x3, waiting for transfers between devices: 12.7 us -> 0.3 us  [routed(): return lax.ppermute(array, 'seq', route)]
    all_to_all x2 -> x0, starting transfers between devices: 8.79 us -> none  [swap(): lax.all_to_all(array, 'seq', 0, 0, axis_index_groups=groups, tiled=True)]
    ppermute x13 -> x17, starting transfers between devices: 17.8 us -> 23.6 us  [flipped(): return lax.ppermute(array, 'seq', [(i, i ^ bits) for i in range(count)])]
    pallas_call x5 -> x4, Pallas kernels: 20.9 us -> 18.4 us  [run(): pl.pallas_call(kernel, out_shape=out_shape, in_specs=[vmem] * len(operand...]
    convert_element_type x2 -> x3, other arithmetic: 0.72 us -> 1.84 us  [the longest x1 1.18 us: on_device(): old_sum = (keep_old + got[:group_rows].astype(f32)).astype(bf16)]
    ppermute x4 -> x3, starting transfers between devices: 6.16 us -> 5.44 us  [routed(): return lax.ppermute(array, 'seq', route)]
    ppermute x13 -> x17, waiting for transfers between devices: 17.4 us -> 17.9 us  [flipped(): return lax.ppermute(array, 'seq', [(i, i ^ bits) for i in range(count)])]
    unnamed x39 -> x42, local copies, waits for them, and re-layouts: 3.37 us -> 3.45 us
  transfers between devices with their start and end apart: 19 -> 20, of which waited for: 8 -> 9; matrix products, arithmetic and copies ran while one was open for 3% -> 3% of each run, Pallas kernels for 3% -> 3%
where the time goes in v4:
time: 73.7 us; the launch traced here: 73.4 us
  starting transfers between devices  29.1 us (39%)
  Pallas kernels  18.4 us (25%)
  waiting for transfers between devices  18.2 us (25%)
  local copies, waits for them, and re-layouts  3.46 us (5%)
  other arithmetic  3.4 us (5%)
  between operations  0.83 us (1%)
    ppermute x17, starting transfers between devices, flipped(): return lax.ppermute(array, 'seq', [(i, i ^ bits) for i in range(count)])  23.6 us
    pallas_call x4, Pallas kernels, run(): pl.pallas_call(kernel, out_shape=out_shape, in_specs=[vmem] * len(operand...  18.4 us
    ppermute x17, waiting for transfers between devices, flipped(): return lax.ppermute(array, 'seq', [(i, i ^ bits) for i in range(count)])  17.9 us
    ppermute x3, starting transfers between devices, routed(): return lax.ppermute(array, 'seq', route)  5.44 us
    unnamed x42, local copies, waits for them, and re-layouts  3.45 us
  transfers between devices with their start and end apart: 20, of which 9 were waited for; matrix products, arithmetic and copies ran while one was open for 3% of the time, Pallas kernels for 3%

profile of v4, /device:TPU:0, one launch (start us, length us, event | category | flops | bytes accessed | tf_op | source)
XLA Modules:
  0.0 73.4 jit_solution(7774084338033836931)
XLA Ops:
  0.6 2.6 %shard_map.84 = (bf16[128,256]{1,0:T(8,128)(2,1)}, bf16[128,256]{1,0:T(8,128)(2,1)}, bf16[128,256]{1,0:T(8,128)(2,1)}, bf16[128,256]{1,0:T(8,128)(2,1)}, bf16[10...) custom-call(bf16[128,2048]{1,0:T(8,128)(2,1)} %bitcast.19, ...), custom_call_target="tpu_custom_call" | custom-call | bytes 2621440 | tf_op jit(solution)/shard_map/pallas_call | solution.py:27
  3.3 2.9 %collective-permute-start = (bf16[128,256]{1,0:T(8,128)(2,1)}, bf16[128,256]{1,0:T(8,128)(2,1)S(1)}, u32[]{:S(2)}, u32[]{:S(2)}) collective-permute-start(bf16[128,256]{1,0:T(8,128)(2,1)} %get-tuple-element.42), channel_id=1, source_target_pairs={{0,2},{1,3},{2,0},{3,1},{4,6},{5,7},{6,4},{7,5},{8,10},{9,11},{10,... | collective-permute-start | bytes 196616 | tf_op jit(solution)/shard_map/ppermute | solution.py:254
  6.2 1.5 %collective-permute-start.1 = (bf16[128,256]{1,0:T(8,128)(2,1)}, bf16[128,256]{1,0:T(8,128)(2,1)S(1)}, u32[]{:S(2)}, u32[]{:S(2)}) collective-permute-start(bf16[128,256]{1,0:T(8,128)(2,1)} %get-tuple-element.43), channel_id=1, source_target_pairs={{0,4},{1,5},{2,6},{3,7},{4,0},{5,1},{6,2},{7,3},{8,12},{9,13},{10,... | collective-permute-start | bytes 196616 | tf_op jit(solution)/shard_map/ppermute | solution.py:254
  7.7 1.2 %collective-permute-done = bf16[128,256]{1,0:T(8,128)(2,1)S(1)} collective-permute-done((bf16[128,256]{1,0:T(8,128)(2,1)}, bf16[128,256]{1,0:T(8,128)(2,1)S(1)}, u32[]{:S(2)}, u32[]{:S(2)}) %collective-permute-start) | collective-permute-done | bytes 65568 | tf_op jit(solution)/shard_map/ppermute | solution.py:254
  8.9 1.8 %collective-permute-done.1 = bf16[128,256]{1,0:T(8,128)(2,1)S(1)} collective-permute-done((bf16[128,256]{1,0:T(8,128)(2,1)}, bf16[128,256]{1,0:T(8,128)(2,1)S(1)}, u32[]{:S(2)}, u32[]{:S(2)}) %collective-permute-start.1) | collective-permute-done | bytes 65568 | tf_op jit(solution)/shard_map/ppermute | solution.py:254
  10.7 2.4 %collective-permute-done.2 = bf16[128,256]{1,0:T(8,128)(2,1)S(1)} collective-permute-done((bf16[128,256]{1,0:T(8,128)(2,1)}, bf16[128,256]{1,0:T(8,128)(2,1)S(1)}, u32[]{:S(2)}, u32[]{:S(2)}) %collective-permute-start.2) | collective-permute-done | bytes 65568 | tf_op jit(solution)/shard_map/ppermute | solution.py:254
  14.0 3.5 %collective-permute-start.3 = (bf16[4,128,256]{2,1,0:T(8,128)(2,1)S(1)}, bf16[4,128,256]{2,1,0:T(8,128)(2,1)S(1)}, u32[]{:S(2)}, u32[]{:S(2)}) collective-permute-start(bf16[4,128,256]{2,1,0:T(8,128)(2,1)S(1)} %pad_maximum_fusion.refs_0_), channel_id=1, source_target_pairs={{0,8},{1,9},{2,10},{3,11},{4,12},{5,13},{6,14},{7,15},{8,16},{9,17... | collective-permute-start | bytes 786440 | tf_op jit(solution)/shard_map/ppermute | solution.py:251
  18.7 2.5 %collective-permute-start.9 = (bf16[1024,128]{1,0:T(8,128)(2,1)S(1)}, bf16[1024,128]{1,0:T(8,128)(2,1)S(1)}, u32[]{:S(2)}, u32[]{:S(2)}) collective-permute-start(bf16[1024,128]{1,0:T(8,128)(2,1)S(1)} %copy-done.9), channel_id=1, source_target_pairs={{0,6},{1,7},{2,4},{3,5},{4,2},{5,3},{6,0},{7,1},{8,14},{9,15},{10,... | collective-permute-start | bytes 786440 | tf_op jit(solution)/shard_map/ppermute | solution.py:254
  21.9 4.8 %collective-permute-done.7.refs_7_ = bf16[1024,128]{1,0:T(8,128)(2,1)S(1)} collective-permute-done((bf16[1024,128]{1,0:T(8,128)(2,1)}, bf16[1024,128]{1,0:T(8,128)(2,1)S(1)}, u32[]{:S(2)}, u32[]{:S(2)}) %collective-permute-start.7) | collective-permute-done | bytes 262176 | tf_op jit(solution)/shard_map/ppermute | solution.py:254
  27.4 2.6 %collective-permute-done.8.refs_8_ = bf16[1024,128]{1,0:T(8,128)(2,1)S(1)} collective-permute-done((bf16[1024,128]{1,0:T(8,128)(2,1)S(1)}, bf16[1024,128]{1,0:T(8,128)(2,1)S(1)}, u32[]{:S(2)}, u32[]{:S(2)}) %collective-permute-start.8) | collective-permute-done | bytes 262176 | tf_op jit(solution)/shard_map/ppermute | solution.py:254
  31.6 12.1 %shard_map.85 = (bf16[128,512]{1,0:T(8,128)(2,1)}, bf16[128,512]{1,0:T(8,128)(2,1)}, bf16[128,512]{1,0:T(8,128)(2,1)}, bf16[128,512]{1,0:T(8,128)(2,1)}, bf16[10...) custom-call(bf16[4,128,256]{2,1,0:T(8,128)(2,1)} %copy-done.1, ...), custom_call_target="tpu_custom_call" | custom-call | flops 3019898880 | bytes 4215808 | tf_op jit(solution)/shard_map/pallas_call | solution.py:27
  43.7 1.9 %collective-permute-start.10 = (bf16[1040,256]{1,0:T(8,128)(2,1)}, bf16[1040,256]{1,0:T(8,128)(2,1)S(1)}, u32[]{:S(2)}, u32[]{:S(2)}) collective-permute-start(bf16[1040,256]{1,0:T(8,128)(2,1)} %get-tuple-element.60), channel_id=1, source_target_pairs={{0,1},{1,0},{2,3},{3,2},{4,5},{5,4},{6,7},{7,6},{8,9},{9,8},{10,11... | collective-permute-start | bytes 1597448 | tf_op jit(solution)/shard_map/ppermute | solution.py:254
  45.6 1.8 %collective-permute-done.10 = bf16[1040,256]{1,0:T(8,128)(2,1)S(1)} collective-permute-done((bf16[1040,256]{1,0:T(8,128)(2,1)}, bf16[1040,256]{1,0:T(8,128)(2,1)S(1)}, u32[]{:S(2)}, u32[]{:S(2)}) %collective-permute-start.10) | collective-permute-done | bytes 532512 | tf_op jit(solution)/shard_map/ppermute | solution.py:254
  48.0 3.5 %collective-permute-start.15 = (f32[24,128]{1,0:T(8,128)S(1)}, f32[24,128]{1,0:T(8,128)S(1)}, u32[]{:S(2)}, u32[]{:S(2)}) collective-permute-start(f32[24,128]{1,0:T(8,128)S(1)} %select_maximum_fusion), channel_id=1, source_target_pairs={{0,16},{1,17},{2,18},{3,19},{4,20},{5,21},{6,22},{7,23},{8,24},{9,... | collective-permute-start | bytes 36872 | tf_op jit(solution)/shard_map/ppermute | solution.py:254
  51.5 1.2 %add_convert_fusion = bf16[512,256]{1,0:T(8,128)(2,1)S(1)} fusion(f32[512,256]{1,0:T(8,128)} %get-tuple-element.59, bf16[1040,256]{1,0:T(8,128)(2,1)S(1)} %collective-permute-done.10), kind=kLoop, calls=%fused_computation.1 | loop fusion | flops 393216 | bytes 1048576 | tf_op jit(solution)/shard_map/convert_element_type | solution.py:305
  52.7 1.3 %collective-permute-start.14 = (bf16[512,256]{1,0:T(8,128)(2,1)S(1)}, bf16[512,256]{1,0:T(8,128)(2,1)S(1)}, u32[]{:S(2)}, u32[]{:S(2)}) collective-permute-start(bf16[512,256]{1,0:T(8,128)(2,1)S(1)} %add_convert_fusion), channel_id=1, source_target_pairs={{8,0},{9,1},{10,2},{11,3},{12,4},{13,5},{14,6},{15,7},{16,8},{17,9... | collective-permute-start | bytes 786440 | tf_op jit(solution)/shard_map/ppermute | solution.py:251
  54.0 1.0 %collective-permute-start.11 = (bf16[128,512]{1,0:T(8,128)(2,1)S(1)}, bf16[128,512]{1,0:T(8,128)(2,1)S(1)}, u32[]{:S(2)}, u32[]{:S(2)}) collective-permute-start(bf16[128,512]{1,0:T(8,128)(2,1)S(1)} %copy-done.19), channel_id=1, source_target_pairs={{0,2},{1,3},{2,0},{3,1},{4,6},{5,7},{6,4},{7,5},{8,10},{9,11},{10,... | collective-permute-start | bytes 393224 | tf_op jit(solution)/shard_map/ppermute | solution.py:254
  55.5 2.1 %collective-permute-start.13 = (bf16[128,512]{1,0:T(8,128)(2,1)S(1)}, bf16[128,512]{1,0:T(8,128)(2,1)S(1)}, u32[]{:S(2)}, u32[]{:S(2)}) collective-permute-start(bf16[128,512]{1,0:T(8,128)(2,1)S(1)} %copy-done.17), channel_id=1, source_target_pairs={{0,6},{1,7},{2,4},{3,5},{4,2},{5,3},{6,0},{7,1},{8,14},{9,15},{10,... | collective-permute-start | bytes 393224 | tf_op jit(solution)/shard_map/ppermute | solution.py:254
  57.6 2.7 %collective-permute-start.19 = (f32[64]{0:T(128)S(1)}, f32[64]{0:T(128)S(1)}, u32[]{:S(2)}, u32[]{:S(2)}) collective-permute-start(f32[64]{0:T(128)S(1)} %fusion.11), channel_id=1, source_target_pairs={{0,8},{1,9},{2,10},{3,11},{4,12},{5,13},{6,14},{7,15},{8,0},{9,1},... | collective-permute-start | bytes 776 | tf_op jit(solution)/shard_map/ppermute | solution.py:254
  60.4 2.4 %collective-permute-done.12.refs_2_ = bf16[128,512]{1,0:T(8,128)(2,1)S(1)} collective-permute-done((bf16[128,512]{1,0:T(8,128)(2,1)S(1)}, bf16[128,512]{1,0:T(8,128)(2,1)S(1)}, u32[]{:S(2)}, u32[]{:S(2)}) %collective-permute-start.12) | collective-permute-done | bytes 131104 | tf_op jit(solution)/shard_map/ppermute | solution.py:254
  64.2 1.1 %collective-permute-start.16 = (bf16[128,256]{1,0:T(8,128)(2,1)S(1)}, bf16[128,256]{1,0:T(8,128)(2,1)S(1)}, u32[]{:S(2)}, u32[]{:S(2)}) collective-permute-start(bf16[128,256]{1,0:T(8,128)(2,1)S(1)} %get-tuple-element.79), channel_id=1, source_target_pairs={{0,2},{1,3},{2,0},{3,1},{4,6},{5,7},{6,4},{7,5},{8,10},{9,11},{10,... | collective-permute-start | bytes 196616 | tf_op jit(solution)/shard_map/ppermute | solution.py:254
  65.9 1.8 %collective-permute-start.18 = (bf16[128,256]{1,0:T(8,128)(2,1)S(1)}, bf16[128,256]{1,0:T(8,128)(2,1)S(1)}, u32[]{:S(2)}, u32[]{:S(2)}) collective-permute-start(bf16[128,256]{1,0:T(8,128)(2,1)S(1)} %get-tuple-element.78), channel_id=1, source_target_pairs={{0,6},{1,7},{2,4},{3,5},{4,2},{5,3},{6,0},{7,1},{8,14},{9,15},{10,... | collective-permute-start | bytes 196616 | tf_op jit(solution)/shard_map/ppermute | solution.py:254
  68.2 1.9 %shard_map.86 = bf16[128,2048]{1,0:T(8,128)(2,1)} custom-call(bf16[128,512]{1,0:T(8,128)(2,1)} %get-tuple-element.68.refs_0_, bf16[128,512]{1,0:T(8,128)(2,1)} %copy-done.2, bf16[128,512]{1,0:T(8,128)(2,1)} %copy-done.3, bf16[128,512]{1,0:T(8,128)(2,1)} %copy-done.4), custom_call_target="tpu_custom_call" | custom-call | bytes 1048576 | tf_op jit(solution)/shard_map/pallas_call | solution.py:27
  71.7 1.7 %shard_map.87 = (bf16[128,512]{1,0:T(8,128)(2,1)}, bf16[128,512]{1,0:T(8,128)(2,1)}) custom-call(bf16[128,256]{1,0:T(8,128)(2,1)} %get-tuple-element.72.refs_0_, bf16[128,256]{1,0:T(8,128)(2,1)} %copy-done.5, bf16[128,256]{1,0:T(8,128)(2,1)} %copy-done.6, bf16[128,256]{1,0:T(8,128)(2,1)} %copy-done.7), custom_call_target="tpu_custom_call" | custom-call | bytes 524288 | tf_op jit(solution)/shard_map/pallas_call | solution.py:27
  (77 shorter events, 10.3 us)
Async XLA Ops:
  3.3 5.6 %collective-permute-start = (bf16[128,256]{1,0:T(8,128)(2,1)}, bf16[128,256]{1,0:T(8,128)(2,1)S(1)}, u32[]{:S(2)}, u32[]{:S(2)}) collective-permute-start(bf16[128,256]{1,0:T(8,128)(2,1)} %get-tuple-element.42), channel_id=1, source_target_pairs={{0,2},{1,3},{2,0},{3,1},{4,6},{5,7},{6,4},{7,5},{8,10},{9,11},{10,... | collective-permute-start | bytes 196616 | tf_op jit(solution)/shard_map/ppermute | solution.py:254
  6.2 4.5 %collective-permute-start.1 = (bf16[128,256]{1,0:T(8,128)(2,1)}, bf16[128,256]{1,0:T(8,128)(2,1)S(1)}, u32[]{:S(2)}, u32[]{:S(2)}) collective-permute-start(bf16[128,256]{1,0:T(8,128)(2,1)} %get-tuple-element.43), channel_id=1, source_target_pairs={{0,4},{1,5},{2,6},{3,7},{4,0},{5,1},{6,2},{7,3},{8,12},{9,13},{10,... | collective-permute-start | bytes 196616 | tf_op jit(solution)/shard_map/ppermute | solution.py:254
  7.7 5.4 %collective-permute-start.2 = (bf16[128,256]{1,0:T(8,128)(2,1)}, bf16[128,256]{1,0:T(8,128)(2,1)S(1)}, u32[]{:S(2)}, u32[]{:S(2)}) collective-permute-start(bf16[128,256]{1,0:T(8,128)(2,1)} %get-tuple-element.44), channel_id=1, source_target_pairs={{0,6},{1,7},{2,4},{3,5},{4,2},{5,3},{6,0},{7,1},{8,14},{9,15},{10,... | collective-permute-start | bytes 196616 | tf_op jit(solution)/shard_map/ppermute | solution.py:254
  13.1 5.6 %copy-start.9 = (bf16[1024,128]{1,0:T(8,128)(2,1)S(1)}, bf16[1024,128]{1,0:T(8,128)(2,1)}, u32[]{:S(2)}) copy-start(bf16[1024,128]{1,0:T(8,128)(2,1)} %get-tuple-element.54) | copy-start | bytes 786436
  14.0 16.0 %copy-start.1 = (bf16[4,128,256]{2,1,0:T(8,128)(2,1)}, bf16[4,128,256]{2,1,0:T(8,128)(2,1)S(1)}, u32[]{:S(2)}) copy-start(bf16[4,128,256]{2,1,0:T(8,128)(2,1)S(1)} %pad_maximum_fusion.refs_0_) | copy-start | bytes 786436
  14.0 7.4 %collective-permute-start.3 = (bf16[4,128,256]{2,1,0:T(8,128)(2,1)S(1)}, bf16[4,128,256]{2,1,0:T(8,128)(2,1)S(1)}, u32[]{:S(2)}, u32[]{:S(2)}) collective-permute-start(bf16[4,128,256]{2,1,0:T(8,128)(2,1)S(1)} %pad_maximum_fusion.refs_0_), channel_id=1, source_target_pairs={{0,8},{1,9},{2,10},{3,11},{4,12},{5,13},{6,14},{7,15},{8,16},{9,17... | collective-permute-start | bytes 786440 | tf_op jit(solution)/shard_map/ppermute | solution.py:251
  17.6 9.1 %collective-permute-start.7 = (bf16[1024,128]{1,0:T(8,128)(2,1)}, bf16[1024,128]{1,0:T(8,128)(2,1)S(1)}, u32[]{:S(2)}, u32[]{:S(2)}) collective-permute-start(bf16[1024,128]{1,0:T(8,128)(2,1)} %get-tuple-element.52), channel_id=1, source_target_pairs={{0,2},{1,3},{2,0},{3,1},{4,6},{5,7},{6,4},{7,5},{8,10},{9,11},{10,... | collective-permute-start | bytes 786440 | tf_op jit(solution)/shard_map/ppermute | solution.py:254
  18.2 11.8 %collective-permute-start.8 = (bf16[1024,128]{1,0:T(8,128)(2,1)S(1)}, bf16[1024,128]{1,0:T(8,128)(2,1)S(1)}, u32[]{:S(2)}, u32[]{:S(2)}) collective-permute-start(bf16[1024,128]{1,0:T(8,128)(2,1)S(1)} %copy-done.10), channel_id=1, source_target_pairs={{0,4},{1,5},{2,6},{3,7},{4,0},{5,1},{6,2},{7,3},{8,12},{9,13},{10,... | collective-permute-start | bytes 786440 | tf_op jit(solution)/shard_map/ppermute | solution.py:254
  18.7 11.3 %collective-permute-start.9 = (bf16[1024,128]{1,0:T(8,128)(2,1)S(1)}, bf16[1024,128]{1,0:T(8,128)(2,1)S(1)}, u32[]{:S(2)}, u32[]{:S(2)}) collective-permute-start(bf16[1024,128]{1,0:T(8,128)(2,1)S(1)} %copy-done.9), channel_id=1, source_target_pairs={{0,6},{1,7},{2,4},{3,5},{4,2},{5,3},{6,0},{7,1},{8,14},{9,15},{10,... | collective-permute-start | bytes 786440 | tf_op jit(solution)/shard_map/ppermute | solution.py:254
  21.4 8.6 %copy-start.11 = (bf16[4,128,256]{2,1,0:T(8,128)(2,1)}, bf16[4,128,256]{2,1,0:T(8,128)(2,1)S(1)}, u32[]{:S(2)}) copy-start(bf16[4,128,256]{2,1,0:T(8,128)(2,1)S(1)} %collective-permute-done.3.refs_2_) | copy-start | bytes 786436
  21.4 8.6 %collective-permute-start.4 = (bf16[4,128,256]{2,1,0:T(8,128)(2,1)S(1)}, bf16[4,128,256]{2,1,0:T(8,128)(2,1)S(1)}, u32[]{:S(2)}, u32[]{:S(2)}) collective-permute-start(bf16[4,128,256]{2,1,0:T(8,128)(2,1)S(1)} %pad_maximum_fusion.refs_0_), channel_id=1, source_target_pairs={{0,1},{1,0},{2,3},{3,2},{4,5},{5,4},{6,7},{7,6},{8,9},{9,8},{10,11... | collective-permute-start | bytes 786440 | tf_op jit(solution)/shard_map/ppermute | solution.py:254
  21.4 8.6 %collective-permute-start.5 = (bf16[4,128,256]{2,1,0:T(8,128)(2,1)S(1)}, bf16[4,128,256]{2,1,0:T(8,128)(2,1)S(1)}, u32[]{:S(2)}, u32[]{:S(2)}) collective-permute-start(bf16[4,128,256]{2,1,0:T(8,128)(2,1)S(1)} %collective-permute-done.3.refs_2_), channel_id=1, source_target_pairs={{0,1},{1,0},{2,3},{3,2},{4,5},{5,4},{6,7},{7,6},{8,9},{9,8},{10,11... | collective-permute-start | bytes 786440 | tf_op jit(solution)/shard_map/ppermute | solution.py:254
  26.7 3.3 %collective-permute-start.6 = (bf16[16,128]{1,0:T(8,128)(2,1)S(1)}, bf16[16,128]{1,0:T(8,128)(2,1)S(1)}, u32[]{:S(2)}, u32[]{:S(2)}) collective-permute-start(bf16[16,128]{1,0:T(8,128)(2,1)S(1)} %slice.63), channel_id=1, source_target_pairs={{1,16},{3,18},{5,20},{7,22},{9,24},{11,26},{13,28},{15,30}} | collective-permute-start | bytes 12296 | tf_op jit(solution)/shard_map/ppermute | solution.py:251
  43.7 3.6 %collective-permute-start.10 = (bf16[1040,256]{1,0:T(8,128)(2,1)}, bf16[1040,256]{1,0:T(8,128)(2,1)S(1)}, u32[]{:S(2)}, u32[]{:S(2)}) collective-permute-start(bf16[1040,256]{1,0:T(8,128)(2,1)} %get-tuple-element.60), channel_id=1, source_target_pairs={{0,1},{1,0},{2,3},{3,2},{4,5},{5,4},{6,7},{7,6},{8,9},{9,8},{10,11... | collective-permute-start | bytes 1597448 | tf_op jit(solution)/shard_map/ppermute | solution.py:254
  48.0 9.6 %collective-permute-start.15 = (f32[24,128]{1,0:T(8,128)S(1)}, f32[24,128]{1,0:T(8,128)S(1)}, u32[]{:S(2)}, u32[]{:S(2)}) collective-permute-start(f32[24,128]{1,0:T(8,128)S(1)} %select_maximum_fusion), channel_id=1, source_target_pairs={{0,16},{1,17},{2,18},{3,19},{4,20},{5,21},{6,22},{7,23},{8,24},{9,... | collective-permute-start | bytes 36872 | tf_op jit(solution)/shard_map/ppermute | solution.py:254
  51.5 11.3 %copy-start = (f32[512,256]{1,0:T(8,128)S(1)}, f32[512,256]{1,0:T(8,128)}, u32[]{:S(2)}) copy-start(f32[512,256]{1,0:T(8,128)} %get-tuple-element.66) | copy-start | bytes 1572868
  52.7 10.1 %collective-permute-start.14 = (bf16[512,256]{1,0:T(8,128)(2,1)S(1)}, bf16[512,256]{1,0:T(8,128)(2,1)S(1)}, u32[]{:S(2)}, u32[]{:S(2)}) collective-permute-start(bf16[512,256]{1,0:T(8,128)(2,1)S(1)} %add_convert_fusion), channel_id=1, source_target_pairs={{8,0},{9,1},{10,2},{11,3},{12,4},{13,5},{14,6},{15,7},{16,8},{17,9... | collective-permute-start | bytes 786440 | tf_op jit(solution)/shard_map/ppermute | solution.py:251
  54.0 6.3 %collective-permute-start.11 = (bf16[128,512]{1,0:T(8,128)(2,1)S(1)}, bf16[128,512]{1,0:T(8,128)(2,1)S(1)}, u32[]{:S(2)}, u32[]{:S(2)}) collective-permute-start(bf16[128,512]{1,0:T(8,128)(2,1)S(1)} %copy-done.19), channel_id=1, source_target_pairs={{0,2},{1,3},{2,0},{3,1},{4,6},{5,7},{6,4},{7,5},{8,10},{9,11},{10,... | collective-permute-start | bytes 393224 | tf_op jit(solution)/shard_map/ppermute | solution.py:254
  55.0 7.8 %collective-permute-start.12 = (bf16[128,512]{1,0:T(8,128)(2,1)S(1)}, bf16[128,512]{1,0:T(8,128)(2,1)S(1)}, u32[]{:S(2)}, u32[]{:S(2)}) collective-permute-start(bf16[128,512]{1,0:T(8,128)(2,1)S(1)} %copy-done.18), channel_id=1, source_target_pairs={{0,4},{1,5},{2,6},{3,7},{4,0},{5,1},{6,2},{7,3},{8,12},{9,13},{10,... | collective-permute-start | bytes 393224 | tf_op jit(solution)/shard_map/ppermute | solution.py:254
  55.5 7.3 %collective-permute-start.13 = (bf16[128,512]{1,0:T(8,128)(2,1)S(1)}, bf16[128,512]{1,0:T(8,128)(2,1)S(1)}, u32[]{:S(2)}, u32[]{:S(2)}) collective-permute-start(bf16[128,512]{1,0:T(8,128)(2,1)S(1)} %copy-done.17), channel_id=1, source_target_pairs={{0,6},{1,7},{2,4},{3,5},{4,2},{5,3},{6,0},{7,1},{8,14},{9,15},{10,... | collective-permute-start | bytes 393224 | tf_op jit(solution)/shard_map/ppermute | solution.py:254
  57.6 10.0 %collective-permute-start.19 = (f32[64]{0:T(128)S(1)}, f32[64]{0:T(128)S(1)}, u32[]{:S(2)}, u32[]{:S(2)}) collective-permute-start(f32[64]{0:T(128)S(1)} %fusion.11), channel_id=1, source_target_pairs={{0,8},{1,9},{2,10},{3,11},{4,12},{5,13},{6,14},{7,15},{8,0},{9,1},... | collective-permute-start | bytes 776 | tf_op jit(solution)/shard_map/ppermute | solution.py:254
  64.2 5.9 %collective-permute-start.16 = (bf16[128,256]{1,0:T(8,128)(2,1)S(1)}, bf16[128,256]{1,0:T(8,128)(2,1)S(1)}, u32[]{:S(2)}, u32[]{:S(2)}) collective-permute-start(bf16[128,256]{1,0:T(8,128)(2,1)S(1)} %get-tuple-element.79), channel_id=1, source_target_pairs={{0,2},{1,3},{2,0},{3,1},{4,6},{5,7},{6,4},{7,5},{8,10},{9,11},{10,... | collective-permute-start | bytes 196616 | tf_op jit(solution)/shard_map/ppermute | solution.py:254
  65.3 4.8 %collective-permute-start.17 = (bf16[128,256]{1,0:T(8,128)(2,1)S(1)}, bf16[128,256]{1,0:T(8,128)(2,1)S(1)}, u32[]{:S(2)}, u32[]{:S(2)}) collective-permute-start(bf16[128,256]{1,0:T(8,128)(2,1)S(1)} %get-tuple-element.80), channel_id=1, source_target_pairs={{0,4},{1,5},{2,6},{3,7},{4,0},{5,1},{6,2},{7,3},{8,12},{9,13},{10,... | collective-permute-start | bytes 196616 | tf_op jit(solution)/shard_map/ppermute | solution.py:254
  65.9 5.2 %collective-permute-start.18 = (bf16[128,256]{1,0:T(8,128)(2,1)S(1)}, bf16[128,256]{1,0:T(8,128)(2,1)S(1)}, u32[]{:S(2)}, u32[]{:S(2)}) collective-permute-start(bf16[128,256]{1,0:T(8,128)(2,1)S(1)} %get-tuple-element.78), channel_id=1, source_target_pairs={{0,6},{1,7},{2,4},{3,5},{4,2},{5,3},{6,0},{7,1},{8,14},{9,15},{10,... | collective-permute-start | bytes 196616 | tf_op jit(solution)/shard_map/ppermute | solution.py:254
  (17 other events, 29.3 us)

commit v5 on v4

--- a/solution.py
+++ b/solution.py
@@ -12,7 +12,7 @@
 WINDOW = 1024
 NEG_FILL = -1e30
 HALO = 16
-VMEM_BYTES = 56 * 1024 * 1024
+VMEM_BYTES = 18 * 1024 * 1024
 NT = (((1,), (1,)), ((), ()))
 
 
@@ -21,13 +21,15 @@
     return lax.div(device, group), lax.rem(device, share), lax.div(lax.rem(device, group), share)
 
 
-def run(kernel, out_shape, operands, scratch=(), flops=0):
+def run(kernel, out_shape, operands, scratch=(), flops=0, held=True, made=True):
     vmem = pl.BlockSpec(memory_space=pltpu.VMEM)
+    home = pltpu.VMEM if held else pltpu.HBM
     moved = list(operands) + list(out_shape)
+    operands = [pltpu.with_memory_space_constraint(a, home) for a in operands]
     return pl.pallas_call(
         kernel,
-        out_shape=out_shape,
-        in_specs=[vmem] * len(operands),
+        out_shape=[pltpu.VMEM(a.shape, a.dtype) for a in out_shape] if made else out_shape,
+        in_specs=[pl.BlockSpec(memory_space=home)] * len(operands),
         out_specs=[vmem] * len(out_shape),
         scratch_shapes=list(scratch),
         cost_estimate=pl.CostEstimate(
@@ -41,35 +43,36 @@
     return pl.ds(pl.multiple_of(index * width, HEAD_SIZE), width)
 
 
-def pack_kernel(place, queries, grad_out, keys, values, *parts):
+def pack_kernel(place, queries, grad_out, keys, values, *refs):
+    *parts, sems = refs
     rows = queries.shape[0]
     turns = len(parts) // 2
     heads = queries.shape[1] // HEAD_SIZE // turns
+    moves = []
     for turn in range(turns):
         target = place[2] ^ turn
-        part = parts[turn]
-        part[:, :HEAD_SIZE] = keys[:, columns_of(target)]
-        part[:, HEAD_SIZE:] = values[:, columns_of(target)]
-        part = parts[turns + turn]
+        moves.append((keys, target, parts[turn].at[:, :HEAD_SIZE]))
+        moves.append((values, target, parts[turn].at[:, HEAD_SIZE:]))
+    for turn in range(turns):
+        target = place[2] ^ turn
         for base, source in ((0, queries), (heads, grad_out)):
             for head in range(heads):
-                at = slice((base + head) * rows, (base + head + 1) * rows)
-                part[at] = source[:, columns_of(target * heads + head)]
+                at = pl.ds((base + head) * rows, rows)
+                moves.append((source, target * heads + head, parts[turns + turn].at[at]))
+    copies = [
+        pltpu.make_async_copy(source.at[:, columns_of(column)], target, sems.at[n])
+        for n, (source, column, target) in enumerate(moves)
+    ]
+    for copy in copies:
+        copy.start()
+    for copy in copies:
+        copy.wait()
 
 
 def unpack_queries_kernel(place, *refs):
     parts, grad_queries = refs[:-1], refs[-1]
     for turn, part in enumerate(parts):
         grad_queries[:, columns_of(place[2] ^ turn, part.shape[1])] = part[...]
-
-
-def unpack_kernel(place, *refs):
-    parts, (grad_keys, grad_values) = refs[:-2], refs[-2:]
-    head_at = place[2]
-    for turn, part in enumerate(parts):
-        at = columns_of(head_at ^ turn)
-        grad_keys[:, at] = part[:, :HEAD_SIZE]
-        grad_values[:, at] = part[:, HEAD_SIZE:]
 
 
 def attend_kernel(scale, turns, place, *refs):
@@ -265,6 +268,8 @@
         pack_kernel,
         [kv_shape] * kv_heads + [query_shape] * kv_heads,
         (queries[0], grad_out[0], keys[0], values[0]),
+        scratch=[pltpu.SemaphoreType.DMA((2 * kv_heads * (1 + own_width // HEAD_SIZE),))],
+        held=False,
     )
     kv_same = jnp.stack(exchanged(parts[:kv_heads]))
     old_same = routed(kv_same, group)
@@ -277,17 +282,18 @@
     halo = routed(last[rows - HALO :, HEAD_SIZE:], reach, lambda i: i % share == share - 1)
     lanes = 2 * HEAD_SIZE
     group_rows = kv_heads * rows
+    operands = (kv_same, kv_other, old_same, old_other, halo, conv_taps, *query_grads)
+    results = [shape((rows, own_width), bf16)] * kv_heads + [
+        shape((2 * group_rows + HALO, lanes), bf16),
+        shape((group_rows, lanes), bf16),
+        shape((group_rows, lanes), bf16),
+        shape((tap_count, HEAD_SIZE // 2), f32),
+    ]
     scale = 1.0 / math.sqrt(rows * count * lax.axis_size("rep"))
     *grad_q, send, keep_old, keep_own, tap_keep = launch(
         functools.partial(attend_kernel, scale, kv_heads),
-        [shape((rows, own_width), bf16)] * kv_heads
-        + [
-            shape((2 * group_rows + HALO, lanes), bf16),
-            shape((group_rows, lanes), f32),
-            shape((group_rows, lanes), f32),
-            shape((tap_count, HEAD_SIZE // 2), f32),
-        ],
-        (kv_same, kv_other, old_same, old_other, halo, conv_taps, *query_grads),
+        results,
+        operands,
         scratch=[
             pltpu.VMEM((2 * WINDOW, HEAD_SIZE), bf16),
             pltpu.VMEM((HEAD_SIZE, 2 * WINDOW), bf16),
@@ -302,8 +308,8 @@
     )
     got = flipped(send, 1)
     note = got[2 * group_rows :].astype(f32)
-    old_sum = (keep_old + got[:group_rows].astype(f32)).astype(bf16)
-    grad_q = after([old_sum], *grad_q)
+    old_sum = (keep_old.astype(f32) + got[:group_rows].astype(f32)).astype(bf16)
+    note, *grad_q = after([old_sum], note, *grad_q)
     returned = routed(old_sum, -group)
     grad_q = exchanged(grad_q)
     halo, tap_grads = note[:, HEAD_SIZE:], note[:, : HEAD_SIZE // 2]
@@ -319,7 +325,7 @@
     else:
         returned_halo = routed(halo, -2 * group)
     (keep_own,) = after(grad_q, keep_own)
-    total = keep_own + got[group_rows : 2 * group_rows].astype(f32) + returned.astype(f32)
+    total = keep_own.astype(f32) + got[group_rows : 2 * group_rows].astype(f32) + returned.astype(f32)
     halo_block = jnp.pad(returned_halo, ((rows - HALO, 0), (HEAD_SIZE, 0)))
     owned = []
     for turn in range(kv_heads):
@@ -327,11 +333,19 @@
         owned.append((mine + jnp.where((head_at ^ turn) == kv_heads - 1, halo_block, 0.0)).astype(bf16))
     grad_q = after(owned, *grad_q)
     owned = exchanged(owned)
-    (grad_queries,) = launch(unpack_queries_kernel, [shape((rows, width), bf16)], tuple(grad_q))
-    owned = after([grad_queries], *owned)
-    grad_keys, grad_values = launch(
-        unpack_kernel, [shape((rows, kv_width), bf16), shape((rows, kv_width), bf16)], tuple(owned)
-    )
+    (grad_queries,) = launch(unpack_queries_kernel, [shape((rows, width), bf16)], tuple(grad_q), made=False)
+
+    def in_order(parts):
+        heads = []
+        for head in range(kv_heads):
+            chosen = parts[0]
+            for turn in range(1, kv_heads):
+                chosen = jnp.where((head_at ^ turn) == head, parts[turn], chosen)
+            heads.append(chosen)
+        return jnp.concatenate(heads, axis=1)
+
+    grad_keys = in_order([part[:, :HEAD_SIZE] for part in owned])
+    grad_values = in_order([part[:, HEAD_SIZE:] for part in owned])
     if short:
         low, high = tap_grads[0], tap_grads[1]
         even = plane % 2 == 0

time: 73.7 us -> 63.3 us (0.86)
  Pallas kernels: 18.4 us -> 12 us
  local copies, waits for them, and re-layouts: 3.46 us -> 0.67 us
  other arithmetic: 3.4 us -> 1.57 us
    pallas_call x4 -> x3, Pallas kernels: 18.4 us -> 12 us  [run(): pl.pallas_call(kernel, out_shape=[pltpu.VMEM(a.shape, a.dtype) for a in o...]
    unnamed x42 -> x6, local copies, waits for them, and re-layouts: 3.45 us -> 0.66 us
    convert_element_type x1, other arithmetic: 1.18 us -> 0.07 us  [on_device(): old_sum = (keep_old.astype(f32) + got[:group_rows].astype(f32)).astype(bf16)]
    another operation x1, other arithmetic: 0.93 us -> 0.04 us  [on_device(): kv_same = jnp.stack(exchanged(parts[:kv_heads]))]
  transfers between devices with their start and end apart: 20 -> 20, of which waited for: 9 -> 12; matrix products, arithmetic and copies ran while one was open for 3% -> 1% of each run, Pallas kernels for 3% -> 1%
where the time goes in v5:
time: 63.3 us; the launch traced here: 63 us
  starting transfers between devices  29.2 us (46%)
  waiting for transfers between devices  18.8 us (30%)
  Pallas kernels  12 us (19%)
  other arithmetic  1.57 us (2%)
  between operations  0.81 us (1%)
  local copies, waits for them, and re-layouts  0.67 us (1%)
    ppermute x17, starting transfers between devices, flipped(): return lax.ppermute(array, 'seq', [(i, i ^ bits) for i in range(count)])  23.8 us
    ppermute x17, waiting for transfers between devices, flipped(): return lax.ppermute(array, 'seq', [(i, i ^ bits) for i in range(count)])  18.5 us
    pallas_call x3, Pallas kernels, run(): pl.pallas_call(kernel, out_shape=[pltpu.VMEM(a.shape, a.dtype) for a in o...  12 us
    ppermute x3, starting transfers between devices, routed(): return lax.ppermute(array, 'seq', route)  5.43 us
  transfers between devices with their start and end apart: 20, of which 12 were waited for; matrix products, arithmetic and copies ran while one was open for 1% of the time, Pallas kernels for 1%

profile of v5, /device:TPU:0, one launch (start us, length us, event | category | flops | bytes accessed | tf_op | source)
XLA Modules:
  0.0 63.0 jit_solution(3784371486520684929)
XLA Ops:
  0.6 1.6 %shard_map.84 = (bf16[128,256]{1,0:T(8,128)(2,1)S(1)}, bf16[128,256]{1,0:T(8,128)(2,1)S(1)}, bf16[128,256]{1,0:T(8,128)(2,1)S(1)}, bf16[128,256]{1,0:T(8,128)(2,...) custom-call(bf16[128,2048]{1,0:T(8,128)(2,1)} %bitcast.22, ...), custom_call_target="tpu_custom_call" | custom-call | bytes 2621440 | tf_op jit(solution)/shard_map/pallas_call | solution.py:29
  2.3 3.0 %collective-permute-start = (bf16[128,256]{1,0:T(8,128)(2,1)S(1)}, bf16[128,256]{1,0:T(8,128)(2,1)S(1)}, u32[]{:S(2)}, u32[]{:S(2)}) collective-permute-start(bf16[128,256]{1,0:T(8,128)(2,1)S(1)} %get-tuple-element.37), channel_id=1, source_target_pairs={{0,2},{1,3},{2,0},{3,1},{4,6},{5,7},{6,4},{7,5},{8,10},{9,11},{10,... | collective-permute-start | bytes 196616 | tf_op jit(solution)/shard_map/ppermute | solution.py:257
  5.3 1.5 %collective-permute-start.1 = (bf16[128,256]{1,0:T(8,128)(2,1)S(1)}, bf16[128,256]{1,0:T(8,128)(2,1)S(1)}, u32[]{:S(2)}, u32[]{:S(2)}) collective-permute-start(bf16[128,256]{1,0:T(8,128)(2,1)S(1)} %get-tuple-element.38), channel_id=1, source_target_pairs={{0,4},{1,5},{2,6},{3,7},{4,0},{5,1},{6,2},{7,3},{8,12},{9,13},{10,... | collective-permute-start | bytes 196616 | tf_op jit(solution)/shard_map/ppermute | solution.py:257
  6.8 0.8 %collective-permute-done = bf16[128,256]{1,0:T(8,128)(2,1)S(1)} collective-permute-done((bf16[128,256]{1,0:T(8,128)(2,1)S(1)}, bf16[128,256]{1,0:T(8,128)(2,1)S(1)}, u32[]{:S(2)}, u32[]{:S(2)}) %collective-permute-start) | collective-permute-done | bytes 65568 | tf_op jit(solution)/shard_map/ppermute | solution.py:257
  7.6 1.9 %collective-permute-done.1 = bf16[128,256]{1,0:T(8,128)(2,1)S(1)} collective-permute-done((bf16[128,256]{1,0:T(8,128)(2,1)S(1)}, bf16[128,256]{1,0:T(8,128)(2,1)S(1)}, u32[]{:S(2)}, u32[]{:S(2)}) %collective-permute-start.1) | collective-permute-done | bytes 65568 | tf_op jit(solution)/shard_map/ppermute | solution.py:257
  9.6 2.4 %collective-permute-done.2 = bf16[128,256]{1,0:T(8,128)(2,1)S(1)} collective-permute-done((bf16[128,256]{1,0:T(8,128)(2,1)S(1)}, bf16[128,256]{1,0:T(8,128)(2,1)S(1)}, u32[]{:S(2)}, u32[]{:S(2)}) %collective-permute-start.2) | collective-permute-done | bytes 65568 | tf_op jit(solution)/shard_map/ppermute | solution.py:257
  12.0 3.5 %collective-permute-start.3 = (bf16[4,128,256]{2,1,0:T(8,128)(2,1)S(1)}, bf16[4,128,256]{2,1,0:T(8,128)(2,1)S(1)}, u32[]{:S(2)}, u32[]{:S(2)}) collective-permute-start(bf16[4,128,256]{2,1,0:T(8,128)(2,1)S(1)} %pad_maximum_fusion.refs_0_), channel_id=1, source_target_pairs={{0,8},{1,9},{2,10},{3,11},{4,12},{5,13},{6,14},{7,15},{8,16},{9,17... | collective-permute-start | bytes 786440 | tf_op jit(solution)/shard_map/ppermute | solution.py:254
  16.6 2.4 %collective-permute-start.9 = (bf16[1024,128]{1,0:T(8,128)(2,1)S(1)}, bf16[1024,128]{1,0:T(8,128)(2,1)S(1)}, u32[]{:S(2)}, u32[]{:S(2)}) collective-permute-start(bf16[1024,128]{1,0:T(8,128)(2,1)S(1)} %get-tuple-element.49), channel_id=1, source_target_pairs={{0,6},{1,7},{2,4},{3,5},{4,2},{5,3},{6,0},{7,1},{8,14},{9,15},{10,... | collective-permute-start | bytes 786440 | tf_op jit(solution)/shard_map/ppermute | solution.py:257
  19.9 4.5 %collective-permute-done.7.refs_7_ = bf16[1024,128]{1,0:T(8,128)(2,1)S(1)} collective-permute-done((bf16[1024,128]{1,0:T(8,128)(2,1)S(1)}, bf16[1024,128]{1,0:T(8,128)(2,1)S(1)}, u32[]{:S(2)}, u32[]{:S(2)}) %collective-permute-start.7) | collective-permute-done | bytes 262176 | tf_op jit(solution)/shard_map/ppermute | solution.py:257
  25.1 2.8 %collective-permute-done.8.refs_8_ = bf16[1024,128]{1,0:T(8,128)(2,1)S(1)} collective-permute-done((bf16[1024,128]{1,0:T(8,128)(2,1)S(1)}, bf16[1024,128]{1,0:T(8,128)(2,1)S(1)}, u32[]{:S(2)}, u32[]{:S(2)}) %collective-permute-start.8) | collective-permute-done | bytes 262176 | tf_op jit(solution)/shard_map/ppermute | solution.py:257
  27.9 9.5 %shard_map.85 = (bf16[128,512]{1,0:T(8,128)(2,1)S(1)}, bf16[128,512]{1,0:T(8,128)(2,1)S(1)}, bf16[128,512]{1,0:T(8,128)(2,1)S(1)}, bf16[128,512]{1,0:T(8,128)(2,...) custom-call(bf16[4,128,256]{2,1,0:T(8,128)(2,1)S(1)} %pad_maximum_fu, ...), custom_call_target="tpu_custom_call" | custom-call | flops 3019898880 | bytes 3691520 | tf_op jit(solution)/shard_map/pallas_call | solution.py:29
  38.1 1.9 %collective-permute-start.10 = (bf16[1040,256]{1,0:T(8,128)(2,1)S(1)}, bf16[1040,256]{1,0:T(8,128)(2,1)S(1)}, u32[]{:S(2)}, u32[]{:S(2)}) collective-permute-start(bf16[1040,256]{1,0:T(8,128)(2,1)S(1)} %get-tuple-element.50), channel_id=1, source_target_pairs={{0,1},{1,0},{2,3},{3,2},{4,5},{5,4},{6,7},{7,6},{8,9},{9,8},{10,11... | collective-permute-start | bytes 1597448 | tf_op jit(solution)/shard_map/ppermute | solution.py:257
  40.0 1.5 %collective-permute-done.10 = bf16[1040,256]{1,0:T(8,128)(2,1)S(1)} collective-permute-done((bf16[1040,256]{1,0:T(8,128)(2,1)S(1)}, bf16[1040,256]{1,0:T(8,128)(2,1)S(1)}, u32[]{:S(2)}, u32[]{:S(2)}) %collective-permute-start.10) | collective-permute-done | bytes 532512 | tf_op jit(solution)/shard_map/ppermute | solution.py:257
  41.7 3.4 %collective-permute-start.15 = (f32[24,128]{1,0:T(8,128)S(1)}, f32[24,128]{1,0:T(8,128)S(1)}, u32[]{:S(2)}, u32[]{:S(2)}) collective-permute-start(f32[24,128]{1,0:T(8,128)S(1)} %select_maximum_fusion), channel_id=1, source_target_pairs={{0,16},{1,17},{2,18},{3,19},{4,20},{5,21},{6,22},{7,23},{8,24},{9,... | collective-permute-start | bytes 36872 | tf_op jit(solution)/shard_map/ppermute | solution.py:257
  45.1 1.3 %collective-permute-start.14 = (bf16[512,256]{1,0:T(8,128)(2,1)S(1)}, bf16[512,256]{1,0:T(8,128)(2,1)S(1)}, u32[]{:S(2)}, u32[]{:S(2)}) collective-permute-start(bf16[512,256]{1,0:T(8,128)(2,1)S(1)} %add_convert_fusion), channel_id=1, source_target_pairs={{8,0},{9,1},{10,2},{11,3},{12,4},{13,5},{14,6},{15,7},{16,8},{17,9... | collective-permute-start | bytes 786440 | tf_op jit(solution)/shard_map/ppermute | solution.py:254
  46.4 1.0 %collective-permute-start.11 = (bf16[128,512]{1,0:T(8,128)(2,1)S(1)}, bf16[128,512]{1,0:T(8,128)(2,1)S(1)}, u32[]{:S(2)}, u32[]{:S(2)}) collective-permute-start(bf16[128,512]{1,0:T(8,128)(2,1)S(1)} %copy-done.1), channel_id=1, source_target_pairs={{0,2},{1,3},{2,0},{3,1},{4,6},{5,7},{6,4},{7,5},{8,10},{9,11},{10,... | collective-permute-start | bytes 393224 | tf_op jit(solution)/shard_map/ppermute | solution.py:257
  47.9 2.0 %collective-permute-start.13 = (bf16[128,512]{1,0:T(8,128)(2,1)S(1)}, bf16[128,512]{1,0:T(8,128)(2,1)S(1)}, u32[]{:S(2)}, u32[]{:S(2)}) collective-permute-start(bf16[128,512]{1,0:T(8,128)(2,1)S(1)} %get-tuple-element.59), channel_id=1, source_target_pairs={{0,6},{1,7},{2,4},{3,5},{4,2},{5,3},{6,0},{7,1},{8,14},{9,15},{10,... | collective-permute-start | bytes 393224 | tf_op jit(solution)/shard_map/ppermute | solution.py:257
  50.0 2.7 %collective-permute-start.19 = (f32[64]{0:T(128)S(1)}, f32[64]{0:T(128)S(1)}, u32[]{:S(2)}, u32[]{:S(2)}) collective-permute-start(f32[64]{0:T(128)S(1)} %fusion.10), channel_id=1, source_target_pairs={{0,8},{1,9},{2,10},{3,11},{4,12},{5,13},{6,14},{7,15},{8,0},{9,1},... | collective-permute-start | bytes 776 | tf_op jit(solution)/shard_map/ppermute | solution.py:257
  52.8 2.4 %collective-permute-done.12.refs_2_ = bf16[128,512]{1,0:T(8,128)(2,1)S(1)} collective-permute-done((bf16[128,512]{1,0:T(8,128)(2,1)S(1)}, bf16[128,512]{1,0:T(8,128)(2,1)S(1)}, u32[]{:S(2)}, u32[]{:S(2)}) %collective-permute-start.12) | collective-permute-done | bytes 131104 | tf_op jit(solution)/shard_map/ppermute | solution.py:257
  55.3 1.2 %collective-permute-start.16 = (bf16[128,256]{1,0:T(8,128)(2,1)S(1)}, bf16[128,256]{1,0:T(8,128)(2,1)S(1)}, u32[]{:S(2)}, u32[]{:S(2)}) collective-permute-start(bf16[128,256]{1,0:T(8,128)(2,1)S(1)} %get-tuple-element.68), channel_id=1, source_target_pairs={{0,6},{1,7},{2,4},{3,5},{4,2},{5,3},{6,0},{7,1},{8,14},{9,15},{10,... | collective-permute-start | bytes 196616 | tf_op jit(solution)/shard_map/ppermute | solution.py:257
  56.6 1.4 %collective-permute-start.17 = (bf16[128,256]{1,0:T(8,128)(2,1)S(1)}, bf16[128,256]{1,0:T(8,128)(2,1)S(1)}, u32[]{:S(2)}, u32[]{:S(2)}) collective-permute-start(bf16[128,256]{1,0:T(8,128)(2,1)S(1)} %get-tuple-element.70), channel_id=1, source_target_pairs={{0,4},{1,5},{2,6},{3,7},{4,0},{5,1},{6,2},{7,3},{8,12},{9,13},{10,... | collective-permute-start | bytes 196616 | tf_op jit(solution)/shard_map/ppermute | solution.py:257
  58.0 0.9 %collective-permute-start.18 = (bf16[128,256]{1,0:T(8,128)(2,1)S(1)}, bf16[128,256]{1,0:T(8,128)(2,1)S(1)}, u32[]{:S(2)}, u32[]{:S(2)}) collective-permute-start(bf16[128,256]{1,0:T(8,128)(2,1)S(1)} %get-tuple-element.69), channel_id=1, source_target_pairs={{0,2},{1,3},{2,0},{3,1},{4,6},{5,7},{6,4},{7,5},{8,10},{9,11},{10,... | collective-permute-start | bytes 196616 | tf_op jit(solution)/shard_map/ppermute | solution.py:257
  59.4 0.8 %shard_map.86 = bf16[128,2048]{1,0:T(8,128)(2,1)} custom-call(bf16[128,512]{1,0:T(8,128)(2,1)S(1)} %get-tuple-element.64.refs_0_, bf16[128,512]{1,0:T(8,128)(2,1)S(1)} %collective-permute-done.11.refs_1_, bf16[128,512]{1,0:T(8,128)(2,1)S(1)} %collective-permute-done.12.refs_2_, bf16[128,512]{1,0:T(8,128)(2,1)S(1)} %collective-permute-done.13.refs_3_), custom_call_target="tpu_custom_call" | custom-call | bytes 1048576 | tf_op jit(solution)/shard_map/pallas_call | solution.py:29
  61.3 0.9 %collective-permute-done.18 = bf16[128,256]{1,0:T(8,128)(2,1)S(1)} collective-permute-done((bf16[128,256]{1,0:T(8,128)(2,1)S(1)}, bf16[128,256]{1,0:T(8,128)(2,1)S(1)}, u32[]{:S(2)}, u32[]{:S(2)}) %collective-permute-start.18) | collective-permute-done | bytes 65568 | tf_op jit(solution)/shard_map/ppermute | solution.py:257
  (44 shorter events, 6.5 us)
Async XLA Ops:
  2.3 5.4 %collective-permute-start = (bf16[128,256]{1,0:T(8,128)(2,1)S(1)}, bf16[128,256]{1,0:T(8,128)(2,1)S(1)}, u32[]{:S(2)}, u32[]{:S(2)}) collective-permute-start(bf16[128,256]{1,0:T(8,128)(2,1)S(1)} %get-tuple-element.37), channel_id=1, source_target_pairs={{0,2},{1,3},{2,0},{3,1},{4,6},{5,7},{6,4},{7,5},{8,10},{9,11},{10,... | collective-permute-start | bytes 196616 | tf_op jit(solution)/shard_map/ppermute | solution.py:257
  5.3 4.3 %collective-permute-start.1 = (bf16[128,256]{1,0:T(8,128)(2,1)S(1)}, bf16[128,256]{1,0:T(8,128)(2,1)S(1)}, u32[]{:S(2)}, u32[]{:S(2)}) collective-permute-start(bf16[128,256]{1,0:T(8,128)(2,1)S(1)} %get-tuple-element.38), channel_id=1, source_target_pairs={{0,4},{1,5},{2,6},{3,7},{4,0},{5,1},{6,2},{7,3},{8,12},{9,13},{10,... | collective-permute-start | bytes 196616 | tf_op jit(solution)/shard_map/ppermute | solution.py:257
  6.8 5.2 %collective-permute-start.2 = (bf16[128,256]{1,0:T(8,128)(2,1)S(1)}, bf16[128,256]{1,0:T(8,128)(2,1)S(1)}, u32[]{:S(2)}, u32[]{:S(2)}) collective-permute-start(bf16[128,256]{1,0:T(8,128)(2,1)S(1)} %get-tuple-element.39), channel_id=1, source_target_pairs={{0,6},{1,7},{2,4},{3,5},{4,2},{5,3},{6,0},{7,1},{8,14},{9,15},{10,... | collective-permute-start | bytes 196616 | tf_op jit(solution)/shard_map/ppermute | solution.py:257
  12.0 7.4 %collective-permute-start.3 = (bf16[4,128,256]{2,1,0:T(8,128)(2,1)S(1)}, bf16[4,128,256]{2,1,0:T(8,128)(2,1)S(1)}, u32[]{:S(2)}, u32[]{:S(2)}) collective-permute-start(bf16[4,128,256]{2,1,0:T(8,128)(2,1)S(1)} %pad_maximum_fusion.refs_0_), channel_id=1, source_target_pairs={{0,8},{1,9},{2,10},{3,11},{4,12},{5,13},{6,14},{7,15},{8,16},{9,17... | collective-permute-start | bytes 786440 | tf_op jit(solution)/shard_map/ppermute | solution.py:254
  15.5 8.9 %collective-permute-start.7 = (bf16[1024,128]{1,0:T(8,128)(2,1)S(1)}, bf16[1024,128]{1,0:T(8,128)(2,1)S(1)}, u32[]{:S(2)}, u32[]{:S(2)}) collective-permute-start(bf16[1024,128]{1,0:T(8,128)(2,1)S(1)} %get-tuple-element.47), channel_id=1, source_target_pairs={{0,2},{1,3},{2,0},{3,1},{4,6},{5,7},{6,4},{7,5},{8,10},{9,11},{10,... | collective-permute-start | bytes 786440 | tf_op jit(solution)/shard_map/ppermute | solution.py:257
  16.1 11.8 %collective-permute-start.8 = (bf16[1024,128]{1,0:T(8,128)(2,1)S(1)}, bf16[1024,128]{1,0:T(8,128)(2,1)S(1)}, u32[]{:S(2)}, u32[]{:S(2)}) collective-permute-start(bf16[1024,128]{1,0:T(8,128)(2,1)S(1)} %get-tuple-element.48), channel_id=1, source_target_pairs={{0,4},{1,5},{2,6},{3,7},{4,0},{5,1},{6,2},{7,3},{8,12},{9,13},{10,... | collective-permute-start | bytes 786440 | tf_op jit(solution)/shard_map/ppermute | solution.py:257
  16.6 11.3 %collective-permute-start.9 = (bf16[1024,128]{1,0:T(8,128)(2,1)S(1)}, bf16[1024,128]{1,0:T(8,128)(2,1)S(1)}, u32[]{:S(2)}, u32[]{:S(2)}) collective-permute-start(bf16[1024,128]{1,0:T(8,128)(2,1)S(1)} %get-tuple-element.49), channel_id=1, source_target_pairs={{0,6},{1,7},{2,4},{3,5},{4,2},{5,3},{6,0},{7,1},{8,14},{9,15},{10,... | collective-permute-start | bytes 786440 | tf_op jit(solution)/shard_map/ppermute | solution.py:257
  19.4 8.5 %collective-permute-start.4 = (bf16[4,128,256]{2,1,0:T(8,128)(2,1)S(1)}, bf16[4,128,256]{2,1,0:T(8,128)(2,1)S(1)}, u32[]{:S(2)}, u32[]{:S(2)}) collective-permute-start(bf16[4,128,256]{2,1,0:T(8,128)(2,1)S(1)} %pad_maximum_fusion.refs_0_), channel_id=1, source_target_pairs={{0,1},{1,0},{2,3},{3,2},{4,5},{5,4},{6,7},{7,6},{8,9},{9,8},{10,11... | collective-permute-start | bytes 786440 | tf_op jit(solution)/shard_map/ppermute | solution.py:257
  19.4 8.5 %collective-permute-start.5 = (bf16[4,128,256]{2,1,0:T(8,128)(2,1)S(1)}, bf16[4,128,256]{2,1,0:T(8,128)(2,1)S(1)}, u32[]{:S(2)}, u32[]{:S(2)}) collective-permute-start(bf16[4,128,256]{2,1,0:T(8,128)(2,1)S(1)} %collective-permute-done.3.refs_2_), channel_id=1, source_target_pairs={{0,1},{1,0},{2,3},{3,2},{4,5},{5,4},{6,7},{7,6},{8,9},{9,8},{10,11... | collective-permute-start | bytes 786440 | tf_op jit(solution)/shard_map/ppermute | solution.py:257
  19.9 8.0 %copy-start.2 = (f32[4,512]{1,0:T(4,128)S(1)}, f32[4,512]{1,0:T(4,128)}, u32[]{:S(2)}) copy-start(f32[4,512]{1,0:T(4,128)} %refs_5_.1) | copy-start | bytes 24580
  24.5 3.5 %collective-permute-start.6 = (bf16[16,128]{1,0:T(8,128)(2,1)S(1)}, bf16[16,128]{1,0:T(8,128)(2,1)S(1)}, u32[]{:S(2)}, u32[]{:S(2)}) collective-permute-start(bf16[16,128]{1,0:T(8,128)(2,1)S(1)} %slice.95), channel_id=1, source_target_pairs={{1,16},{3,18},{5,20},{7,22},{9,24},{11,26},{13,28},{15,30}} | collective-permute-start | bytes 12296 | tf_op jit(solution)/shard_map/ppermute | solution.py:254
  37.4 0.7 %copy-start = (bf16[128,512]{1,0:T(8,128)(2,1)}, bf16[128,512]{1,0:T(8,128)(2,1)S(1)}, u32[]{:S(2)}) copy-start(bf16[128,512]{1,0:T(8,128)(2,1)S(1)} %get-tuple-element.57) | copy-start | bytes 393220
  38.1 3.4 %collective-permute-start.10 = (bf16[1040,256]{1,0:T(8,128)(2,1)S(1)}, bf16[1040,256]{1,0:T(8,128)(2,1)S(1)}, u32[]{:S(2)}, u32[]{:S(2)}) collective-permute-start(bf16[1040,256]{1,0:T(8,128)(2,1)S(1)} %get-tuple-element.50), channel_id=1, source_target_pairs={{0,1},{1,0},{2,3},{3,2},{4,5},{5,4},{6,7},{7,6},{8,9},{9,8},{10,11... | collective-permute-start | bytes 1597448 | tf_op jit(solution)/shard_map/ppermute | solution.py:257
  41.5 4.9 %copy-start.1 = (bf16[128,512]{1,0:T(8,128)(2,1)S(1)}, bf16[128,512]{1,0:T(8,128)(2,1)}, u32[]{:S(2)}) copy-start(bf16[128,512]{1,0:T(8,128)(2,1)} %copy-done) | copy-start | bytes 393220
  41.7 8.3 %collective-permute-start.15 = (f32[24,128]{1,0:T(8,128)S(1)}, f32[24,128]{1,0:T(8,128)S(1)}, u32[]{:S(2)}, u32[]{:S(2)}) collective-permute-start(f32[24,128]{1,0:T(8,128)S(1)} %select_maximum_fusion), channel_id=1, source_target_pairs={{0,16},{1,17},{2,18},{3,19},{4,20},{5,21},{6,22},{7,23},{8,24},{9,... | collective-permute-start | bytes 36872 | tf_op jit(solution)/shard_map/ppermute | solution.py:257
  45.1 10.1 %collective-permute-start.14 = (bf16[512,256]{1,0:T(8,128)(2,1)S(1)}, bf16[512,256]{1,0:T(8,128)(2,1)S(1)}, u32[]{:S(2)}, u32[]{:S(2)}) collective-permute-start(bf16[512,256]{1,0:T(8,128)(2,1)S(1)} %add_convert_fusion), channel_id=1, source_target_pairs={{8,0},{9,1},{10,2},{11,3},{12,4},{13,5},{14,6},{15,7},{16,8},{17,9... | collective-permute-start | bytes 786440 | tf_op jit(solution)/shard_map/ppermute | solution.py:254
  46.4 6.4 %collective-permute-start.11 = (bf16[128,512]{1,0:T(8,128)(2,1)S(1)}, bf16[128,512]{1,0:T(8,128)(2,1)S(1)}, u32[]{:S(2)}, u32[]{:S(2)}) collective-permute-start(bf16[128,512]{1,0:T(8,128)(2,1)S(1)} %copy-done.1), channel_id=1, source_target_pairs={{0,2},{1,3},{2,0},{3,1},{4,6},{5,7},{6,4},{7,5},{8,10},{9,11},{10,... | collective-permute-start | bytes 393224 | tf_op jit(solution)/shard_map/ppermute | solution.py:257
  47.4 7.8 %collective-permute-start.12 = (bf16[128,512]{1,0:T(8,128)(2,1)S(1)}, bf16[128,512]{1,0:T(8,128)(2,1)S(1)}, u32[]{:S(2)}, u32[]{:S(2)}) collective-permute-start(bf16[128,512]{1,0:T(8,128)(2,1)S(1)} %get-tuple-element.58), channel_id=1, source_target_pairs={{0,4},{1,5},{2,6},{3,7},{4,0},{5,1},{6,2},{7,3},{8,12},{9,13},{10,... | collective-permute-start | bytes 393224 | tf_op jit(solution)/shard_map/ppermute | solution.py:257
  47.9 7.3 %collective-permute-start.13 = (bf16[128,512]{1,0:T(8,128)(2,1)S(1)}, bf16[128,512]{1,0:T(8,128)(2,1)S(1)}, u32[]{:S(2)}, u32[]{:S(2)}) collective-permute-start(bf16[128,512]{1,0:T(8,128)(2,1)S(1)} %get-tuple-element.59), channel_id=1, source_target_pairs={{0,6},{1,7},{2,4},{3,5},{4,2},{5,3},{6,0},{7,1},{8,14},{9,15},{10,... | collective-permute-start | bytes 393224 | tf_op jit(solution)/shard_map/ppermute | solution.py:257
  50.0 8.9 %collective-permute-start.19 = (f32[64]{0:T(128)S(1)}, f32[64]{0:T(128)S(1)}, u32[]{:S(2)}, u32[]{:S(2)}) collective-permute-start(f32[64]{0:T(128)S(1)} %fusion.10), channel_id=1, source_target_pairs={{0,8},{1,9},{2,10},{3,11},{4,12},{5,13},{6,14},{7,15},{8,0},{9,1},... | collective-permute-start | bytes 776 | tf_op jit(solution)/shard_map/ppermute | solution.py:257
  55.3 5.4 %collective-permute-start.16 = (bf16[128,256]{1,0:T(8,128)(2,1)S(1)}, bf16[128,256]{1,0:T(8,128)(2,1)S(1)}, u32[]{:S(2)}, u32[]{:S(2)}) collective-permute-start(bf16[128,256]{1,0:T(8,128)(2,1)S(1)} %get-tuple-element.68), channel_id=1, source_target_pairs={{0,6},{1,7},{2,4},{3,5},{4,2},{5,3},{6,0},{7,1},{8,14},{9,15},{10,... | collective-permute-start | bytes 196616 | tf_op jit(solution)/shard_map/ppermute | solution.py:257
  56.6 4.8 %collective-permute-start.17 = (bf16[128,256]{1,0:T(8,128)(2,1)S(1)}, bf16[128,256]{1,0:T(8,128)(2,1)S(1)}, u32[]{:S(2)}, u32[]{:S(2)}) collective-permute-start(bf16[128,256]{1,0:T(8,128)(2,1)S(1)} %get-tuple-element.70), channel_id=1, source_target_pairs={{0,4},{1,5},{2,6},{3,7},{4,0},{5,1},{6,2},{7,3},{8,12},{9,13},{10,... | collective-permute-start | bytes 196616 | tf_op jit(solution)/shard_map/ppermute | solution.py:257
  58.0 4.3 %collective-permute-start.18 = (bf16[128,256]{1,0:T(8,128)(2,1)S(1)}, bf16[128,256]{1,0:T(8,128)(2,1)S(1)}, u32[]{:S(2)}, u32[]{:S(2)}) collective-permute-start(bf16[128,256]{1,0:T(8,128)(2,1)S(1)} %get-tuple-element.69), channel_id=1, source_target_pairs={{0,2},{1,3},{2,0},{3,1},{4,6},{5,7},{6,4},{7,5},{8,10},{9,11},{10,... | collective-permute-start | bytes 196616 | tf_op jit(solution)/shard_map/ppermute | solution.py:257

commit v6 on v5

--- a/solution.py
+++ b/solution.py
@@ -78,8 +78,8 @@
 def attend_kernel(scale, turns, place, *refs):
     kv_same, kv_other, old_same, old_other, halo, all_taps = refs[:6]
     query_grads = refs[6 : 6 + turns]
-    grad_qs = refs[6 + turns : 6 + 2 * turns]
-    send, keep_old, keep_own, tap_keep = refs[6 + 2 * turns : 10 + 2 * turns]
+    send, keep_old, keep_own, tap_keep = refs[6 + turns : 10 + turns]
+    grad_qs = refs[10 + turns : 10 + 2 * turns]
     key_all, key_t, value_all, mix_all, dkey, dmix, *work = refs[10 + 2 * turns :]
     rows, width = grad_qs[0].shape
     blocks = turns
@@ -283,14 +283,14 @@
     lanes = 2 * HEAD_SIZE
     group_rows = kv_heads * rows
     operands = (kv_same, kv_other, old_same, old_other, halo, conv_taps, *query_grads)
-    results = [shape((rows, own_width), bf16)] * kv_heads + [
+    results = [
         shape((2 * group_rows + HALO, lanes), bf16),
         shape((group_rows, lanes), bf16),
         shape((group_rows, lanes), bf16),
         shape((tap_count, HEAD_SIZE // 2), f32),
-    ]
+    ] + [shape((rows, own_width), bf16)] * kv_heads
     scale = 1.0 / math.sqrt(rows * count * lax.axis_size("rep"))
-    *grad_q, send, keep_old, keep_own, tap_keep = launch(
+    send, keep_old, keep_own, tap_keep, *grad_q = launch(
         functools.partial(attend_kernel, scale, kv_heads),
         results,
         operands,
@@ -324,7 +324,6 @@
         returned_halo = jnp.where(plane < 2, note[:HALO], 0.0)
     else:
         returned_halo = routed(halo, -2 * group)
-    (keep_own,) = after(grad_q, keep_own)
     total = keep_own.astype(f32) + got[group_rows : 2 * group_rows].astype(f32) + returned.astype(f32)
     halo_block = jnp.pad(returned_halo, ((rows - HALO, 0), (HEAD_SIZE, 0)))
     owned = []

time: 63.3 us -> 63 us (level)
    ppermute x17, waiting for transfers between devices: 18.5 us -> 15.9 us  [flipped(): return lax.ppermute(array, 'seq', [(i, i ^ bits) for i in range(count)])]
    ppermute x3, waiting for transfers between devices: 0.31 us -> 2.67 us  [routed(): return lax.ppermute(array, 'seq', route)]
  transfers between devices with their start and end apart: 20 -> 20, of which waited for: 12 -> 11; matrix products, arithmetic and copies ran while one was open for 1% -> 1% of each run, Pallas kernels for 1% -> 1%
where the time goes in v6:
time: 63 us; the launch traced here: 62.7 us
  starting transfers between devices  29.2 us (46%)
  waiting for transfers between devices  18.5 us (29%)
  Pallas kernels  12 us (19%)
  other arithmetic  1.57 us (2%)
  between operations  0.81 us (1%)
  local copies, waits for them, and re-layouts  0.67 us (1%)
    ppermute x17, starting transfers between devices, flipped(): return lax.ppermute(array, 'seq', [(i, i ^ bits) for i in range(count)])  23.8 us
    ppermute x17, waiting for transfers between devices, flipped(): return lax.ppermute(array, 'seq', [(i, i ^ bits) for i in range(count)])  15.9 us
    pallas_call x3, Pallas kernels, run(): pl.pallas_call(kernel, out_shape=[pltpu.VMEM(a.shape, a.dtype) for a in o...  12 us
    ppermute x3, starting transfers between devices, routed(): return lax.ppermute(array, 'seq', route)  5.43 us
    ppermute x3, waiting for transfers between devices, routed(): return lax.ppermute(array, 'seq', route)  2.67 us
  transfers between devices with their start and end apart: 20, of which 11 were waited for; matrix products, arithmetic and copies ran while one was open for 1% of the time, Pallas kernels for 1%

profile of v6, /device:TPU:0, one launch (start us, length us, event | category | flops | bytes accessed | tf_op | source)
XLA Modules:
  0.0 62.7 jit_solution(7427297814645388652)
XLA Ops:
  0.6 1.6 %shard_map.84 = (bf16[128,256]{1,0:T(8,128)(2,1)S(1)}, bf16[128,256]{1,0:T(8,128)(2,1)S(1)}, bf16[128,256]{1,0:T(8,128)(2,1)S(1)}, bf16[128,256]{1,0:T(8,128)(2,...) custom-call(bf16[128,2048]{1,0:T(8,128)(2,1)} %bitcast.22, ...), custom_call_target="tpu_custom_call" | custom-call | bytes 2621440 | tf_op jit(solution)/shard_map/pallas_call | solution.py:29
  2.3 3.0 %collective-permute-start = (bf16[128,256]{1,0:T(8,128)(2,1)S(1)}, bf16[128,256]{1,0:T(8,128)(2,1)S(1)}, u32[]{:S(2)}, u32[]{:S(2)}) collective-permute-start(bf16[128,256]{1,0:T(8,128)(2,1)S(1)} %get-tuple-element.36), channel_id=1, source_target_pairs={{0,2},{1,3},{2,0},{3,1},{4,6},{5,7},{6,4},{7,5},{8,10},{9,11},{10,... | collective-permute-start | bytes 196616 | tf_op jit(solution)/shard_map/ppermute | solution.py:257
  5.3 1.5 %collective-permute-start.1 = (bf16[128,256]{1,0:T(8,128)(2,1)S(1)}, bf16[128,256]{1,0:T(8,128)(2,1)S(1)}, u32[]{:S(2)}, u32[]{:S(2)}) collective-permute-start(bf16[128,256]{1,0:T(8,128)(2,1)S(1)} %get-tuple-element.37), channel_id=1, source_target_pairs={{0,4},{1,5},{2,6},{3,7},{4,0},{5,1},{6,2},{7,3},{8,12},{9,13},{10,... | collective-permute-start | bytes 196616 | tf_op jit(solution)/shard_map/ppermute | solution.py:257
  6.8 0.8 %collective-permute-done = bf16[128,256]{1,0:T(8,128)(2,1)S(1)} collective-permute-done((bf16[128,256]{1,0:T(8,128)(2,1)S(1)}, bf16[128,256]{1,0:T(8,128)(2,1)S(1)}, u32[]{:S(2)}, u32[]{:S(2)}) %collective-permute-start) | collective-permute-done | bytes 65568 | tf_op jit(solution)/shard_map/ppermute | solution.py:257
  7.6 1.9 %collective-permute-done.1 = bf16[128,256]{1,0:T(8,128)(2,1)S(1)} collective-permute-done((bf16[128,256]{1,0:T(8,128)(2,1)S(1)}, bf16[128,256]{1,0:T(8,128)(2,1)S(1)}, u32[]{:S(2)}, u32[]{:S(2)}) %collective-permute-start.1) | collective-permute-done | bytes 65568 | tf_op jit(solution)/shard_map/ppermute | solution.py:257
  9.6 2.4 %collective-permute-done.2 = bf16[128,256]{1,0:T(8,128)(2,1)S(1)} collective-permute-done((bf16[128,256]{1,0:T(8,128)(2,1)S(1)}, bf16[128,256]{1,0:T(8,128)(2,1)S(1)}, u32[]{:S(2)}, u32[]{:S(2)}) %collective-permute-start.2) | collective-permute-done | bytes 65568 | tf_op jit(solution)/shard_map/ppermute | solution.py:257
  12.0 3.5 %collective-permute-start.3 = (bf16[4,128,256]{2,1,0:T(8,128)(2,1)S(1)}, bf16[4,128,256]{2,1,0:T(8,128)(2,1)S(1)}, u32[]{:S(2)}, u32[]{:S(2)}) collective-permute-start(bf16[4,128,256]{2,1,0:T(8,128)(2,1)S(1)} %pad_maximum_fusion.refs_0_), channel_id=1, source_target_pairs={{0,8},{1,9},{2,10},{3,11},{4,12},{5,13},{6,14},{7,15},{8,16},{9,17... | collective-permute-start | bytes 786440 | tf_op jit(solution)/shard_map/ppermute | solution.py:254
  16.6 2.4 %collective-permute-start.9 = (bf16[1024,128]{1,0:T(8,128)(2,1)S(1)}, bf16[1024,128]{1,0:T(8,128)(2,1)S(1)}, u32[]{:S(2)}, u32[]{:S(2)}) collective-permute-start(bf16[1024,128]{1,0:T(8,128)(2,1)S(1)} %get-tuple-element.48), channel_id=1, source_target_pairs={{0,6},{1,7},{2,4},{3,5},{4,2},{5,3},{6,0},{7,1},{8,14},{9,15},{10,... | collective-permute-start | bytes 786440 | tf_op jit(solution)/shard_map/ppermute | solution.py:257
  19.9 4.5 %collective-permute-done.7.refs_7_ = bf16[1024,128]{1,0:T(8,128)(2,1)S(1)} collective-permute-done((bf16[1024,128]{1,0:T(8,128)(2,1)S(1)}, bf16[1024,128]{1,0:T(8,128)(2,1)S(1)}, u32[]{:S(2)}, u32[]{:S(2)}) %collective-permute-start.7) | collective-permute-done | bytes 262176 | tf_op jit(solution)/shard_map/ppermute | solution.py:257
  25.1 2.8 %collective-permute-done.8.refs_8_ = bf16[1024,128]{1,0:T(8,128)(2,1)S(1)} collective-permute-done((bf16[1024,128]{1,0:T(8,128)(2,1)S(1)}, bf16[1024,128]{1,0:T(8,128)(2,1)S(1)}, u32[]{:S(2)}, u32[]{:S(2)}) %collective-permute-start.8) | collective-permute-done | bytes 262176 | tf_op jit(solution)/shard_map/ppermute | solution.py:257
  27.9 9.5 %shard_map.85 = (bf16[1040,256]{1,0:T(8,128)(2,1)S(1)}, bf16[512,256]{1,0:T(8,128)(2,1)S(1)}, bf16[512,256]{1,0:T(8,128)(2,1)S(1)}, f32[4,64]{1,0:T(4,128)S(1)},...) custom-call(bf16[4,128,256]{2,1,0:T(8,128)(2,1)S(1)} %pad_maximum_fu, ...), custom_call_target="tpu_custom_call" | custom-call | flops 3019898880 | bytes 3691520 | tf_op jit(solution)/shard_map/pallas_call | solution.py:29
  38.1 1.9 %collective-permute-start.10 = (bf16[1040,256]{1,0:T(8,128)(2,1)S(1)}, bf16[1040,256]{1,0:T(8,128)(2,1)S(1)}, u32[]{:S(2)}, u32[]{:S(2)}) collective-permute-start(bf16[1040,256]{1,0:T(8,128)(2,1)S(1)} %get-tuple-element.49), channel_id=1, source_target_pairs={{0,1},{1,0},{2,3},{3,2},{4,5},{5,4},{6,7},{7,6},{8,9},{9,8},{10,11... | collective-permute-start | bytes 1597448 | tf_op jit(solution)/shard_map/ppermute | solution.py:257
  40.0 1.5 %collective-permute-done.10 = bf16[1040,256]{1,0:T(8,128)(2,1)S(1)} collective-permute-done((bf16[1040,256]{1,0:T(8,128)(2,1)S(1)}, bf16[1040,256]{1,0:T(8,128)(2,1)S(1)}, u32[]{:S(2)}, u32[]{:S(2)}) %collective-permute-start.10) | collective-permute-done | bytes 532512 | tf_op jit(solution)/shard_map/ppermute | solution.py:257
  41.7 3.4 %collective-permute-start.15 = (f32[24,128]{1,0:T(8,128)S(1)}, f32[24,128]{1,0:T(8,128)S(1)}, u32[]{:S(2)}, u32[]{:S(2)}) collective-permute-start(f32[24,128]{1,0:T(8,128)S(1)} %select_maximum_fusion), channel_id=1, source_target_pairs={{0,16},{1,17},{2,18},{3,19},{4,20},{5,21},{6,22},{7,23},{8,24},{9,... | collective-permute-start | bytes 36872 | tf_op jit(solution)/shard_map/ppermute | solution.py:257
  45.1 1.3 %collective-permute-start.14 = (bf16[512,256]{1,0:T(8,128)(2,1)S(1)}, bf16[512,256]{1,0:T(8,128)(2,1)S(1)}, u32[]{:S(2)}, u32[]{:S(2)}) collective-permute-start(bf16[512,256]{1,0:T(8,128)(2,1)S(1)} %add_convert_fusion), channel_id=1, source_target_pairs={{8,0},{9,1},{10,2},{11,3},{12,4},{13,5},{14,6},{15,7},{16,8},{17,9... | collective-permute-start | bytes 786440 | tf_op jit(solution)/shard_map/ppermute | solution.py:254
  46.4 1.0 %collective-permute-start.11 = (bf16[128,512]{1,0:T(8,128)(2,1)S(1)}, bf16[128,512]{1,0:T(8,128)(2,1)S(1)}, u32[]{:S(2)}, u32[]{:S(2)}) collective-permute-start(bf16[128,512]{1,0:T(8,128)(2,1)S(1)} %copy-done.1), channel_id=1, source_target_pairs={{0,2},{1,3},{2,0},{3,1},{4,6},{5,7},{6,4},{7,5},{8,10},{9,11},{10,... | collective-permute-start | bytes 393224 | tf_op jit(solution)/shard_map/ppermute | solution.py:257
  47.9 2.0 %collective-permute-start.13 = (bf16[128,512]{1,0:T(8,128)(2,1)S(1)}, bf16[128,512]{1,0:T(8,128)(2,1)S(1)}, u32[]{:S(2)}, u32[]{:S(2)}) collective-permute-start(bf16[128,512]{1,0:T(8,128)(2,1)S(1)} %get-tuple-element.58), channel_id=1, source_target_pairs={{0,6},{1,7},{2,4},{3,5},{4,2},{5,3},{6,0},{7,1},{8,14},{9,15},{10,... | collective-permute-start | bytes 393224 | tf_op jit(solution)/shard_map/ppermute | solution.py:257
  50.0 2.7 %collective-permute-start.19 = (f32[64]{0:T(128)S(1)}, f32[64]{0:T(128)S(1)}, u32[]{:S(2)}, u32[]{:S(2)}) collective-permute-start(f32[64]{0:T(128)S(1)} %fusion.10), channel_id=1, source_target_pairs={{0,8},{1,9},{2,10},{3,11},{4,12},{5,13},{6,14},{7,15},{8,0},{9,1},... | collective-permute-start | bytes 776 | tf_op jit(solution)/shard_map/ppermute | solution.py:257
  52.7 2.4 %collective-permute-done.14 = bf16[512,256]{1,0:T(8,128)(2,1)S(1)} collective-permute-done((bf16[512,256]{1,0:T(8,128)(2,1)S(1)}, bf16[512,256]{1,0:T(8,128)(2,1)S(1)}, u32[]{:S(2)}, u32[]{:S(2)}) %collective-permute-start.14) | collective-permute-done | bytes 262176 | tf_op jit(solution)/shard_map/ppermute | solution.py:254
  55.2 0.9 %collective-permute-start.16 = (bf16[128,256]{1,0:T(8,128)(2,1)S(1)}, bf16[128,256]{1,0:T(8,128)(2,1)S(1)}, u32[]{:S(2)}, u32[]{:S(2)}) collective-permute-start(bf16[128,256]{1,0:T(8,128)(2,1)S(1)} %get-tuple-element.66), channel_id=1, source_target_pairs={{0,6},{1,7},{2,4},{3,5},{4,2},{5,3},{6,0},{7,1},{8,14},{9,15},{10,... | collective-permute-start | bytes 196616 | tf_op jit(solution)/shard_map/ppermute | solution.py:257
  56.2 1.5 %collective-permute-start.17 = (bf16[128,256]{1,0:T(8,128)(2,1)S(1)}, bf16[128,256]{1,0:T(8,128)(2,1)S(1)}, u32[]{:S(2)}, u32[]{:S(2)}) collective-permute-start(bf16[128,256]{1,0:T(8,128)(2,1)S(1)} %get-tuple-element.68), channel_id=1, source_target_pairs={{0,4},{1,5},{2,6},{3,7},{4,0},{5,1},{6,2},{7,3},{8,12},{9,13},{10,... | collective-permute-start | bytes 196616 | tf_op jit(solution)/shard_map/ppermute | solution.py:257
  57.7 1.1 %collective-permute-start.18 = (bf16[128,256]{1,0:T(8,128)(2,1)S(1)}, bf16[128,256]{1,0:T(8,128)(2,1)S(1)}, u32[]{:S(2)}, u32[]{:S(2)}) collective-permute-start(bf16[128,256]{1,0:T(8,128)(2,1)S(1)} %get-tuple-element.67), channel_id=1, source_target_pairs={{0,2},{1,3},{2,0},{3,1},{4,6},{5,7},{6,4},{7,5},{8,10},{9,11},{10,... | collective-permute-start | bytes 196616 | tf_op jit(solution)/shard_map/ppermute | solution.py:257
  59.3 0.8 %shard_map.86 = bf16[128,2048]{1,0:T(8,128)(2,1)} custom-call(bf16[128,512]{1,0:T(8,128)(2,1)S(1)} %get-tuple-element.62.refs_0_, bf16[128,512]{1,0:T(8,128)(2,1)S(1)} %collective-permute-done.11.refs_1_, bf16[128,512]{1,0:T(8,128)(2,1)S(1)} %collective-permute-done.12.refs_2_, bf16[128,512]{1,0:T(8,128)(2,1)S(1)} %collective-permute-done.13.refs_3_), custom_call_target="tpu_custom_call" | custom-call | bytes 1048576 | tf_op jit(solution)/shard_map/pallas_call | solution.py:29
  61.1 0.8 %collective-permute-done.18 = bf16[128,256]{1,0:T(8,128)(2,1)S(1)} collective-permute-done((bf16[128,256]{1,0:T(8,128)(2,1)S(1)}, bf16[128,256]{1,0:T(8,128)(2,1)S(1)}, u32[]{:S(2)}, u32[]{:S(2)}) %collective-permute-start.18) | collective-permute-done | bytes 65568 | tf_op jit(solution)/shard_map/ppermute | solution.py:257
  (44 shorter events, 6.4 us)
Async XLA Ops:
  2.3 5.4 %collective-permute-start = (bf16[128,256]{1,0:T(8,128)(2,1)S(1)}, bf16[128,256]{1,0:T(8,128)(2,1)S(1)}, u32[]{:S(2)}, u32[]{:S(2)}) collective-permute-start(bf16[128,256]{1,0:T(8,128)(2,1)S(1)} %get-tuple-element.36), channel_id=1, source_target_pairs={{0,2},{1,3},{2,0},{3,1},{4,6},{5,7},{6,4},{7,5},{8,10},{9,11},{10,... | collective-permute-start | bytes 196616 | tf_op jit(solution)/shard_map/ppermute | solution.py:257
  5.3 4.3 %collective-permute-start.1 = (bf16[128,256]{1,0:T(8,128)(2,1)S(1)}, bf16[128,256]{1,0:T(8,128)(2,1)S(1)}, u32[]{:S(2)}, u32[]{:S(2)}) collective-permute-start(bf16[128,256]{1,0:T(8,128)(2,1)S(1)} %get-tuple-element.37), channel_id=1, source_target_pairs={{0,4},{1,5},{2,6},{3,7},{4,0},{5,1},{6,2},{7,3},{8,12},{9,13},{10,... | collective-permute-start | bytes 196616 | tf_op jit(solution)/shard_map/ppermute | solution.py:257
  6.8 5.2 %collective-permute-start.2 = (bf16[128,256]{1,0:T(8,128)(2,1)S(1)}, bf16[128,256]{1,0:T(8,128)(2,1)S(1)}, u32[]{:S(2)}, u32[]{:S(2)}) collective-permute-start(bf16[128,256]{1,0:T(8,128)(2,1)S(1)} %get-tuple-element.38), channel_id=1, source_target_pairs={{0,6},{1,7},{2,4},{3,5},{4,2},{5,3},{6,0},{7,1},{8,14},{9,15},{10,... | collective-permute-start | bytes 196616 | tf_op jit(solution)/shard_map/ppermute | solution.py:257
  12.0 7.4 %collective-permute-start.3 = (bf16[4,128,256]{2,1,0:T(8,128)(2,1)S(1)}, bf16[4,128,256]{2,1,0:T(8,128)(2,1)S(1)}, u32[]{:S(2)}, u32[]{:S(2)}) collective-permute-start(bf16[4,128,256]{2,1,0:T(8,128)(2,1)S(1)} %pad_maximum_fusion.refs_0_), channel_id=1, source_target_pairs={{0,8},{1,9},{2,10},{3,11},{4,12},{5,13},{6,14},{7,15},{8,16},{9,17... | collective-permute-start | bytes 786440 | tf_op jit(solution)/shard_map/ppermute | solution.py:254
  15.5 8.9 %collective-permute-start.7 = (bf16[1024,128]{1,0:T(8,128)(2,1)S(1)}, bf16[1024,128]{1,0:T(8,128)(2,1)S(1)}, u32[]{:S(2)}, u32[]{:S(2)}) collective-permute-start(bf16[1024,128]{1,0:T(8,128)(2,1)S(1)} %get-tuple-element.46), channel_id=1, source_target_pairs={{0,2},{1,3},{2,0},{3,1},{4,6},{5,7},{6,4},{7,5},{8,10},{9,11},{10,... | collective-permute-start | bytes 786440 | tf_op jit(solution)/shard_map/ppermute | solution.py:257
  16.1 11.8 %collective-permute-start.8 = (bf16[1024,128]{1,0:T(8,128)(2,1)S(1)}, bf16[1024,128]{1,0:T(8,128)(2,1)S(1)}, u32[]{:S(2)}, u32[]{:S(2)}) collective-permute-start(bf16[1024,128]{1,0:T(8,128)(2,1)S(1)} %get-tuple-element.47), channel_id=1, source_target_pairs={{0,4},{1,5},{2,6},{3,7},{4,0},{5,1},{6,2},{7,3},{8,12},{9,13},{10,... | collective-permute-start | bytes 786440 | tf_op jit(solution)/shard_map/ppermute | solution.py:257
  16.6 11.3 %collective-permute-start.9 = (bf16[1024,128]{1,0:T(8,128)(2,1)S(1)}, bf16[1024,128]{1,0:T(8,128)(2,1)S(1)}, u32[]{:S(2)}, u32[]{:S(2)}) collective-permute-start(bf16[1024,128]{1,0:T(8,128)(2,1)S(1)} %get-tuple-element.48), channel_id=1, source_target_pairs={{0,6},{1,7},{2,4},{3,5},{4,2},{5,3},{6,0},{7,1},{8,14},{9,15},{10,... | collective-permute-start | bytes 786440 | tf_op jit(solution)/shard_map/ppermute | solution.py:257
  19.4 8.5 %collective-permute-start.4 = (bf16[4,128,256]{2,1,0:T(8,128)(2,1)S(1)}, bf16[4,128,256]{2,1,0:T(8,128)(2,1)S(1)}, u32[]{:S(2)}, u32[]{:S(2)}) collective-permute-start(bf16[4,128,256]{2,1,0:T(8,128)(2,1)S(1)} %pad_maximum_fusion.refs_0_), channel_id=1, source_target_pairs={{0,1},{1,0},{2,3},{3,2},{4,5},{5,4},{6,7},{7,6},{8,9},{9,8},{10,11... | collective-permute-start | bytes 786440 | tf_op jit(solution)/shard_map/ppermute | solution.py:257
  19.4 8.5 %collective-permute-start.5 = (bf16[4,128,256]{2,1,0:T(8,128)(2,1)S(1)}, bf16[4,128,256]{2,1,0:T(8,128)(2,1)S(1)}, u32[]{:S(2)}, u32[]{:S(2)}) collective-permute-start(bf16[4,128,256]{2,1,0:T(8,128)(2,1)S(1)} %collective-permute-done.3.refs_2_), channel_id=1, source_target_pairs={{0,1},{1,0},{2,3},{3,2},{4,5},{5,4},{6,7},{7,6},{8,9},{9,8},{10,11... | collective-permute-start | bytes 786440 | tf_op jit(solution)/shard_map/ppermute | solution.py:257
  19.9 8.0 %copy-start.2 = (f32[4,512]{1,0:T(4,128)S(1)}, f32[4,512]{1,0:T(4,128)}, u32[]{:S(2)}) copy-start(f32[4,512]{1,0:T(4,128)} %refs_5_.1) | copy-start | bytes 24580
  24.5 3.5 %collective-permute-start.6 = (bf16[16,128]{1,0:T(8,128)(2,1)S(1)}, bf16[16,128]{1,0:T(8,128)(2,1)S(1)}, u32[]{:S(2)}, u32[]{:S(2)}) collective-permute-start(bf16[16,128]{1,0:T(8,128)(2,1)S(1)} %slice.95), channel_id=1, source_target_pairs={{1,16},{3,18},{5,20},{7,22},{9,24},{11,26},{13,28},{15,30}} | collective-permute-start | bytes 12296 | tf_op jit(solution)/shard_map/ppermute | solution.py:254
  37.4 0.7 %copy-start = (bf16[128,512]{1,0:T(8,128)(2,1)}, bf16[128,512]{1,0:T(8,128)(2,1)S(1)}, u32[]{:S(2)}) copy-start(bf16[128,512]{1,0:T(8,128)(2,1)S(1)} %get-tuple-element.56) | copy-start | bytes 393220
  38.1 3.4 %collective-permute-start.10 = (bf16[1040,256]{1,0:T(8,128)(2,1)S(1)}, bf16[1040,256]{1,0:T(8,128)(2,1)S(1)}, u32[]{:S(2)}, u32[]{:S(2)}) collective-permute-start(bf16[1040,256]{1,0:T(8,128)(2,1)S(1)} %get-tuple-element.49), channel_id=1, source_target_pairs={{0,1},{1,0},{2,3},{3,2},{4,5},{5,4},{6,7},{7,6},{8,9},{9,8},{10,11... | collective-permute-start | bytes 1597448 | tf_op jit(solution)/shard_map/ppermute | solution.py:257
  41.5 4.9 %copy-start.1 = (bf16[128,512]{1,0:T(8,128)(2,1)S(1)}, bf16[128,512]{1,0:T(8,128)(2,1)}, u32[]{:S(2)}) copy-start(bf16[128,512]{1,0:T(8,128)(2,1)} %copy-done) | copy-start | bytes 393220
  41.7 8.3 %collective-permute-start.15 = (f32[24,128]{1,0:T(8,128)S(1)}, f32[24,128]{1,0:T(8,128)S(1)}, u32[]{:S(2)}, u32[]{:S(2)}) collective-permute-start(f32[24,128]{1,0:T(8,128)S(1)} %select_maximum_fusion), channel_id=1, source_target_pairs={{0,16},{1,17},{2,18},{3,19},{4,20},{5,21},{6,22},{7,23},{8,24},{9,... | collective-permute-start | bytes 36872 | tf_op jit(solution)/shard_map/ppermute | solution.py:257
  45.1 10.0 %collective-permute-start.14 = (bf16[512,256]{1,0:T(8,128)(2,1)S(1)}, bf16[512,256]{1,0:T(8,128)(2,1)S(1)}, u32[]{:S(2)}, u32[]{:S(2)}) collective-permute-start(bf16[512,256]{1,0:T(8,128)(2,1)S(1)} %add_convert_fusion), channel_id=1, source_target_pairs={{8,0},{9,1},{10,2},{11,3},{12,4},{13,5},{14,6},{15,7},{16,8},{17,9... | collective-permute-start | bytes 786440 | tf_op jit(solution)/shard_map/ppermute | solution.py:254
  46.4 11.2 %collective-permute-start.11 = (bf16[128,512]{1,0:T(8,128)(2,1)S(1)}, bf16[128,512]{1,0:T(8,128)(2,1)S(1)}, u32[]{:S(2)}, u32[]{:S(2)}) collective-permute-start(bf16[128,512]{1,0:T(8,128)(2,1)S(1)} %copy-done.1), channel_id=1, source_target_pairs={{0,2},{1,3},{2,0},{3,1},{4,6},{5,7},{6,4},{7,5},{8,10},{9,11},{10,... | collective-permute-start | bytes 393224 | tf_op jit(solution)/shard_map/ppermute | solution.py:257
  47.4 11.9 %collective-permute-start.12 = (bf16[128,512]{1,0:T(8,128)(2,1)S(1)}, bf16[128,512]{1,0:T(8,128)(2,1)S(1)}, u32[]{:S(2)}, u32[]{:S(2)}) collective-permute-start(bf16[128,512]{1,0:T(8,128)(2,1)S(1)} %get-tuple-element.57), channel_id=1, source_target_pairs={{0,4},{1,5},{2,6},{3,7},{4,0},{5,1},{6,2},{7,3},{8,12},{9,13},{10,... | collective-permute-start | bytes 393224 | tf_op jit(solution)/shard_map/ppermute | solution.py:257
  47.9 11.4 %collective-permute-start.13 = (bf16[128,512]{1,0:T(8,128)(2,1)S(1)}, bf16[128,512]{1,0:T(8,128)(2,1)S(1)}, u32[]{:S(2)}, u32[]{:S(2)}) collective-permute-start(bf16[128,512]{1,0:T(8,128)(2,1)S(1)} %get-tuple-element.58), channel_id=1, source_target_pairs={{0,6},{1,7},{2,4},{3,5},{4,2},{5,3},{6,0},{7,1},{8,14},{9,15},{10,... | collective-permute-start | bytes 393224 | tf_op jit(solution)/shard_map/ppermute | solution.py:257
  50.0 6.2 %collective-permute-start.19 = (f32[64]{0:T(128)S(1)}, f32[64]{0:T(128)S(1)}, u32[]{:S(2)}, u32[]{:S(2)}) collective-permute-start(f32[64]{0:T(128)S(1)} %fusion.10), channel_id=1, source_target_pairs={{0,8},{1,9},{2,10},{3,11},{4,12},{5,13},{6,14},{7,15},{8,0},{9,1},... | collective-permute-start | bytes 776 | tf_op jit(solution)/shard_map/ppermute | solution.py:257
  55.2 5.3 %collective-permute-start.16 = (bf16[128,256]{1,0:T(8,128)(2,1)S(1)}, bf16[128,256]{1,0:T(8,128)(2,1)S(1)}, u32[]{:S(2)}, u32[]{:S(2)}) collective-permute-start(bf16[128,256]{1,0:T(8,128)(2,1)S(1)} %get-tuple-element.66), channel_id=1, source_target_pairs={{0,6},{1,7},{2,4},{3,5},{4,2},{5,3},{6,0},{7,1},{8,14},{9,15},{10,... | collective-permute-start | bytes 196616 | tf_op jit(solution)/shard_map/ppermute | solution.py:257
  56.2 5.0 %collective-permute-start.17 = (bf16[128,256]{1,0:T(8,128)(2,1)S(1)}, bf16[128,256]{1,0:T(8,128)(2,1)S(1)}, u32[]{:S(2)}, u32[]{:S(2)}) collective-permute-start(bf16[128,256]{1,0:T(8,128)(2,1)S(1)} %get-tuple-element.68), channel_id=1, source_target_pairs={{0,4},{1,5},{2,6},{3,7},{4,0},{5,1},{6,2},{7,3},{8,12},{9,13},{10,... | collective-permute-start | bytes 196616 | tf_op jit(solution)/shard_map/ppermute | solution.py:257
  57.7 4.3 %collective-permute-start.18 = (bf16[128,256]{1,0:T(8,128)(2,1)S(1)}, bf16[128,256]{1,0:T(8,128)(2,1)S(1)}, u32[]{:S(2)}, u32[]{:S(2)}) collective-permute-start(bf16[128,256]{1,0:T(8,128)(2,1)S(1)} %get-tuple-element.67), channel_id=1, source_target_pairs={{0,2},{1,3},{2,0},{3,1},{4,6},{5,7},{6,4},{7,5},{8,10},{9,11},{10,... | collective-permute-start | bytes 196616 | tf_op jit(solution)/shard_map/ppermute | solution.py:257

commit v7 on v5

--- a/solution.py
+++ b/solution.py
@@ -75,43 +75,20 @@
         grad_queries[:, columns_of(place[2] ^ turn, part.shape[1])] = part[...]
 
 
-def attend_kernel(scale, turns, place, *refs):
-    kv_same, kv_other, old_same, old_other, halo, all_taps = refs[:6]
-    query_grads = refs[6 : 6 + turns]
-    grad_qs = refs[6 + turns : 6 + 2 * turns]
-    send, keep_old, keep_own, tap_keep = refs[6 + 2 * turns : 10 + 2 * turns]
-    key_all, key_t, value_all, mix_all, dkey, dmix, *work = refs[10 + 2 * turns :]
+def by_eight(array):
+    return array.reshape(-1, 8, array.shape[1])
+
+
+def sweep(place, turns, query_grads, grad_qs, key_all, key_t, mix_all, dkey, dmix, work):
     rows, width = grad_qs[0].shape
-    blocks = turns
-    span = 2 * blocks
-    length = span * rows
+    length = WINDOW
+    span = length // rows
     lanes = 2 * HEAD_SIZE
     pairs = width // lanes
-    tap_count = all_taps.shape[0]
     group_at, parity, head_at = place
-    taps = all_taps[:, columns_of(head_at)]
     inv_root = 1.0 / math.sqrt(HEAD_SIZE)
     log2_scale = inv_root * math.log2(math.e)
     score_refs, gprob_refs, low_refs, dscore_refs = work[0:2], work[2:4], work[4:6], work[6:8]
-
-    def block_at(turn, core):
-        return 2 * (head_at ^ turn) + core
-
-    value_all[:HALO] = halo[...].astype(jnp.float32)
-    for start, same, other in ((0, old_same, old_other), (span, kv_same, kv_other)):
-        for turn in range(blocks):
-            for source, core in ((same, parity), (other, 1 - parity)):
-                first = pl.multiple_of((start + block_at(turn, core)) * rows, rows)
-                key_all[pl.ds(first, rows)] = source[turn, :, :HEAD_SIZE]
-                value_all[pl.ds(first + HALO, rows)] = source[turn, :, HEAD_SIZE:].astype(jnp.float32)
-    for start in range(HALO, HALO + 2 * length, rows):
-        mixed = taps[0:1] * value_all[start : start + rows]
-        for index_k in range(1, tap_count):
-            mixed = mixed + taps[index_k : index_k + 1] * value_all[start - index_k : start - index_k + rows]
-        mix_all[start - HALO : start - HALO + rows] = mixed.astype(jnp.bfloat16)
-    key_t[...] = jnp.transpose(key_all[...])
-    dkey[...] = jnp.zeros_like(dkey)
-    dmix[...] = jnp.zeros_like(dmix)
     fill = jnp.where(group_at == 0, NEG_FILL, 0.0).astype(jnp.float32)
     key_at = lax.broadcasted_iota(jnp.int32, (rows, lanes), 0)
     query_at = lax.broadcasted_iota(jnp.int32, (rows, lanes), 1) & (rows - 1)
@@ -120,14 +97,11 @@
 
     def places(n):
         step, pair = n // pairs, n % pairs
-        number = block_at(step, parity)
+        number = block_at(place, turns[step], parity)
         return step, pair, number, pl.multiple_of(number * rows, rows)
 
     def stacked(step, base):
         return query_grads[step][base // HEAD_SIZE * rows : (base + lanes) // HEAD_SIZE * rows]
-
-    def by_eight(array):
-        return array.reshape(-1, 8, array.shape[1])
 
     def scores_stage(n):
         step, pair, number, first = places(n)
@@ -190,7 +164,7 @@
             base = pair * lanes + h * HEAD_SIZE
             grad_qs[step][:, base : base + HEAD_SIZE] = dquery[h * rows : (h + 1) * rows]
 
-    count = blocks * pairs
+    count = len(turns) * pairs
     for n in range(count + 2):
         if n < count:
             scores_stage(n)
@@ -199,6 +173,57 @@
         if n >= 2:
             gradient_stage(n - 2)
 
+
+def block_at(place, turn, core):
+    return 2 * (place[2] ^ turn) + core
+
+
+def attend_first_kernel(turns, place, *refs):
+    kv_same, kv_other, old_same, old_other, halo, all_taps = refs[:6]
+    query_grads, refs = refs[6 : 6 + turns], refs[6 + turns :]
+    grad_qs, refs = refs[:turns], refs[turns:]
+    key_all, key_t, mix_all, value_all, dkey, dmix, *work = refs
+    blocks, rows = kv_same.shape[:2]
+    span = 2 * blocks
+    length = span * rows
+    tap_count = all_taps.shape[0]
+    parity = place[1]
+    taps = all_taps[:, columns_of(place[2])]
+    value_all[:HALO] = halo[...].astype(jnp.float32)
+    for start, same, other in ((0, old_same, old_other), (span, kv_same, kv_other)):
+        for turn in range(blocks):
+            for source, core in ((same, parity), (other, 1 - parity)):
+                first = pl.multiple_of((start + block_at(place, turn, core)) * rows, rows)
+                key_all[pl.ds(first, rows)] = source[turn, :, :HEAD_SIZE]
+                value_all[pl.ds(first + HALO, rows)] = source[turn, :, HEAD_SIZE:].astype(jnp.float32)
+    for start in range(HALO, HALO + 2 * length, rows):
+        mixed = taps[0:1] * value_all[start : start + rows]
+        for index_k in range(1, tap_count):
+            mixed = mixed + taps[index_k : index_k + 1] * value_all[start - index_k : start - index_k + rows]
+        mix_all[start - HALO : start - HALO + rows] = mixed.astype(jnp.bfloat16)
+    key_t[...] = jnp.transpose(key_all[...])
+    dkey[...] = jnp.zeros_like(dkey)
+    dmix[...] = jnp.zeros_like(dmix)
+    sweep(place, range(turns), query_grads, grad_qs, key_all, key_t, mix_all, dkey, dmix, work)
+
+
+def attend_last_kernel(scale, turns, place, *refs):
+    all_taps, key_all, key_t, mix_all, value_all, dkey_before, dmix_before = refs[:7]
+    query_grads, refs = refs[7 : 7 + turns], refs[7 + turns :]
+    grad_qs, refs = refs[:turns], refs[turns:]
+    send, keep_old, keep_own, tap_keep, dkey, dmix, *work = refs
+    rows = grad_qs[0].shape[0]
+    blocks = keep_old.shape[0] // rows
+    span = 2 * blocks
+    length = span * rows
+    tap_count = all_taps.shape[0]
+    parity = place[1]
+    taps = all_taps[:, columns_of(place[2])]
+    inv_root = 1.0 / math.sqrt(HEAD_SIZE)
+    dkey[...] = dkey_before[...]
+    dmix[...] = dmix_before[...]
+    sweep(place, range(blocks - turns, blocks), query_grads, grad_qs, key_all, key_t, mix_all, dkey, dmix, work)
+
     def convolved(start, size):
         total = taps[0:1] * dmix[pl.ds(start, size)]
         for index_k in range(1, tap_count):
@@ -208,7 +233,7 @@
     for start, keep, base in ((0, keep_old, 0), (span, keep_own, blocks * rows)):
         for turn in range(blocks):
             for target, core, offset in ((keep, parity, 0), (send, 1 - parity, base)):
-                first = pl.multiple_of((start + block_at(turn, core)) * rows, rows)
+                first = pl.multiple_of((start + block_at(place, turn, core)) * rows, rows)
                 at = slice(offset + turn * rows, offset + (turn + 1) * rows)
                 target[at, :HEAD_SIZE] = (dkey[pl.ds(first, rows)] * inv_root).astype(target.dtype)
                 target[at, HEAD_SIZE:] = convolved(first + HALO, rows).astype(target.dtype)
@@ -282,36 +307,40 @@
     halo = routed(last[rows - HALO :, HEAD_SIZE:], reach, lambda i: i % share == share - 1)
     lanes = 2 * HEAD_SIZE
     group_rows = kv_heads * rows
-    operands = (kv_same, kv_other, old_same, old_other, halo, conv_taps, *query_grads)
-    results = [shape((rows, own_width), bf16)] * kv_heads + [
-        shape((2 * group_rows + HALO, lanes), bf16),
-        shape((group_rows, lanes), bf16),
-        shape((group_rows, lanes), bf16),
-        shape((tap_count, HEAD_SIZE // 2), f32),
+    half = kv_heads - 1
+    work = [pltpu.VMEM((WINDOW, lanes), f32)] * 4 + [pltpu.VMEM((WINDOW + rows, lanes), bf16)] * 4
+    sums = [shape((2 * WINDOW, HEAD_SIZE), f32), shape((HALO + 2 * WINDOW + HALO, HEAD_SIZE), f32)]
+    kept = [
+        shape((2 * WINDOW, HEAD_SIZE), bf16),
+        shape((HEAD_SIZE, 2 * WINDOW), bf16),
+        shape((2 * WINDOW, HEAD_SIZE), bf16),
+        shape((HALO + 2 * WINDOW, HEAD_SIZE), f32),
     ]
+    *early, key_all, key_t, mix_all, value_all, dkey, dmix = launch(
+        functools.partial(attend_first_kernel, half),
+        [shape((rows, own_width), bf16)] * half + kept + sums,
+        (kv_same, kv_other, old_same, old_other, halo, conv_taps, *query_grads[:half]),
+        scratch=work,
+    )
     scale = 1.0 / math.sqrt(rows * count * lax.axis_size("rep"))
-    *grad_q, send, keep_old, keep_own, tap_keep = launch(
-        functools.partial(attend_kernel, scale, kv_heads),
-        results,
-        operands,
-        scratch=[
-            pltpu.VMEM((2 * WINDOW, HEAD_SIZE), bf16),
-            pltpu.VMEM((HEAD_SIZE, 2 * WINDOW), bf16),
-            pltpu.VMEM((HALO + 2 * WINDOW, HEAD_SIZE), f32),
-            pltpu.VMEM((2 * WINDOW, HEAD_SIZE), bf16),
-            pltpu.VMEM((2 * WINDOW, HEAD_SIZE), f32),
-            pltpu.VMEM((HALO + 2 * WINDOW + HALO, HEAD_SIZE), f32),
-        ]
-        + [pltpu.VMEM((WINDOW, lanes), f32)] * 4
-        + [pltpu.VMEM((WINDOW + rows, lanes), bf16)] * 4,
-        flops=10 * kv_heads * rows * (WINDOW + rows) * own_width,
+    *late, send, keep_old, keep_own, tap_keep = launch(
+        functools.partial(attend_last_kernel, scale, kv_heads - half),
+        [shape((rows, own_width), bf16)] * (kv_heads - half)
+        + [
+            shape((2 * group_rows + HALO, lanes), bf16),
+            shape((group_rows, lanes), bf16),
+            shape((group_rows, lanes), bf16),
+            shape((tap_count, HEAD_SIZE // 2), f32),
+        ],
+        (conv_taps, key_all, key_t, mix_all, value_all, dkey, dmix, *query_grads[half:]),
+        scratch=[pltpu.VMEM(a.shape, a.dtype) for a in sums] + work,
     )
     got = flipped(send, 1)
     note = got[2 * group_rows :].astype(f32)
     old_sum = (keep_old.astype(f32) + got[:group_rows].astype(f32)).astype(bf16)
-    note, *grad_q = after([old_sum], note, *grad_q)
+    note, *late = after([old_sum], note, *late)
     returned = routed(old_sum, -group)
-    grad_q = exchanged(grad_q)
+    grad_q = exchanged([*early, *late])
     halo, tap_grads = note[:, HEAD_SIZE:], note[:, : HEAD_SIZE // 2]
     tap_grads = tap_keep + (tap_grads[:tap_count] + tap_grads[tap_count : 2 * tap_count])
     short = planes == tap_count == 4
@@ -324,7 +353,6 @@
         returned_halo = jnp.where(plane < 2, note[:HALO], 0.0)
     else:
         returned_halo = routed(halo, -2 * group)
-    (keep_own,) = after(grad_q, keep_own)
     total = keep_own.astype(f32) + got[group_rows : 2 * group_rows].astype(f32) + returned.astype(f32)
     halo_block = jnp.pad(returned_halo, ((rows - HALO, 0), (HEAD_SIZE, 0)))
     owned = []

time: 63.3 us -> 62.3 us (0.984)
  waiting for transfers between devices: 18.8 us -> 16.5 us
  starting transfers between devices: 29.2 us -> 30.6 us
  local copies, waits for them, and re-layouts: 0.67 us -> 0.02 us
    ppermute x17, waiting for transfers between devices: 18.5 us -> 9.59 us  [flipped(): return lax.ppermute(array, 'seq', [(i, i ^ bits) for i in range(count)])]
    ppermute x3, waiting for transfers between devices: 0.31 us -> 6.95 us  [routed(): return lax.ppermute(array, 'seq', route)]
    ppermute x17, starting transfers between devices: 23.8 us -> 25.1 us  [flipped(): return lax.ppermute(array, 'seq', [(i, i ^ bits) for i in range(count)])]
    unnamed x6 -> x2, local copies, waits for them, and re-layouts: 0.66 us -> 0.01 us
    pallas_call x3 -> x4, Pallas kernels: 12 us -> 12.5 us  [run(): pl.pallas_call(kernel, out_shape=[pltpu.VMEM(a.shape, a.dtype) for a in o...]
  transfers between devices with their start and end apart: 20 -> 20, of which waited for: 12 -> 10; matrix products, arithmetic and copies ran while one was open for 1% -> 1% of each run, Pallas kernels for 1% -> 12%
where the time goes in v7:
time: 62.3 us; the launch traced here: 62 us
  starting transfers between devices  30.6 us (49%)
  waiting for transfers between devices  16.5 us (26%)
  Pallas kernels  12.5 us (20%)
  other arithmetic  1.57 us (3%)
  between operations  0.83 us (1%)
    ppermute x17, starting transfers between devices, flipped(): return lax.ppermute(array, 'seq', [(i, i ^ bits) for i in range(count)])  25.1 us
    pallas_call x4, Pallas kernels, run(): pl.pallas_call(kernel, out_shape=[pltpu.VMEM(a.shape, a.dtype) for a in o...  12.5 us
    ppermute x17, waiting for transfers between devices, flipped(): return lax.ppermute(array, 'seq', [(i, i ^ bits) for i in range(count)])  9.59 us
    ppermute x3, waiting for transfers between devices, routed(): return lax.ppermute(array, 'seq', route)  6.95 us
    ppermute x3, starting transfers between devices, routed(): return lax.ppermute(array, 'seq', route)  5.43 us
  transfers between devices with their start and end apart: 20, of which 10 were waited for; matrix products, arithmetic and copies ran while one was open for 1% of the time, Pallas kernels for 12%

profile of v7, /device:TPU:0, one launch (start us, length us, event | category | flops | bytes accessed | tf_op | source)
XLA Modules:
  0.0 62.0 jit_solution(11422705432132573299)
XLA Ops:
  0.6 1.6 %shard_map.84 = (bf16[128,256]{1,0:T(8,128)(2,1)S(1)}, bf16[128,256]{1,0:T(8,128)(2,1)S(1)}, bf16[128,256]{1,0:T(8,128)(2,1)S(1)}, bf16[128,256]{1,0:T(8,128)(2,...) custom-call(bf16[128,2048]{1,0:T(8,128)(2,1)} %bitcast.22, ...), custom_call_target="tpu_custom_call" | custom-call | bytes 2621440 | tf_op jit(solution)/shard_map/pallas_call | solution.py:29
  2.3 3.0 %collective-permute-start = (bf16[128,256]{1,0:T(8,128)(2,1)S(1)}, bf16[128,256]{1,0:T(8,128)(2,1)S(1)}, u32[]{:S(2)}, u32[]{:S(2)}) collective-permute-start(bf16[128,256]{1,0:T(8,128)(2,1)S(1)} %get-tuple-element.39), channel_id=1, source_target_pairs={{0,2},{1,3},{2,0},{3,1},{4,6},{5,7},{6,4},{7,5},{8,10},{9,11},{10,... | collective-permute-start | bytes 196616 | tf_op jit(solution)/shard_map/ppermute | solution.py:282
  5.3 1.5 %collective-permute-start.1 = (bf16[128,256]{1,0:T(8,128)(2,1)S(1)}, bf16[128,256]{1,0:T(8,128)(2,1)S(1)}, u32[]{:S(2)}, u32[]{:S(2)}) collective-permute-start(bf16[128,256]{1,0:T(8,128)(2,1)S(1)} %get-tuple-element.40), channel_id=1, source_target_pairs={{0,4},{1,5},{2,6},{3,7},{4,0},{5,1},{6,2},{7,3},{8,12},{9,13},{10,... | collective-permute-start | bytes 196616 | tf_op jit(solution)/shard_map/ppermute | solution.py:282
  7.7 1.9 %collective-permute-done.1 = bf16[128,256]{1,0:T(8,128)(2,1)S(1)} collective-permute-done((bf16[128,256]{1,0:T(8,128)(2,1)S(1)}, bf16[128,256]{1,0:T(8,128)(2,1)S(1)}, u32[]{:S(2)}, u32[]{:S(2)}) %collective-permute-start.1) | collective-permute-done | bytes 65568 | tf_op jit(solution)/shard_map/ppermute | solution.py:282
  9.6 2.4 %collective-permute-done.2 = bf16[128,256]{1,0:T(8,128)(2,1)S(1)} collective-permute-done((bf16[128,256]{1,0:T(8,128)(2,1)S(1)}, bf16[128,256]{1,0:T(8,128)(2,1)S(1)}, u32[]{:S(2)}, u32[]{:S(2)}) %collective-permute-start.2) | collective-permute-done | bytes 65568 | tf_op jit(solution)/shard_map/ppermute | solution.py:282
  12.0 3.5 %collective-permute-start.3 = (bf16[4,128,256]{2,1,0:T(8,128)(2,1)S(1)}, bf16[4,128,256]{2,1,0:T(8,128)(2,1)S(1)}, u32[]{:S(2)}, u32[]{:S(2)}) collective-permute-start(bf16[4,128,256]{2,1,0:T(8,128)(2,1)S(1)} %pad_maximum_fusion.refs_0_), channel_id=1, source_target_pairs={{0,8},{1,9},{2,10},{3,11},{4,12},{5,13},{6,14},{7,15},{8,16},{9,17... | collective-permute-start | bytes 786440 | tf_op jit(solution)/shard_map/ppermute | solution.py:279
  16.6 2.7 %collective-permute-done.3.refs_2_ = bf16[4,128,256]{2,1,0:T(8,128)(2,1)S(1)} collective-permute-done((bf16[4,128,256]{2,1,0:T(8,128)(2,1)S(1)}, bf16[4,128,256]{2,1,0:T(8,128)(2,1)S(1)}, u32[]{:S(2)}, u32[]{:S(2)}) %collective-permute-start.3) | collective-permute-done | bytes 262176 | tf_op jit(solution)/shard_map/ppermute | solution.py:279
  19.9 1.0 %collective-permute-start.11 = (bf16[1024,128]{1,0:T(8,128)(2,1)S(1)}, bf16[1024,128]{1,0:T(8,128)(2,1)S(1)}, u32[]{:S(2)}, u32[]{:S(2)}) collective-permute-start(bf16[1024,128]{1,0:T(8,128)(2,1)S(1)} %get-tuple-element.60), channel_id=1, source_target_pairs={{0,6},{1,7},{2,4},{3,5},{4,2},{5,3},{6,0},{7,1},{8,14},{9,15},{10,... | collective-permute-start | bytes 786440 | tf_op jit(solution)/shard_map/ppermute | solution.py:282
  20.9 1.1 %collective-permute-done.7.refs_7_ = bf16[1024,128]{1,0:T(8,128)(2,1)S(1)} collective-permute-done((bf16[1024,128]{1,0:T(8,128)(2,1)S(1)}, bf16[1024,128]{1,0:T(8,128)(2,1)S(1)}, u32[]{:S(2)}, u32[]{:S(2)}) %collective-permute-start.7) | collective-permute-done | bytes 262176 | tf_op jit(solution)/shard_map/ppermute | solution.py:282
  22.7 6.7 %shard_map.85 = (bf16[128,512]{1,0:T(8,128)(2,1)S(1)}, bf16[128,512]{1,0:T(8,128)(2,1)S(1)}, bf16[128,512]{1,0:T(8,128)(2,1)S(1)}, bf16[2048,128]{1,0:T(8,128)(2...) custom-call(bf16[4,128,256]{2,1,0:T(8,128)(2,1)S(1)} %pad_maximum_fu, ...), custom_call_target="tpu_custom_call" | custom-call | bytes 6983680 | tf_op jit(solution)/shard_map/pallas_call | solution.py:29
  29.4 3.3 %shard_map.86 = (bf16[128,512]{1,0:T(8,128)(2,1)S(1)}, bf16[1040,256]{1,0:T(8,128)(2,1)S(1)}, bf16[512,256]{1,0:T(8,128)(2,1)S(1)}, bf16[512,256]{1,0:T(8,128)(2,1)S(1)}, f32[4,64]{1,0:T(4,128)S(1)}) custom-call(f32[4,512]{1,0:T(4,128)S(1)} %copy-done, bf16[2048,128]{1,0:T(8,128)(2,1)S(1)} %get-tuple-element.54.refs_1_, ...), custom_call_target="tpu_custom_call" | custom-call | bytes 6202368 | tf_op jit(solution)/shard_map/pallas_call | solution.py:29
  32.7 4.8 %collective-permute-start.12 = (bf16[1040,256]{1,0:T(8,128)(2,1)S(1)}, bf16[1040,256]{1,0:T(8,128)(2,1)S(1)}, u32[]{:S(2)}, u32[]{:S(2)}) collective-permute-start(bf16[1040,256]{1,0:T(8,128)(2,1)S(1)} %get-tuple-element.61), channel_id=1, source_target_pairs={{0,1},{1,0},{2,3},{3,2},{4,5},{5,4},{6,7},{7,6},{8,9},{9,8},{10,11... | collective-permute-start | bytes 1597448 | tf_op jit(solution)/shard_map/ppermute | solution.py:282
  37.5 1.5 %collective-permute-done.12 = bf16[1040,256]{1,0:T(8,128)(2,1)S(1)} collective-permute-done((bf16[1040,256]{1,0:T(8,128)(2,1)S(1)}, bf16[1040,256]{1,0:T(8,128)(2,1)S(1)}, u32[]{:S(2)}, u32[]{:S(2)}) %collective-permute-start.12) | collective-permute-done | bytes 532512 | tf_op jit(solution)/shard_map/ppermute | solution.py:282
  39.2 3.4 %collective-permute-start.15 = (f32[24,128]{1,0:T(8,128)S(1)}, f32[24,128]{1,0:T(8,128)S(1)}, u32[]{:S(2)}, u32[]{:S(2)}) collective-permute-start(f32[24,128]{1,0:T(8,128)S(1)} %select_maximum_fusion), channel_id=1, source_target_pairs={{0,16},{1,17},{2,18},{3,19},{4,20},{5,21},{6,22},{7,23},{8,24},{9,... | collective-permute-start | bytes 36872 | tf_op jit(solution)/shard_map/ppermute | solution.py:282
  42.6 1.3 %collective-permute-start.10 = (bf16[128,512]{1,0:T(8,128)(2,1)S(1)}, bf16[128,512]{1,0:T(8,128)(2,1)S(1)}, u32[]{:S(2)}, u32[]{:S(2)}) collective-permute-start(bf16[128,512]{1,0:T(8,128)(2,1)S(1)} %get-tuple-element.53), channel_id=1, source_target_pairs={{0,4},{1,5},{2,6},{3,7},{4,0},{5,1},{6,2},{7,3},{8,12},{9,13},{10,... | collective-permute-start | bytes 393224 | tf_op jit(solution)/shard_map/ppermute | solution.py:282
  43.9 1.1 %collective-permute-start.9 = (bf16[128,512]{1,0:T(8,128)(2,1)S(1)}, bf16[128,512]{1,0:T(8,128)(2,1)S(1)}, u32[]{:S(2)}, u32[]{:S(2)}) collective-permute-start(bf16[128,512]{1,0:T(8,128)(2,1)S(1)} %get-tuple-element.52), channel_id=1, source_target_pairs={{0,2},{1,3},{2,0},{3,1},{4,6},{5,7},{6,4},{7,5},{8,10},{9,11},{10,... | collective-permute-start | bytes 393224 | tf_op jit(solution)/shard_map/ppermute | solution.py:282
  45.0 1.3 %collective-permute-start.14 = (bf16[512,256]{1,0:T(8,128)(2,1)S(1)}, bf16[512,256]{1,0:T(8,128)(2,1)S(1)}, u32[]{:S(2)}, u32[]{:S(2)}) collective-permute-start(bf16[512,256]{1,0:T(8,128)(2,1)S(1)} %add_convert_fusion), channel_id=1, source_target_pairs={{8,0},{9,1},{10,2},{11,3},{12,4},{13,5},{14,6},{15,7},{16,8},{17,9... | collective-permute-start | bytes 786440 | tf_op jit(solution)/shard_map/ppermute | solution.py:279
  46.3 1.2 %collective-permute-start.13 = (bf16[128,512]{1,0:T(8,128)(2,1)S(1)}, bf16[128,512]{1,0:T(8,128)(2,1)S(1)}, u32[]{:S(2)}, u32[]{:S(2)}) collective-permute-start(bf16[128,512]{1,0:T(8,128)(2,1)S(1)} %get-tuple-element.64), channel_id=1, source_target_pairs={{0,6},{1,7},{2,4},{3,5},{4,2},{5,3},{6,0},{7,1},{8,14},{9,15},{10,... | collective-permute-start | bytes 393224 | tf_op jit(solution)/shard_map/ppermute | solution.py:282
  47.5 2.7 %collective-permute-start.19 = (f32[64]{0:T(128)S(1)}, f32[64]{0:T(128)S(1)}, u32[]{:S(2)}, u32[]{:S(2)}) collective-permute-start(f32[64]{0:T(128)S(1)} %fusion.10), channel_id=1, source_target_pairs={{0,8},{1,9},{2,10},{3,11},{4,12},{5,13},{6,14},{7,15},{8,0},{9,1},... | collective-permute-start | bytes 776 | tf_op jit(solution)/shard_map/ppermute | solution.py:282
  50.2 4.2 %collective-permute-done.14 = bf16[512,256]{1,0:T(8,128)(2,1)S(1)} collective-permute-done((bf16[512,256]{1,0:T(8,128)(2,1)S(1)}, bf16[512,256]{1,0:T(8,128)(2,1)S(1)}, u32[]{:S(2)}, u32[]{:S(2)}) %collective-permute-start.14) | collective-permute-done | bytes 262176 | tf_op jit(solution)/shard_map/ppermute | solution.py:279
  54.5 1.2 %collective-permute-start.16 = (bf16[128,256]{1,0:T(8,128)(2,1)S(1)}, bf16[128,256]{1,0:T(8,128)(2,1)S(1)}, u32[]{:S(2)}, u32[]{:S(2)}) collective-permute-start(bf16[128,256]{1,0:T(8,128)(2,1)S(1)} %get-tuple-element.72), channel_id=1, source_target_pairs={{0,6},{1,7},{2,4},{3,5},{4,2},{5,3},{6,0},{7,1},{8,14},{9,15},{10,... | collective-permute-start | bytes 196616 | tf_op jit(solution)/shard_map/ppermute | solution.py:282
  55.7 1.3 %collective-permute-start.17 = (bf16[128,256]{1,0:T(8,128)(2,1)S(1)}, bf16[128,256]{1,0:T(8,128)(2,1)S(1)}, u32[]{:S(2)}, u32[]{:S(2)}) collective-permute-start(bf16[128,256]{1,0:T(8,128)(2,1)S(1)} %get-tuple-element.74), channel_id=1, source_target_pairs={{0,4},{1,5},{2,6},{3,7},{4,0},{5,1},{6,2},{7,3},{8,12},{9,13},{10,... | collective-permute-start | bytes 196616 | tf_op jit(solution)/shard_map/ppermute | solution.py:282
  57.0 1.1 %collective-permute-start.18 = (bf16[128,256]{1,0:T(8,128)(2,1)S(1)}, bf16[128,256]{1,0:T(8,128)(2,1)S(1)}, u32[]{:S(2)}, u32[]{:S(2)}) collective-permute-start(bf16[128,256]{1,0:T(8,128)(2,1)S(1)} %get-tuple-element.73), channel_id=1, source_target_pairs={{0,2},{1,3},{2,0},{3,1},{4,6},{5,7},{6,4},{7,5},{8,10},{9,11},{10,... | collective-permute-start | bytes 196616 | tf_op jit(solution)/shard_map/ppermute | solution.py:282
  58.6 0.8 %shard_map.87 = bf16[128,2048]{1,0:T(8,128)(2,1)} custom-call(bf16[128,512]{1,0:T(8,128)(2,1)S(1)} %get-tuple-element.68.refs_0_, bf16[128,512]{1,0:T(8,128)(2,1)S(1)} %collective-permute-done.9.refs_1_, bf16[128,512]{1,0:T(8,128)(2,1)S(1)} %collective-permute-done.10.refs_2_, bf16[128,512]{1,0:T(8,128)(2,1)S(1)} %collective-permute-done.13.refs_3_), custom_call_target="tpu_custom_call" | custom-call | bytes 1048576 | tf_op jit(solution)/shard_map/pallas_call | solution.py:29
  (41 shorter events, 6.5 us)
Async XLA Ops:
  0.6 22.0 %copy-start = (f32[4,512]{1,0:T(4,128)S(1)}, f32[4,512]{1,0:T(4,128)}, u32[]{:S(2)}) copy-start(f32[4,512]{1,0:T(4,128)} %refs_0_.1) | copy-start | bytes 24580
  2.3 5.4 %collective-permute-start = (bf16[128,256]{1,0:T(8,128)(2,1)S(1)}, bf16[128,256]{1,0:T(8,128)(2,1)S(1)}, u32[]{:S(2)}, u32[]{:S(2)}) collective-permute-start(bf16[128,256]{1,0:T(8,128)(2,1)S(1)} %get-tuple-element.39), channel_id=1, source_target_pairs={{0,2},{1,3},{2,0},{3,1},{4,6},{5,7},{6,4},{7,5},{8,10},{9,11},{10,... | collective-permute-start | bytes 196616 | tf_op jit(solution)/shard_map/ppermute | solution.py:282
  5.3 4.3 %collective-permute-start.1 = (bf16[128,256]{1,0:T(8,128)(2,1)S(1)}, bf16[128,256]{1,0:T(8,128)(2,1)S(1)}, u32[]{:S(2)}, u32[]{:S(2)}) collective-permute-start(bf16[128,256]{1,0:T(8,128)(2,1)S(1)} %get-tuple-element.40), channel_id=1, source_target_pairs={{0,4},{1,5},{2,6},{3,7},{4,0},{5,1},{6,2},{7,3},{8,12},{9,13},{10,... | collective-permute-start | bytes 196616 | tf_op jit(solution)/shard_map/ppermute | solution.py:282
  6.8 5.2 %collective-permute-start.2 = (bf16[128,256]{1,0:T(8,128)(2,1)S(1)}, bf16[128,256]{1,0:T(8,128)(2,1)S(1)}, u32[]{:S(2)}, u32[]{:S(2)}) collective-permute-start(bf16[128,256]{1,0:T(8,128)(2,1)S(1)} %get-tuple-element.41), channel_id=1, source_target_pairs={{0,6},{1,7},{2,4},{3,5},{4,2},{5,3},{6,0},{7,1},{8,14},{9,15},{10,... | collective-permute-start | bytes 196616 | tf_op jit(solution)/shard_map/ppermute | solution.py:282
  12.0 7.4 %collective-permute-start.3 = (bf16[4,128,256]{2,1,0:T(8,128)(2,1)S(1)}, bf16[4,128,256]{2,1,0:T(8,128)(2,1)S(1)}, u32[]{:S(2)}, u32[]{:S(2)}) collective-permute-start(bf16[4,128,256]{2,1,0:T(8,128)(2,1)S(1)} %pad_maximum_fusion.refs_0_), channel_id=1, source_target_pairs={{0,8},{1,9},{2,10},{3,11},{4,12},{5,13},{6,14},{7,15},{8,16},{9,17... | collective-permute-start | bytes 786440 | tf_op jit(solution)/shard_map/ppermute | solution.py:279
  15.5 6.4 %collective-permute-start.7 = (bf16[1024,128]{1,0:T(8,128)(2,1)S(1)}, bf16[1024,128]{1,0:T(8,128)(2,1)S(1)}, u32[]{:S(2)}, u32[]{:S(2)}) collective-permute-start(bf16[1024,128]{1,0:T(8,128)(2,1)S(1)} %get-tuple-element.49), channel_id=1, source_target_pairs={{0,2},{1,3},{2,0},{3,1},{4,6},{5,7},{6,4},{7,5},{8,10},{9,11},{10,... | collective-permute-start | bytes 786440 | tf_op jit(solution)/shard_map/ppermute | solution.py:282
  16.1 6.5 %collective-permute-start.8 = (bf16[1024,128]{1,0:T(8,128)(2,1)S(1)}, bf16[1024,128]{1,0:T(8,128)(2,1)S(1)}, u32[]{:S(2)}, u32[]{:S(2)}) collective-permute-start(bf16[1024,128]{1,0:T(8,128)(2,1)S(1)} %get-tuple-element.50), channel_id=1, source_target_pairs={{0,4},{1,5},{2,6},{3,7},{4,0},{5,1},{6,2},{7,3},{8,12},{9,13},{10,... | collective-permute-start | bytes 786440 | tf_op jit(solution)/shard_map/ppermute | solution.py:282
  19.4 3.3 %collective-permute-start.4 = (bf16[4,128,256]{2,1,0:T(8,128)(2,1)S(1)}, bf16[4,128,256]{2,1,0:T(8,128)(2,1)S(1)}, u32[]{:S(2)}, u32[]{:S(2)}) collective-permute-start(bf16[4,128,256]{2,1,0:T(8,128)(2,1)S(1)} %pad_maximum_fusion.refs_0_), channel_id=1, source_target_pairs={{0,1},{1,0},{2,3},{3,2},{4,5},{5,4},{6,7},{7,6},{8,9},{9,8},{10,11... | collective-permute-start | bytes 786440 | tf_op jit(solution)/shard_map/ppermute | solution.py:282
  19.4 3.3 %collective-permute-start.5 = (bf16[4,128,256]{2,1,0:T(8,128)(2,1)S(1)}, bf16[4,128,256]{2,1,0:T(8,128)(2,1)S(1)}, u32[]{:S(2)}, u32[]{:S(2)}) collective-permute-start(bf16[4,128,256]{2,1,0:T(8,128)(2,1)S(1)} %collective-permute-done.3.refs_2_), channel_id=1, source_target_pairs={{0,1},{1,0},{2,3},{3,2},{4,5},{5,4},{6,7},{7,6},{8,9},{9,8},{10,11... | collective-permute-start | bytes 786440 | tf_op jit(solution)/shard_map/ppermute | solution.py:282
  19.9 9.5 %collective-permute-start.11 = (bf16[1024,128]{1,0:T(8,128)(2,1)S(1)}, bf16[1024,128]{1,0:T(8,128)(2,1)S(1)}, u32[]{:S(2)}, u32[]{:S(2)}) collective-permute-start(bf16[1024,128]{1,0:T(8,128)(2,1)S(1)} %get-tuple-element.60), channel_id=1, source_target_pairs={{0,6},{1,7},{2,4},{3,5},{4,2},{5,3},{6,0},{7,1},{8,14},{9,15},{10,... | collective-permute-start | bytes 786440 | tf_op jit(solution)/shard_map/ppermute | solution.py:282
  22.0 0.7 %collective-permute-start.6 = (bf16[16,128]{1,0:T(8,128)(2,1)S(1)}, bf16[16,128]{1,0:T(8,128)(2,1)S(1)}, u32[]{:S(2)}, u32[]{:S(2)}) collective-permute-start(bf16[16,128]{1,0:T(8,128)(2,1)S(1)} %slice.95), channel_id=1, source_target_pairs={{1,16},{3,18},{5,20},{7,22},{9,24},{11,26},{13,28},{15,30}} | collective-permute-start | bytes 12296 | tf_op jit(solution)/shard_map/ppermute | solution.py:279
  32.7 6.3 %collective-permute-start.12 = (bf16[1040,256]{1,0:T(8,128)(2,1)S(1)}, bf16[1040,256]{1,0:T(8,128)(2,1)S(1)}, u32[]{:S(2)}, u32[]{:S(2)}) collective-permute-start(bf16[1040,256]{1,0:T(8,128)(2,1)S(1)} %get-tuple-element.61), channel_id=1, source_target_pairs={{0,1},{1,0},{2,3},{3,2},{4,5},{5,4},{6,7},{7,6},{8,9},{9,8},{10,11... | collective-permute-start | bytes 1597448 | tf_op jit(solution)/shard_map/ppermute | solution.py:282
  39.2 8.3 %collective-permute-start.15 = (f32[24,128]{1,0:T(8,128)S(1)}, f32[24,128]{1,0:T(8,128)S(1)}, u32[]{:S(2)}, u32[]{:S(2)}) collective-permute-start(f32[24,128]{1,0:T(8,128)S(1)} %select_maximum_fusion), channel_id=1, source_target_pairs={{0,16},{1,17},{2,18},{3,19},{4,20},{5,21},{6,22},{7,23},{8,24},{9,... | collective-permute-start | bytes 36872 | tf_op jit(solution)/shard_map/ppermute | solution.py:282
  42.6 13.1 %collective-permute-start.10 = (bf16[128,512]{1,0:T(8,128)(2,1)S(1)}, bf16[128,512]{1,0:T(8,128)(2,1)S(1)}, u32[]{:S(2)}, u32[]{:S(2)}) collective-permute-start(bf16[128,512]{1,0:T(8,128)(2,1)S(1)} %get-tuple-element.53), channel_id=1, source_target_pairs={{0,4},{1,5},{2,6},{3,7},{4,0},{5,1},{6,2},{7,3},{8,12},{9,13},{10,... | collective-permute-start | bytes 393224 | tf_op jit(solution)/shard_map/ppermute | solution.py:282
  43.9 14.7 %collective-permute-start.9 = (bf16[128,512]{1,0:T(8,128)(2,1)S(1)}, bf16[128,512]{1,0:T(8,128)(2,1)S(1)}, u32[]{:S(2)}, u32[]{:S(2)}) collective-permute-start(bf16[128,512]{1,0:T(8,128)(2,1)S(1)} %get-tuple-element.52), channel_id=1, source_target_pairs={{0,2},{1,3},{2,0},{3,1},{4,6},{5,7},{6,4},{7,5},{8,10},{9,11},{10,... | collective-permute-start | bytes 393224 | tf_op jit(solution)/shard_map/ppermute | solution.py:282
  45.0 9.4 %collective-permute-start.14 = (bf16[512,256]{1,0:T(8,128)(2,1)S(1)}, bf16[512,256]{1,0:T(8,128)(2,1)S(1)}, u32[]{:S(2)}, u32[]{:S(2)}) collective-permute-start(bf16[512,256]{1,0:T(8,128)(2,1)S(1)} %add_convert_fusion), channel_id=1, source_target_pairs={{8,0},{9,1},{10,2},{11,3},{12,4},{13,5},{14,6},{15,7},{16,8},{17,9... | collective-permute-start | bytes 786440 | tf_op jit(solution)/shard_map/ppermute | solution.py:279
  46.3 12.3 %collective-permute-start.13 = (bf16[128,512]{1,0:T(8,128)(2,1)S(1)}, bf16[128,512]{1,0:T(8,128)(2,1)S(1)}, u32[]{:S(2)}, u32[]{:S(2)}) collective-permute-start(bf16[128,512]{1,0:T(8,128)(2,1)S(1)} %get-tuple-element.64), channel_id=1, source_target_pairs={{0,6},{1,7},{2,4},{3,5},{4,2},{5,3},{6,0},{7,1},{8,14},{9,15},{10,... | collective-permute-start | bytes 393224 | tf_op jit(solution)/shard_map/ppermute | solution.py:282
  47.5 9.5 %collective-permute-start.19 = (f32[64]{0:T(128)S(1)}, f32[64]{0:T(128)S(1)}, u32[]{:S(2)}, u32[]{:S(2)}) collective-permute-start(f32[64]{0:T(128)S(1)} %fusion.10), channel_id=1, source_target_pairs={{0,8},{1,9},{2,10},{3,11},{4,12},{5,13},{6,14},{7,15},{8,0},{9,1},... | collective-permute-start | bytes 776 | tf_op jit(solution)/shard_map/ppermute | solution.py:282
  54.5 5.3 %collective-permute-start.16 = (bf16[128,256]{1,0:T(8,128)(2,1)S(1)}, bf16[128,256]{1,0:T(8,128)(2,1)S(1)}, u32[]{:S(2)}, u32[]{:S(2)}) collective-permute-start(bf16[128,256]{1,0:T(8,128)(2,1)S(1)} %get-tuple-element.72), channel_id=1, source_target_pairs={{0,6},{1,7},{2,4},{3,5},{4,2},{5,3},{6,0},{7,1},{8,14},{9,15},{10,... | collective-permute-start | bytes 196616 | tf_op jit(solution)/shard_map/ppermute | solution.py:282
  55.7 4.8 %collective-permute-start.17 = (bf16[128,256]{1,0:T(8,128)(2,1)S(1)}, bf16[128,256]{1,0:T(8,128)(2,1)S(1)}, u32[]{:S(2)}, u32[]{:S(2)}) collective-permute-start(bf16[128,256]{1,0:T(8,128)(2,1)S(1)} %get-tuple-element.74), channel_id=1, source_target_pairs={{0,4},{1,5},{2,6},{3,7},{4,0},{5,1},{6,2},{7,3},{8,12},{9,13},{10,... | collective-permute-start | bytes 196616 | tf_op jit(solution)/shard_map/ppermute | solution.py:282
  57.0 4.3 %collective-permute-start.18 = (bf16[128,256]{1,0:T(8,128)(2,1)S(1)}, bf16[128,256]{1,0:T(8,128)(2,1)S(1)}, u32[]{:S(2)}, u32[]{:S(2)}) collective-permute-start(bf16[128,256]{1,0:T(8,128)(2,1)S(1)} %get-tuple-element.73), channel_id=1, source_target_pairs={{0,2},{1,3},{2,0},{3,1},{4,6},{5,7},{6,4},{7,5},{8,10},{9,11},{10,... | collective-permute-start | bytes 196616 | tf_op jit(solution)/shard_map/ppermute | solution.py:282

commit v8 on v7

--- a/solution.py
+++ b/solution.py
@@ -338,9 +338,9 @@
     got = flipped(send, 1)
     note = got[2 * group_rows :].astype(f32)
     old_sum = (keep_old.astype(f32) + got[:group_rows].astype(f32)).astype(bf16)
-    note, *late = after([old_sum], note, *late)
+    note, *grad_q = after([old_sum], note, *early, *late)
     returned = routed(old_sum, -group)
-    grad_q = exchanged([*early, *late])
+    grad_q = exchanged(grad_q)
     halo, tap_grads = note[:, HEAD_SIZE:], note[:, : HEAD_SIZE // 2]
     tap_grads = tap_keep + (tap_grads[:tap_count] + tap_grads[tap_count : 2 * tap_count])
     short = planes == tap_count == 4

time: 62.3 us -> 60.5 us (0.971)
  waiting for transfers between devices: 16.5 us -> 14.7 us
    ppermute x3, waiting for transfers between devices: 6.95 us -> 5.13 us  [routed(): return lax.ppermute(array, 'seq', route)]
  transfers between devices with their start and end apart: 20 -> 20, of which waited for: 10 -> 10; matrix products, arithmetic and copies ran while one was open for 1% -> 1% of each run, Pallas kernels for 12% -> 13%
where the time goes in v8:
time: 60.5 us; the launch traced here: 60.2 us
  starting transfers between devices  30.6 us (51%)
  waiting for transfers between devices  14.7 us (24%)
  Pallas kernels  12.5 us (21%)
  other arithmetic  1.57 us (3%)
  between operations  0.83 us (1%)
    ppermute x17, starting transfers between devices, flipped(): return lax.ppermute(array, 'seq', [(i, i ^ bits) for i in range(count)])  25.1 us
    pallas_call x4, Pallas kernels, run(): pl.pallas_call(kernel, out_shape=[pltpu.VMEM(a.shape, a.dtype) for a in o...  12.5 us
    ppermute x17, waiting for transfers between devices, flipped(): return lax.ppermute(array, 'seq', [(i, i ^ bits) for i in range(count)])  9.56 us
    ppermute x3, starting transfers between devices, routed(): return lax.ppermute(array, 'seq', route)  5.43 us
    ppermute x3, waiting for transfers between devices, routed(): return lax.ppermute(array, 'seq', route)  5.13 us
  transfers between devices with their start and end apart: 20, of which 10 were waited for; matrix products, arithmetic and copies ran while one was open for 1% of the time, Pallas kernels for 13%

profile of v8, /device:TPU:0, one launch (start us, length us, event | category | flops | bytes accessed | tf_op | source)
XLA Modules:
  0.0 60.2 jit_solution(13170067286466410655)
XLA Ops:
  0.6 1.6 %shard_map.84 = (bf16[128,256]{1,0:T(8,128)(2,1)S(1)}, bf16[128,256]{1,0:T(8,128)(2,1)S(1)}, bf16[128,256]{1,0:T(8,128)(2,1)S(1)}, bf16[128,256]{1,0:T(8,128)(2,...) custom-call(bf16[128,2048]{1,0:T(8,128)(2,1)} %bitcast.22, ...), custom_call_target="tpu_custom_call" | custom-call | bytes 2621440 | tf_op jit(solution)/shard_map/pallas_call | solution.py:29
  2.3 3.0 %collective-permute-start = (bf16[128,256]{1,0:T(8,128)(2,1)S(1)}, bf16[128,256]{1,0:T(8,128)(2,1)S(1)}, u32[]{:S(2)}, u32[]{:S(2)}) collective-permute-start(bf16[128,256]{1,0:T(8,128)(2,1)S(1)} %get-tuple-element.42), channel_id=1, source_target_pairs={{0,2},{1,3},{2,0},{3,1},{4,6},{5,7},{6,4},{7,5},{8,10},{9,11},{10,... | collective-permute-start | bytes 196616 | tf_op jit(solution)/shard_map/ppermute | solution.py:282
  5.3 1.5 %collective-permute-start.1 = (bf16[128,256]{1,0:T(8,128)(2,1)S(1)}, bf16[128,256]{1,0:T(8,128)(2,1)S(1)}, u32[]{:S(2)}, u32[]{:S(2)}) collective-permute-start(bf16[128,256]{1,0:T(8,128)(2,1)S(1)} %get-tuple-element.43), channel_id=1, source_target_pairs={{0,4},{1,5},{2,6},{3,7},{4,0},{5,1},{6,2},{7,3},{8,12},{9,13},{10,... | collective-permute-start | bytes 196616 | tf_op jit(solution)/shard_map/ppermute | solution.py:282
  7.7 1.9 %collective-permute-done.1 = bf16[128,256]{1,0:T(8,128)(2,1)S(1)} collective-permute-done((bf16[128,256]{1,0:T(8,128)(2,1)S(1)}, bf16[128,256]{1,0:T(8,128)(2,1)S(1)}, u32[]{:S(2)}, u32[]{:S(2)}) %collective-permute-start.1) | collective-permute-done | bytes 65568 | tf_op jit(solution)/shard_map/ppermute | solution.py:282
  9.6 2.4 %collective-permute-done.2 = bf16[128,256]{1,0:T(8,128)(2,1)S(1)} collective-permute-done((bf16[128,256]{1,0:T(8,128)(2,1)S(1)}, bf16[128,256]{1,0:T(8,128)(2,1)S(1)}, u32[]{:S(2)}, u32[]{:S(2)}) %collective-permute-start.2) | collective-permute-done | bytes 65568 | tf_op jit(solution)/shard_map/ppermute | solution.py:282
  12.0 3.5 %collective-permute-start.3 = (bf16[4,128,256]{2,1,0:T(8,128)(2,1)S(1)}, bf16[4,128,256]{2,1,0:T(8,128)(2,1)S(1)}, u32[]{:S(2)}, u32[]{:S(2)}) collective-permute-start(bf16[4,128,256]{2,1,0:T(8,128)(2,1)S(1)} %pad_maximum_fusion.refs_0_), channel_id=1, source_target_pairs={{0,8},{1,9},{2,10},{3,11},{4,12},{5,13},{6,14},{7,15},{8,16},{9,17... | collective-permute-start | bytes 786440 | tf_op jit(solution)/shard_map/ppermute | solution.py:279
  16.6 2.7 %collective-permute-done.3.refs_2_ = bf16[4,128,256]{2,1,0:T(8,128)(2,1)S(1)} collective-permute-done((bf16[4,128,256]{2,1,0:T(8,128)(2,1)S(1)}, bf16[4,128,256]{2,1,0:T(8,128)(2,1)S(1)}, u32[]{:S(2)}, u32[]{:S(2)}) %collective-permute-start.3) | collective-permute-done | bytes 262176 | tf_op jit(solution)/shard_map/ppermute | solution.py:279
  19.9 1.0 %collective-permute-start.9 = (bf16[1024,128]{1,0:T(8,128)(2,1)S(1)}, bf16[1024,128]{1,0:T(8,128)(2,1)S(1)}, u32[]{:S(2)}, u32[]{:S(2)}) collective-permute-start(bf16[1024,128]{1,0:T(8,128)(2,1)S(1)} %get-tuple-element.60), channel_id=1, source_target_pairs={{0,6},{1,7},{2,4},{3,5},{4,2},{5,3},{6,0},{7,1},{8,14},{9,15},{10,... | collective-permute-start | bytes 786440 | tf_op jit(solution)/shard_map/ppermute | solution.py:282
  20.9 1.1 %collective-permute-done.7.refs_7_ = bf16[1024,128]{1,0:T(8,128)(2,1)S(1)} collective-permute-done((bf16[1024,128]{1,0:T(8,128)(2,1)S(1)}, bf16[1024,128]{1,0:T(8,128)(2,1)S(1)}, u32[]{:S(2)}, u32[]{:S(2)}) %collective-permute-start.7) | collective-permute-done | bytes 262176 | tf_op jit(solution)/shard_map/ppermute | solution.py:282
  22.7 6.7 %shard_map.85 = (bf16[128,512]{1,0:T(8,128)(2,1)S(1)}, bf16[128,512]{1,0:T(8,128)(2,1)S(1)}, bf16[128,512]{1,0:T(8,128)(2,1)S(1)}, bf16[2048,128]{1,0:T(8,128)(2...) custom-call(bf16[4,128,256]{2,1,0:T(8,128)(2,1)S(1)} %pad_maximum_fu, ...), custom_call_target="tpu_custom_call" | custom-call | bytes 6983680 | tf_op jit(solution)/shard_map/pallas_call | solution.py:29
  29.4 3.3 %shard_map.86 = (bf16[128,512]{1,0:T(8,128)(2,1)S(1)}, bf16[1040,256]{1,0:T(8,128)(2,1)S(1)}, bf16[512,256]{1,0:T(8,128)(2,1)S(1)}, bf16[512,256]{1,0:T(8,128)(2,1)S(1)}, f32[4,64]{1,0:T(4,128)S(1)}) custom-call(f32[4,512]{1,0:T(4,128)S(1)} %copy-done, bf16[2048,128]{1,0:T(8,128)(2,1)S(1)} %get-tuple-element.54.refs_1_, ...), custom_call_target="tpu_custom_call" | custom-call | bytes 6202368 | tf_op jit(solution)/shard_map/pallas_call | solution.py:29
  32.7 4.8 %collective-permute-start.10 = (bf16[1040,256]{1,0:T(8,128)(2,1)S(1)}, bf16[1040,256]{1,0:T(8,128)(2,1)S(1)}, u32[]{:S(2)}, u32[]{:S(2)}) collective-permute-start(bf16[1040,256]{1,0:T(8,128)(2,1)S(1)} %get-tuple-element.61), channel_id=1, source_target_pairs={{0,1},{1,0},{2,3},{3,2},{4,5},{5,4},{6,7},{7,6},{8,9},{9,8},{10,11... | collective-permute-start | bytes 1597448 | tf_op jit(solution)/shard_map/ppermute | solution.py:282
  37.5 1.5 %collective-permute-done.10 = bf16[1040,256]{1,0:T(8,128)(2,1)S(1)} collective-permute-done((bf16[1040,256]{1,0:T(8,128)(2,1)S(1)}, bf16[1040,256]{1,0:T(8,128)(2,1)S(1)}, u32[]{:S(2)}, u32[]{:S(2)}) %collective-permute-start.10) | collective-permute-done | bytes 532512 | tf_op jit(solution)/shard_map/ppermute | solution.py:282
  39.2 3.4 %collective-permute-start.15 = (f32[24,128]{1,0:T(8,128)S(1)}, f32[24,128]{1,0:T(8,128)S(1)}, u32[]{:S(2)}, u32[]{:S(2)}) collective-permute-start(f32[24,128]{1,0:T(8,128)S(1)} %select_maximum_fusion), channel_id=1, source_target_pairs={{0,16},{1,17},{2,18},{3,19},{4,20},{5,21},{6,22},{7,23},{8,24},{9,... | collective-permute-start | bytes 36872 | tf_op jit(solution)/shard_map/ppermute | solution.py:282
  42.6 1.3 %collective-permute-start.14 = (bf16[512,256]{1,0:T(8,128)(2,1)S(1)}, bf16[512,256]{1,0:T(8,128)(2,1)S(1)}, u32[]{:S(2)}, u32[]{:S(2)}) collective-permute-start(bf16[512,256]{1,0:T(8,128)(2,1)S(1)} %add_convert_fusion), channel_id=1, source_target_pairs={{8,0},{9,1},{10,2},{11,3},{12,4},{13,5},{14,6},{15,7},{16,8},{17,9... | collective-permute-start | bytes 786440 | tf_op jit(solution)/shard_map/ppermute | solution.py:279
  43.9 0.9 %collective-permute-start.11 = (bf16[128,512]{1,0:T(8,128)(2,1)S(1)}, bf16[128,512]{1,0:T(8,128)(2,1)S(1)}, u32[]{:S(2)}, u32[]{:S(2)}) collective-permute-start(bf16[128,512]{1,0:T(8,128)(2,1)S(1)} %get-tuple-element.68), channel_id=1, source_target_pairs={{0,2},{1,3},{2,0},{3,1},{4,6},{5,7},{6,4},{7,5},{8,10},{9,11},{10,... | collective-permute-start | bytes 393224 | tf_op jit(solution)/shard_map/ppermute | solution.py:282
  44.8 1.5 %collective-permute-start.12 = (bf16[128,512]{1,0:T(8,128)(2,1)S(1)}, bf16[128,512]{1,0:T(8,128)(2,1)S(1)}, u32[]{:S(2)}, u32[]{:S(2)}) collective-permute-start(bf16[128,512]{1,0:T(8,128)(2,1)S(1)} %get-tuple-element.69), channel_id=1, source_target_pairs={{0,4},{1,5},{2,6},{3,7},{4,0},{5,1},{6,2},{7,3},{8,12},{9,13},{10,... | collective-permute-start | bytes 393224 | tf_op jit(solution)/shard_map/ppermute | solution.py:282
  46.4 1.1 %collective-permute-start.13 = (bf16[128,512]{1,0:T(8,128)(2,1)S(1)}, bf16[128,512]{1,0:T(8,128)(2,1)S(1)}, u32[]{:S(2)}, u32[]{:S(2)}) collective-permute-start(bf16[128,512]{1,0:T(8,128)(2,1)S(1)} %get-tuple-element.70), channel_id=1, source_target_pairs={{0,6},{1,7},{2,4},{3,5},{4,2},{5,3},{6,0},{7,1},{8,14},{9,15},{10,... | collective-permute-start | bytes 393224 | tf_op jit(solution)/shard_map/ppermute | solution.py:282
  47.5 2.7 %collective-permute-start.19 = (f32[64]{0:T(128)S(1)}, f32[64]{0:T(128)S(1)}, u32[]{:S(2)}, u32[]{:S(2)}) collective-permute-start(f32[64]{0:T(128)S(1)} %fusion.10), channel_id=1, source_target_pairs={{0,8},{1,9},{2,10},{3,11},{4,12},{5,13},{6,14},{7,15},{8,0},{9,1},... | collective-permute-start | bytes 776 | tf_op jit(solution)/shard_map/ppermute | solution.py:282
  50.2 2.4 %collective-permute-done.14 = bf16[512,256]{1,0:T(8,128)(2,1)S(1)} collective-permute-done((bf16[512,256]{1,0:T(8,128)(2,1)S(1)}, bf16[512,256]{1,0:T(8,128)(2,1)S(1)}, u32[]{:S(2)}, u32[]{:S(2)}) %collective-permute-start.14) | collective-permute-done | bytes 262176 | tf_op jit(solution)/shard_map/ppermute | solution.py:279
  52.7 1.9 %collective-permute-start.16 = (bf16[128,256]{1,0:T(8,128)(2,1)S(1)}, bf16[128,256]{1,0:T(8,128)(2,1)S(1)}, u32[]{:S(2)}, u32[]{:S(2)}) collective-permute-start(bf16[128,256]{1,0:T(8,128)(2,1)S(1)} %get-tuple-element.78), channel_id=1, source_target_pairs={{0,6},{1,7},{2,4},{3,5},{4,2},{5,3},{6,0},{7,1},{8,14},{9,15},{10,... | collective-permute-start | bytes 196616 | tf_op jit(solution)/shard_map/ppermute | solution.py:282
  55.1 1.2 %collective-permute-start.18 = (bf16[128,256]{1,0:T(8,128)(2,1)S(1)}, bf16[128,256]{1,0:T(8,128)(2,1)S(1)}, u32[]{:S(2)}, u32[]{:S(2)}) collective-permute-start(bf16[128,256]{1,0:T(8,128)(2,1)S(1)} %get-tuple-element.79), channel_id=1, source_target_pairs={{0,2},{1,3},{2,0},{3,1},{4,6},{5,7},{6,4},{7,5},{8,10},{9,11},{10,... | collective-permute-start | bytes 196616 | tf_op jit(solution)/shard_map/ppermute | solution.py:282
  56.8 0.8 %shard_map.87 = bf16[128,2048]{1,0:T(8,128)(2,1)} custom-call(bf16[128,512]{1,0:T(8,128)(2,1)S(1)} %get-tuple-element.74.refs_0_, bf16[128,512]{1,0:T(8,128)(2,1)S(1)} %collective-permute-done.11.refs_1_, bf16[128,512]{1,0:T(8,128)(2,1)S(1)} %collective-permute-done.12.refs_2_, bf16[128,512]{1,0:T(8,128)(2,1)S(1)} %collective-permute-done.13.refs_3_), custom_call_target="tpu_custom_call" | custom-call | bytes 1048576 | tf_op jit(solution)/shard_map/pallas_call | solution.py:29
  57.6 1.0 %collective-permute-done.16 = bf16[128,256]{1,0:T(8,128)(2,1)S(1)} collective-permute-done((bf16[128,256]{1,0:T(8,128)(2,1)S(1)}, bf16[128,256]{1,0:T(8,128)(2,1)S(1)}, u32[]{:S(2)}, u32[]{:S(2)}) %collective-permute-start.16) | collective-permute-done | bytes 65568 | tf_op jit(solution)/shard_map/ppermute | solution.py:282
  (41 shorter events, 6.0 us)
Async XLA Ops:
  0.6 22.0 %copy-start = (f32[4,512]{1,0:T(4,128)S(1)}, f32[4,512]{1,0:T(4,128)}, u32[]{:S(2)}) copy-start(f32[4,512]{1,0:T(4,128)} %refs_0_.1) | copy-start | bytes 24580
  2.3 5.4 %collective-permute-start = (bf16[128,256]{1,0:T(8,128)(2,1)S(1)}, bf16[128,256]{1,0:T(8,128)(2,1)S(1)}, u32[]{:S(2)}, u32[]{:S(2)}) collective-permute-start(bf16[128,256]{1,0:T(8,128)(2,1)S(1)} %get-tuple-element.42), channel_id=1, source_target_pairs={{0,2},{1,3},{2,0},{3,1},{4,6},{5,7},{6,4},{7,5},{8,10},{9,11},{10,... | collective-permute-start | bytes 196616 | tf_op jit(solution)/shard_map/ppermute | solution.py:282
  5.3 4.3 %collective-permute-start.1 = (bf16[128,256]{1,0:T(8,128)(2,1)S(1)}, bf16[128,256]{1,0:T(8,128)(2,1)S(1)}, u32[]{:S(2)}, u32[]{:S(2)}) collective-permute-start(bf16[128,256]{1,0:T(8,128)(2,1)S(1)} %get-tuple-element.43), channel_id=1, source_target_pairs={{0,4},{1,5},{2,6},{3,7},{4,0},{5,1},{6,2},{7,3},{8,12},{9,13},{10,... | collective-permute-start | bytes 196616 | tf_op jit(solution)/shard_map/ppermute | solution.py:282
  6.8 5.2 %collective-permute-start.2 = (bf16[128,256]{1,0:T(8,128)(2,1)S(1)}, bf16[128,256]{1,0:T(8,128)(2,1)S(1)}, u32[]{:S(2)}, u32[]{:S(2)}) collective-permute-start(bf16[128,256]{1,0:T(8,128)(2,1)S(1)} %get-tuple-element.44), channel_id=1, source_target_pairs={{0,6},{1,7},{2,4},{3,5},{4,2},{5,3},{6,0},{7,1},{8,14},{9,15},{10,... | collective-permute-start | bytes 196616 | tf_op jit(solution)/shard_map/ppermute | solution.py:282
  12.0 7.4 %collective-permute-start.3 = (bf16[4,128,256]{2,1,0:T(8,128)(2,1)S(1)}, bf16[4,128,256]{2,1,0:T(8,128)(2,1)S(1)}, u32[]{:S(2)}, u32[]{:S(2)}) collective-permute-start(bf16[4,128,256]{2,1,0:T(8,128)(2,1)S(1)} %pad_maximum_fusion.refs_0_), channel_id=1, source_target_pairs={{0,8},{1,9},{2,10},{3,11},{4,12},{5,13},{6,14},{7,15},{8,16},{9,17... | collective-permute-start | bytes 786440 | tf_op jit(solution)/shard_map/ppermute | solution.py:279
  15.5 6.4 %collective-permute-start.7 = (bf16[1024,128]{1,0:T(8,128)(2,1)S(1)}, bf16[1024,128]{1,0:T(8,128)(2,1)S(1)}, u32[]{:S(2)}, u32[]{:S(2)}) collective-permute-start(bf16[1024,128]{1,0:T(8,128)(2,1)S(1)} %get-tuple-element.52), channel_id=1, source_target_pairs={{0,2},{1,3},{2,0},{3,1},{4,6},{5,7},{6,4},{7,5},{8,10},{9,11},{10,... | collective-permute-start | bytes 786440 | tf_op jit(solution)/shard_map/ppermute | solution.py:282
  16.1 6.5 %collective-permute-start.8 = (bf16[1024,128]{1,0:T(8,128)(2,1)S(1)}, bf16[1024,128]{1,0:T(8,128)(2,1)S(1)}, u32[]{:S(2)}, u32[]{:S(2)}) collective-permute-start(bf16[1024,128]{1,0:T(8,128)(2,1)S(1)} %get-tuple-element.53), channel_id=1, source_target_pairs={{0,4},{1,5},{2,6},{3,7},{4,0},{5,1},{6,2},{7,3},{8,12},{9,13},{10,... | collective-permute-start | bytes 786440 | tf_op jit(solution)/shard_map/ppermute | solution.py:282
  19.4 3.3 %collective-permute-start.4 = (bf16[4,128,256]{2,1,0:T(8,128)(2,1)S(1)}, bf16[4,128,256]{2,1,0:T(8,128)(2,1)S(1)}, u32[]{:S(2)}, u32[]{:S(2)}) collective-permute-start(bf16[4,128,256]{2,1,0:T(8,128)(2,1)S(1)} %pad_maximum_fusion.refs_0_), channel_id=1, source_target_pairs={{0,1},{1,0},{2,3},{3,2},{4,5},{5,4},{6,7},{7,6},{8,9},{9,8},{10,11... | collective-permute-start | bytes 786440 | tf_op jit(solution)/shard_map/ppermute | solution.py:282
  19.4 3.3 %collective-permute-start.5 = (bf16[4,128,256]{2,1,0:T(8,128)(2,1)S(1)}, bf16[4,128,256]{2,1,0:T(8,128)(2,1)S(1)}, u32[]{:S(2)}, u32[]{:S(2)}) collective-permute-start(bf16[4,128,256]{2,1,0:T(8,128)(2,1)S(1)} %collective-permute-done.3.refs_2_), channel_id=1, source_target_pairs={{0,1},{1,0},{2,3},{3,2},{4,5},{5,4},{6,7},{7,6},{8,9},{9,8},{10,11... | collective-permute-start | bytes 786440 | tf_op jit(solution)/shard_map/ppermute | solution.py:282
  19.9 9.5 %collective-permute-start.9 = (bf16[1024,128]{1,0:T(8,128)(2,1)S(1)}, bf16[1024,128]{1,0:T(8,128)(2,1)S(1)}, u32[]{:S(2)}, u32[]{:S(2)}) collective-permute-start(bf16[1024,128]{1,0:T(8,128)(2,1)S(1)} %get-tuple-element.60), channel_id=1, source_target_pairs={{0,6},{1,7},{2,4},{3,5},{4,2},{5,3},{6,0},{7,1},{8,14},{9,15},{10,... | collective-permute-start | bytes 786440 | tf_op jit(solution)/shard_map/ppermute | solution.py:282
  22.0 0.7 %collective-permute-start.6 = (bf16[16,128]{1,0:T(8,128)(2,1)S(1)}, bf16[16,128]{1,0:T(8,128)(2,1)S(1)}, u32[]{:S(2)}, u32[]{:S(2)}) collective-permute-start(bf16[16,128]{1,0:T(8,128)(2,1)S(1)} %slice.95), channel_id=1, source_target_pairs={{1,16},{3,18},{5,20},{7,22},{9,24},{11,26},{13,28},{15,30}} | collective-permute-start | bytes 12296 | tf_op jit(solution)/shard_map/ppermute | solution.py:279
  32.7 6.3 %collective-permute-start.10 = (bf16[1040,256]{1,0:T(8,128)(2,1)S(1)}, bf16[1040,256]{1,0:T(8,128)(2,1)S(1)}, u32[]{:S(2)}, u32[]{:S(2)}) collective-permute-start(bf16[1040,256]{1,0:T(8,128)(2,1)S(1)} %get-tuple-element.61), channel_id=1, source_target_pairs={{0,1},{1,0},{2,3},{3,2},{4,5},{5,4},{6,7},{7,6},{8,9},{9,8},{10,11... | collective-permute-start | bytes 1597448 | tf_op jit(solution)/shard_map/ppermute | solution.py:282
  39.2 8.3 %collective-permute-start.15 = (f32[24,128]{1,0:T(8,128)S(1)}, f32[24,128]{1,0:T(8,128)S(1)}, u32[]{:S(2)}, u32[]{:S(2)}) collective-permute-start(f32[24,128]{1,0:T(8,128)S(1)} %select_maximum_fusion), channel_id=1, source_target_pairs={{0,16},{1,17},{2,18},{3,19},{4,20},{5,21},{6,22},{7,23},{8,24},{9,... | collective-permute-start | bytes 36872 | tf_op jit(solution)/shard_map/ppermute | solution.py:282
  42.6 10.0 %collective-permute-start.14 = (bf16[512,256]{1,0:T(8,128)(2,1)S(1)}, bf16[512,256]{1,0:T(8,128)(2,1)S(1)}, u32[]{:S(2)}, u32[]{:S(2)}) collective-permute-start(bf16[512,256]{1,0:T(8,128)(2,1)S(1)} %add_convert_fusion), channel_id=1, source_target_pairs={{8,0},{9,1},{10,2},{11,3},{12,4},{13,5},{14,6},{15,7},{16,8},{17,9... | collective-permute-start | bytes 786440 | tf_op jit(solution)/shard_map/ppermute | solution.py:279
  43.9 11.2 %collective-permute-start.11 = (bf16[128,512]{1,0:T(8,128)(2,1)S(1)}, bf16[128,512]{1,0:T(8,128)(2,1)S(1)}, u32[]{:S(2)}, u32[]{:S(2)}) collective-permute-start(bf16[128,512]{1,0:T(8,128)(2,1)S(1)} %get-tuple-element.68), channel_id=1, source_target_pairs={{0,2},{1,3},{2,0},{3,1},{4,6},{5,7},{6,4},{7,5},{8,10},{9,11},{10,... | collective-permute-start | bytes 393224 | tf_op jit(solution)/shard_map/ppermute | solution.py:282
  44.8 11.9 %collective-permute-start.12 = (bf16[128,512]{1,0:T(8,128)(2,1)S(1)}, bf16[128,512]{1,0:T(8,128)(2,1)S(1)}, u32[]{:S(2)}, u32[]{:S(2)}) collective-permute-start(bf16[128,512]{1,0:T(8,128)(2,1)S(1)} %get-tuple-element.69), channel_id=1, source_target_pairs={{0,4},{1,5},{2,6},{3,7},{4,0},{5,1},{6,2},{7,3},{8,12},{9,13},{10,... | collective-permute-start | bytes 393224 | tf_op jit(solution)/shard_map/ppermute | solution.py:282
  46.4 10.4 %collective-permute-start.13 = (bf16[128,512]{1,0:T(8,128)(2,1)S(1)}, bf16[128,512]{1,0:T(8,128)(2,1)S(1)}, u32[]{:S(2)}, u32[]{:S(2)}) collective-permute-start(bf16[128,512]{1,0:T(8,128)(2,1)S(1)} %get-tuple-element.70), channel_id=1, source_target_pairs={{0,6},{1,7},{2,4},{3,5},{4,2},{5,3},{6,0},{7,1},{8,14},{9,15},{10,... | collective-permute-start | bytes 393224 | tf_op jit(solution)/shard_map/ppermute | solution.py:282
  47.5 7.1 %collective-permute-start.19 = (f32[64]{0:T(128)S(1)}, f32[64]{0:T(128)S(1)}, u32[]{:S(2)}, u32[]{:S(2)}) collective-permute-start(f32[64]{0:T(128)S(1)} %fusion.10), channel_id=1, source_target_pairs={{0,8},{1,9},{2,10},{3,11},{4,12},{5,13},{6,14},{7,15},{8,0},{9,1},... | collective-permute-start | bytes 776 | tf_op jit(solution)/shard_map/ppermute | solution.py:282
  52.7 5.9 %collective-permute-start.16 = (bf16[128,256]{1,0:T(8,128)(2,1)S(1)}, bf16[128,256]{1,0:T(8,128)(2,1)S(1)}, u32[]{:S(2)}, u32[]{:S(2)}) collective-permute-start(bf16[128,256]{1,0:T(8,128)(2,1)S(1)} %get-tuple-element.78), channel_id=1, source_target_pairs={{0,6},{1,7},{2,4},{3,5},{4,2},{5,3},{6,0},{7,1},{8,14},{9,15},{10,... | collective-permute-start | bytes 196616 | tf_op jit(solution)/shard_map/ppermute | solution.py:282
  54.6 4.5 %collective-permute-start.17 = (bf16[128,256]{1,0:T(8,128)(2,1)S(1)}, bf16[128,256]{1,0:T(8,128)(2,1)S(1)}, u32[]{:S(2)}, u32[]{:S(2)}) collective-permute-start(bf16[128,256]{1,0:T(8,128)(2,1)S(1)} %get-tuple-element.80), channel_id=1, source_target_pairs={{0,4},{1,5},{2,6},{3,7},{4,0},{5,1},{6,2},{7,3},{8,12},{9,13},{10,... | collective-permute-start | bytes 196616 | tf_op jit(solution)/shard_map/ppermute | solution.py:282
  55.1 4.3 %collective-permute-start.18 = (bf16[128,256]{1,0:T(8,128)(2,1)S(1)}, bf16[128,256]{1,0:T(8,128)(2,1)S(1)}, u32[]{:S(2)}, u32[]{:S(2)}) collective-permute-start(bf16[128,256]{1,0:T(8,128)(2,1)S(1)} %get-tuple-element.79), channel_id=1, source_target_pairs={{0,2},{1,3},{2,0},{3,1},{4,6},{5,7},{6,4},{7,5},{8,10},{9,11},{10,... | collective-permute-start | bytes 196616 | tf_op jit(solution)/shard_map/ppermute | solution.py:282
